TPU v7x, 32 devices: a whole 2x2x4 slice. The times are simulated.
32 devices in a mesh: dp: 4 (over z), ctx: 2 (over y), tp: 4 (over x, core).
Axes of the slice: x: 2, y: 2, z: 4, core: 2. Of those that a mesh axis runs over, the one named last changes fastest.
Arguments:
- tokens: bfloat16 [8192, 1152], P(('dp', 'ctx'), 'tp'), may hold values from -6 to 6
- out_grad: bfloat16 [8192, 1152], P(('dp', 'ctx'), 'tp'), may hold values from -6 to 6
- w_query: bfloat16 [1152, 1024], P(None, 'tp'), may hold values from -0.1875 to 0.1875
- w_key: bfloat16 [1152, 256], replicated, may hold values from -0.1875 to 0.1875
- w_value: bfloat16 [1152, 256], replicated, may hold values from -0.1875 to 0.1875
- w_out: bfloat16 [1024, 1152], P('tp'), may hold values from -0.1875 to 0.1875
- w_gate: bfloat16 [1152, 6912], P(None, 'tp'), may hold values from -0.1875 to 0.1875
- w_up: bfloat16 [1152, 6912], P(None, 'tp'), may hold values from -0.1875 to 0.1875
- w_down: bfloat16 [6912, 1152], P('tp'), may hold values from -0.078125 to 0.078125
- gain_in: bfloat16 [1152], replicated, may hold values from 0.25 to 1.75
- gain_post_attn: bfloat16 [1152], replicated, may hold values from 0.25 to 1.75
- gain_pre_ffn: bfloat16 [1152], replicated, may hold values from 0.25 to 1.75
- gain_post_ffn: bfloat16 [1152], replicated, may hold values from 0.25 to 1.75
- gain_query: bfloat16 [256], replicated, may hold values from 0.25 to 1.75
- gain_key: bfloat16 [256], replicated, may hold values from 0.25 to 1.75
- bucket_lengths: int32 [4, 2], P('dp'), may hold values from 1024 to 1024, as said below
- true_lengths: int32 [4, 2], P('dp'), may hold values from 768 to 1024, as said below
Outputs:
- out: bfloat16 [8192, 1152], P(('dp', 'ctx'), 'tp')
- x_grad: bfloat16 [8192, 1152], P(('dp', 'ctx'), 'tp')
- w_query_grad: float32 [1152, 1024], P(None, 'tp')
- w_key_grad: float32 [1152, 256], replicated
- w_value_grad: float32 [1152, 256], replicated
- w_out_grad: float32 [1024, 1152], P('tp')
- w_gate_grad: float32 [1152, 6912], P(None, 'tp')
- w_up_grad: float32 [1152, 6912], P(None, 'tp')
- w_down_grad: float32 [6912, 1152], P('tp')
- gain_in_grad: float32 [1152], replicated
- gain_post_attn_grad: float32 [1152], replicated
- gain_pre_ffn_grad: float32 [1152], replicated
- gain_post_ffn_grad: float32 [1152], replicated
- gain_query_grad: float32 [256], replicated
- gain_key_grad: float32 [256], replicated
Inputs may be any that keep to these rules, and one draw needn't show every extreme that they name: `bucket_lengths`: in each group the 2 bucket lengths, in stream order, add up to 2048; each is a multiple of 512; the first or the last is 1024 or longer; some group has a bucket of length 1024 and one of length 1024. `true_lengths`: each is its bucket's length less 0 to 256 padding positions at the bucket's end; in each group the bucket of length 1024 or more that stands first or last has no padding, and each other bucket of length 1024 has 256.
All inputs are finite; a program needn't handle non-finite values.
Results may differ from a plain program's by a relative error of at most 0.03.
Values may be sent and summed in bfloat16 or wider, within the bound.
A program may use at most 320 MiB of HBM per device.

v0:
```python
from functools import partial

import jax
import jax.numpy as jnp
from jax import lax
from jax.sharding import PartitionSpec as P

QBLK = 512


EPSILON = 1e-06
ROPE_BASE = 1000000.0
MASKED = -1e30


def contract(left, right, left_dim, right_dim):
    return lax.dot_general(
        left, right, (((left_dim,), (right_dim,)), ((), ())), preferred_element_type=jnp.float32
    )


def rms_norm(values, gain):
    return values * lax.rsqrt(jnp.mean(values * values, axis=-1, keepdims=True) + EPSILON) * gain


def rotate(values, cosine_table, sine_table):
    half_dim = values.shape[-1] // 2
    turned = jnp.concatenate([-values[..., half_dim:], values[..., :half_dim]], axis=-1)
    return values * cosine_table + turned * sine_table


def rope_tables(seq_pos, head_dim):
    freq_index = jnp.arange(head_dim // 2, dtype=jnp.float32)
    inverse = ROPE_BASE ** (-2.0 * freq_index / head_dim)
    angles = seq_pos.astype(jnp.float32)[:, None] * inverse[None, :]
    angles = jnp.concatenate([angles, angles], axis=-1)
    return (jnp.cos(angles), jnp.sin(angles))


def stream_layout(bucket_row, true_row, tok_dev, n_ctx):
    group_rows = tok_dev * n_ctx
    half_shard = tok_dev // 2
    row_ids = jnp.arange(group_rows, dtype=jnp.int32)
    device = row_ids // tok_dev
    half_index = row_ids % tok_dev // half_shard
    block_ids = jnp.where(half_index == 0, device, 2 * n_ctx - 1 - device)
    stream_pos = block_ids * half_shard + row_ids % half_shard
    starts = jnp.cumsum(bucket_row) - bucket_row
    ends = starts + bucket_row
    inside = (
        (stream_pos[:, None] >= starts[None, :]) & (stream_pos[:, None] < ends[None, :])
    ).astype(jnp.int32)
    slot_ids = jnp.arange(bucket_row.shape[0], dtype=jnp.int32)
    seq_ids = jnp.sum(inside * slot_ids[None, :], axis=1)
    seq_pos = stream_pos - jnp.sum(inside * starts[None, :], axis=1)
    is_valid = (seq_pos < jnp.sum(inside * true_row[None, :], axis=1)).astype(jnp.int32)
    return (seq_ids, stream_pos, seq_pos, is_valid)


def shape_heads(query_raw, key_raw, gain_q, gain_k, cosine_table, sine_table):
    query_heads = query_raw.reshape(query_raw.shape[0], -1, key_raw.shape[1])
    query_rot = rotate(
        rms_norm(query_heads, gain_q), cosine_table[:, None, :], sine_table[:, None, :]
    )
    key_rot = rotate(rms_norm(key_raw, gain_k), cosine_table, sine_table)
    return (query_rot, key_rot)


def geglu(gate_in, up_in):
    return jax.nn.gelu(gate_in, approximate=True) * up_in


def shards(
    tokens,
    out_grad,
    w_query,
    w_key,
    w_value,
    w_out,
    w_gate,
    w_up,
    w_down,
    gain_in,
    gain_post_attn,
    gain_pre_ffn,
    gain_post_ffn,
    gain_query,
    gain_key,
    bucket_lengths,
    true_lengths,
):
    n_ctx = lax.axis_size("ctx")
    ctx_index = lax.axis_index("ctx")
    tp_index = lax.axis_index("tp")
    rows_dev = tokens.shape[0]
    feature_cols = tokens.shape[1]
    head_dim = w_key.shape[1]
    head_count = w_query.shape[1] // head_dim
    group_rows = rows_dev * n_ctx
    blocks = rows_dev // QBLK
    score_scale = head_dim ** (-0.5)
    gain_in32, gain_pa32, gain_pf32, gain_pff32, gain_q32, gain_k32 = [
        tensor.astype(jnp.float32)
        for tensor in (gain_in, gain_post_attn, gain_pre_ffn, gain_post_ffn, gain_query, gain_key)
    ]
    input_full, cot_full = (
        lax.all_gather(tokens, "tp", axis=1, tiled=True),
        lax.all_gather(out_grad, "tp", axis=1, tiled=True),
    )
    inputs = input_full.astype(jnp.float32)
    seq_all, spos_all, rpos_all, valid_all = stream_layout(
        bucket_lengths[0], true_lengths[0], rows_dev, n_ctx
    )
    first_row = ctx_index * rows_dev
    seq_local = lax.dynamic_slice_in_dim(seq_all, first_row, rows_dev)
    spos_local = lax.dynamic_slice_in_dim(spos_all, first_row, rows_dev)
    rpos_local = lax.dynamic_slice_in_dim(rpos_all, first_row, rows_dev)
    cosine_table, sine_table = rope_tables(rpos_local, head_dim)
    normed_in, pull_in = jax.vjp(rms_norm, inputs, gain_in32)
    normed_in16 = normed_in.astype(jnp.bfloat16)
    query_raw = jnp.dot(normed_in16, w_query, preferred_element_type=jnp.float32)
    key_raw = jnp.dot(normed_in16, w_key, preferred_element_type=jnp.float32)
    value_raw = jnp.dot(normed_in16, w_value, preferred_element_type=jnp.float32)
    (query_rot, key_rot), rope_pull = jax.vjp(
        partial(shape_heads, cosine_table=cosine_table, sine_table=sine_table),
        query_raw,
        key_raw,
        gain_q32,
        gain_k32,
    )
    query16 = query_rot.astype(jnp.bfloat16)
    key16 = key_rot.astype(jnp.bfloat16)
    value16 = value_raw.astype(jnp.bfloat16)
    key_group, value_group = (
        lax.all_gather(key16, "ctx", axis=0, tiled=True),
        lax.all_gather(value16, "ctx", axis=0, tiled=True),
    )

    def allowed_mask(seq_rows, spos_rows):
        return (
            (valid_all[None, :] == 1)
            & (seq_all[None, :] == seq_rows[:, None])
            & (spos_all[None, :] <= spos_rows[:, None])
        )

    query_blocks = query16.reshape(blocks, QBLK, head_count, head_dim)
    seq_blocks = seq_local.reshape(blocks, QBLK)
    spos_blocks = spos_local.reshape(blocks, QBLK)

    def forward_block(block_item):
        query_block, seq_rows, spos_rows = block_item
        scores = (
            jnp.einsum("qhd,kd->hqk", query_block, key_group, preferred_element_type=jnp.float32)
            * score_scale
        )
        scores = jnp.where(allowed_mask(seq_rows, spos_rows)[None], scores, MASKED)
        row_max = jnp.max(scores, axis=-1, keepdims=True)
        exp_scores = jnp.exp(scores - row_max)
        row_total = jnp.sum(exp_scores, axis=-1, keepdims=True)
        prob_rows = (exp_scores / row_total).astype(jnp.bfloat16)
        output = jnp.einsum(
            "hqk,kd->qhd", prob_rows, value_group, preferred_element_type=jnp.float32
        )
        return (output, (row_max + jnp.log(row_total))[..., 0])

    attended, log_norm = lax.map(forward_block, (query_blocks, seq_blocks, spos_blocks))
    attended16 = attended.reshape(rows_dev, head_count * head_dim).astype(jnp.bfloat16)
    attention = lax.psum(
        jnp.dot(attended16, w_out, preferred_element_type=jnp.float32).astype(jnp.bfloat16), "tp"
    ).astype(jnp.float32)
    post_attn, pull_post_attn = jax.vjp(rms_norm, attention, gain_pa32)
    residual = inputs + post_attn
    normed_mid, pull_pre_ffn = jax.vjp(rms_norm, residual, gain_pf32)
    mid16 = normed_mid.astype(jnp.bfloat16)
    gate_out = jnp.dot(mid16, w_gate, preferred_element_type=jnp.float32)
    up_out = jnp.dot(mid16, w_up, preferred_element_type=jnp.float32)
    hidden, pull_geglu = jax.vjp(geglu, gate_out, up_out)
    hidden16 = hidden.astype(jnp.bfloat16)
    ffn_branch = lax.psum(
        jnp.dot(hidden16, w_down, preferred_element_type=jnp.float32).astype(jnp.bfloat16), "tp"
    ).astype(jnp.float32)
    post_ffn, pull_post_ffn = jax.vjp(rms_norm, ffn_branch, gain_pff32)
    outputs = residual + post_ffn
    out_rows = lax.dynamic_slice_in_dim(outputs, tp_index * feature_cols, feature_cols, 1).astype(
        jnp.bfloat16
    )
    cotangent = cot_full.astype(jnp.float32)
    d_ffn, d_gain_post_ffn = pull_post_ffn(cotangent)
    d_ffn16 = d_ffn.astype(jnp.bfloat16)
    d_hidden = contract(d_ffn16, w_down, 1, 1)
    grad_down = contract(hidden16, d_ffn16, 0, 0)
    d_gate, d_up = pull_geglu(d_hidden)
    d_gate16 = d_gate.astype(jnp.bfloat16)
    d_up16 = d_up.astype(jnp.bfloat16)
    grad_gate = contract(mid16, d_gate16, 0, 0)
    grad_up = contract(mid16, d_up16, 0, 0)
    d_mid = lax.psum(
        (contract(d_gate16, w_gate, 1, 1) + contract(d_up16, w_up, 1, 1)).astype(jnp.bfloat16), "tp"
    ).astype(jnp.float32)
    d_res_norm, d_gain_pre_ffn = pull_pre_ffn(d_mid)
    d_resid = cotangent + d_res_norm
    d_attn, d_gain_post_attn = pull_post_attn(d_resid)
    d_attn16 = d_attn.astype(jnp.bfloat16)
    d_attended16 = contract(d_attn16, w_out, 1, 1).astype(jnp.bfloat16)
    grad_out = contract(attended16, d_attn16, 0, 0)
    key_back, value_back = (key_group, value_group)

    def backward_block(running, block_item):
        key_sum, value_sum = running
        query_block, dout_block, lse_block, seq_rows, spos_rows = block_item
        scores = (
            jnp.einsum("qhd,kd->hqk", query_block, key_back, preferred_element_type=jnp.float32)
            * score_scale
        )
        scores = jnp.where(allowed_mask(seq_rows, spos_rows)[None], scores, MASKED)
        prob_rows = jnp.exp(scores - lse_block[..., None])
        prob16 = prob_rows.astype(jnp.bfloat16)
        d_probs = jnp.einsum(
            "qhd,kd->hqk", dout_block, value_back, preferred_element_type=jnp.float32
        )
        row_inner = jnp.sum(prob_rows * d_probs, axis=-1, keepdims=True)
        d_scores16 = (prob_rows * (d_probs - row_inner)).astype(jnp.bfloat16)
        d_query = (
            jnp.einsum("hqk,kd->qhd", d_scores16, key_back, preferred_element_type=jnp.float32)
            * score_scale
        )
        key_sum = (
            key_sum
            + jnp.einsum("hqk,qhd->kd", d_scores16, query_block, preferred_element_type=jnp.float32)
            * score_scale
        )
        value_sum = value_sum + jnp.einsum(
            "hqk,qhd->kd", prob16, dout_block, preferred_element_type=jnp.float32
        )
        return ((key_sum, value_sum), d_query)

    zero_rows = jnp.zeros((group_rows, head_dim), jnp.float32)
    (key_sum, value_sum), d_query_blocks = lax.scan(
        backward_block,
        (zero_rows, zero_rows),
        (
            query_blocks,
            d_attended16.reshape(blocks, QBLK, head_count, head_dim),
            log_norm,
            seq_blocks,
            spos_blocks,
        ),
    )
    d_key_rot, d_value = (
        lax.psum_scatter(
            key_sum.astype(jnp.bfloat16), "ctx", scatter_dimension=0, tiled=True
        ).astype(jnp.float32),
        lax.psum_scatter(
            value_sum.astype(jnp.bfloat16), "ctx", scatter_dimension=0, tiled=True
        ).astype(jnp.float32),
    )
    d_query_raw, d_key_raw, d_gain_query, d_gain_key = rope_pull(
        (d_query_blocks.reshape(rows_dev, head_count, head_dim), d_key_rot)
    )
    d_query16 = d_query_raw.astype(jnp.bfloat16)
    d_key16 = d_key_raw.astype(jnp.bfloat16)
    d_value16 = d_value.astype(jnp.bfloat16)
    grad_query = contract(normed_in16, d_query16, 0, 0)
    grad_key = contract(normed_in16, d_key16, 0, 0)
    grad_value = contract(normed_in16, d_value16, 0, 0)
    d_normed_part = (
        contract(d_query16, w_query, 1, 1)
        + contract(d_key16, w_key, 1, 1)
        + contract(d_value16, w_value, 1, 1)
    )
    d_normed_in = lax.psum(d_normed_part.astype(jnp.bfloat16), "tp").astype(jnp.float32)
    d_in_norm, d_gain_in = pull_in(d_normed_in)
    d_inputs = d_resid + d_in_norm
    grad_rows = lax.dynamic_slice_in_dim(d_inputs, tp_index * feature_cols, feature_cols, 1).astype(
        jnp.bfloat16
    )
    sharded = (
        grad_query,
        grad_out,
        grad_gate,
        grad_up,
        grad_down,
        d_gain_in,
        d_gain_post_attn,
        d_gain_pre_ffn,
        d_gain_post_ffn,
    )
    reduced = (
        lax.psum_scatter(
            sharded[0].astype(jnp.bfloat16), ("dp", "ctx"), scatter_dimension=0, tiled=True
        ).astype(jnp.float32),
        lax.psum_scatter(
            sharded[1].astype(jnp.bfloat16), ("dp", "ctx"), scatter_dimension=1, tiled=True
        ).astype(jnp.float32),
        lax.psum_scatter(
            sharded[2].astype(jnp.bfloat16), ("dp", "ctx"), scatter_dimension=0, tiled=True
        ).astype(jnp.float32),
        lax.psum_scatter(
            sharded[3].astype(jnp.bfloat16), ("dp", "ctx"), scatter_dimension=0, tiled=True
        ).astype(jnp.float32),
        lax.psum_scatter(
            sharded[4].astype(jnp.bfloat16), ("dp", "ctx"), scatter_dimension=1, tiled=True
        ).astype(jnp.float32),
        lax.psum_scatter(
            sharded[5].astype(jnp.bfloat16), ("dp", "ctx"), scatter_dimension=0, tiled=True
        ).astype(jnp.float32),
        lax.psum_scatter(
            sharded[6].astype(jnp.bfloat16), ("dp", "ctx"), scatter_dimension=0, tiled=True
        ).astype(jnp.float32),
        lax.psum_scatter(
            sharded[7].astype(jnp.bfloat16), ("dp", "ctx"), scatter_dimension=0, tiled=True
        ).astype(jnp.float32),
        lax.psum_scatter(
            sharded[8].astype(jnp.bfloat16), ("dp", "ctx"), scatter_dimension=0, tiled=True
        ).astype(jnp.float32),
    )
    summed = (
        lax.all_gather(reduced[0].astype(jnp.bfloat16), ("dp", "ctx"), axis=0, tiled=True).astype(
            jnp.float32
        ),
        lax.all_gather(reduced[1].astype(jnp.bfloat16), ("dp", "ctx"), axis=1, tiled=True).astype(
            jnp.float32
        ),
        lax.all_gather(reduced[2].astype(jnp.bfloat16), ("dp", "ctx"), axis=0, tiled=True).astype(
            jnp.float32
        ),
        lax.all_gather(reduced[3].astype(jnp.bfloat16), ("dp", "ctx"), axis=0, tiled=True).astype(
            jnp.float32
        ),
        lax.all_gather(reduced[4].astype(jnp.bfloat16), ("dp", "ctx"), axis=1, tiled=True).astype(
            jnp.float32
        ),
        lax.all_gather(reduced[5].astype(jnp.bfloat16), ("dp", "ctx"), axis=0, tiled=True).astype(
            jnp.float32
        ),
        lax.all_gather(reduced[6].astype(jnp.bfloat16), ("dp", "ctx"), axis=0, tiled=True).astype(
            jnp.float32
        ),
        lax.all_gather(reduced[7].astype(jnp.bfloat16), ("dp", "ctx"), axis=0, tiled=True).astype(
            jnp.float32
        ),
        lax.all_gather(reduced[8].astype(jnp.bfloat16), ("dp", "ctx"), axis=0, tiled=True).astype(
            jnp.float32
        ),
    )
    shared = lax.psum((grad_key, grad_value, d_gain_query, d_gain_key), ("dp", "ctx", "tp"))
    return (
        out_rows,
        grad_rows,
        summed[0],
        shared[0],
        shared[1],
        summed[1],
        summed[2],
        summed[3],
        summed[4],
        summed[5],
        summed[6],
        summed[7],
        summed[8],
        shared[2],
        shared[3],
    )


def solution(mesh):
    return jax.shard_map(
        shards,
        mesh=mesh,
        in_specs=(
            P(("dp", "ctx"), "tp"),
            P(("dp", "ctx"), "tp"),
            P(None, "tp"),
            P(),
            P(),
            P("tp", None),
            P(None, "tp"),
            P(None, "tp"),
            P("tp", None),
            P(),
            P(),
            P(),
            P(),
            P(),
            P(),
            P("dp", None),
            P("dp", None),
        ),
        out_specs=(
            P(("dp", "ctx"), "tp"),
            P(("dp", "ctx"), "tp"),
            P(None, "tp"),
            P(),
            P(),
            P("tp", None),
            P(None, "tp"),
            P(None, "tp"),
            P("tp", None),
            P(),
            P(),
            P(),
            P(),
            P(),
            P(),
        ),
        check_vma=False,
    )
```

profile of v0, /device:TPU:0, one launch (start us, length us, event | category | flops | bytes accessed | tf_op | source)
XLA Modules:
  0.0 1281.1 jit_solution(12412175244597896123)
XLA Ops:
  14.0 22.4 %all-gather.8.cloned.1.call-done = bf16[1024,1152]{0,1:T(8,128)(2,1)} async-done(((bf16[1024,288]{0,1:T(8,128)(2,1)}), bf16[1024,1152]{0,1:T(8,128)(2,1)}) %all-gather.8.cloned.1.call-update) | async-done | bytes 2359312 | tf_op jit(solution)/shard_map/all_gather | solution.py:107
  62.3 16.5 %all-gather.10.cloned.1.call-done = bf16[2048,256]{1,0:T(8,128)(2,1)} async-done(((bf16[1024,256]{1,0:T(8,128)(2,1)}), bf16[2048,256]{1,0:T(8,128)(2,1)}) %all-gather.10.cloned.1.call-update) | async-done | bytes 1048592 | tf_op jit(solution)/shard_map/all_gather | solution.py:135
  78.9 23.5 %all-gather.12.cloned.1.call-done = bf16[2048,256]{1,0:T(8,128)(2,1)} async-done(((bf16[1024,256]{1,0:T(8,128)(2,1)}), bf16[2048,256]{1,0:T(8,128)(2,1)}) %all-gather.12.cloned.1.call-update) | async-done | bytes 1048592 | tf_op jit(solution)/shard_map/all_gather | solution.py:136
  102.3 11.7 while.30
  118.5 54.9 %all-reduce.22.cloned.1.call-done = bf16[1024,1152]{1,0:T(8,128)(2,1)} async-done(((bf16[1024,1152]{1,0:T(8,128)(2,1)}), bf16[1024,1152]{1,0:T(8,128)(2,1)}) %all-reduce.22.cloned.1.call-update) | async-done | bytes 2359312 | tf_op jit(solution)/shard_map/psum | solution.py:168
  187.4 7.8 multiply_convert_fusion.1
  206.9 52.3 %all-reduce.24.cloned.1.call-done = bf16[1024,1152]{1,0:T(8,128)(2,1)} async-done(((bf16[1024,1152]{1,0:T(8,128)(2,1)}), bf16[1024,1152]{1,0:T(8,128)(2,1)}) %all-reduce.24.cloned.1.call-update) | async-done | bytes 2359312 | tf_op jit(solution)/shard_map/psum | solution.py:179
  261.5 6.4 fusion.97
  267.9 13.9 %multiply_convert_fusion = (bf16[1024,1728]{0,1:T(8,128)(2,1)}, bf16[1024,1728]{0,1:T(8,128)(2,1)}) fusion(f32[1024,1728]{0,1:T(8,128)} %copy-done.76, f32[1024,1728]{0,1:T(8,128)} %get-tuple-element.478, bf16[1728,1152]{1,0:T(8,128)(2,1)S(1)} %copy-done.70, bf16[1024,1152]{1,0:T(8,128)(2,1)S(1)} %copy.77, bf16[1024,1152]{1,0:T(8,128)(2,1)S(1)} %copy-done.25, ...), kind=kOutput, calls=%fused_computation.132 | convolution fusion | flops 4128768000 | bytes 29946368 | tf_op jit(solution)/shard_map/dot_general | solution.py:17
  281.9 7.4 fusion.171
  289.3 6.6 add_convert_fusion
  296.0 55.8 %all-reduce.26.cloned.1.call-done = bf16[1024,1152]{1,0:T(8,128)(2,1)} async-done(((bf16[1024,1152]{1,0:T(8,128)(2,1)}), bf16[1024,1152]{1,0:T(8,128)(2,1)}) %all-reduce.26.cloned.1.call-update) | async-done | bytes 2359312 | tf_op jit(solution)/shard_map/psum | solution.py:197
  365.5 33.3 %while.31 = (s32[]{:T(128)}, f32[2048,256]{1,0:T(8,128)}, f32[2048,256]{1,0:T(8,128)}, f32[2,512,1,256]{3,1,2,0:T(8,128)}, s32[2048]{0:T(1024)S(1)}, /*index=5*/...) while((s32[]{:T(128)}, f32[2048,256]{1,0:T(8,128)}, ...), condition=%wide.region_22.23_spmd.clone.clone, body=%wide.region_20.22_spmd.clone.sunk.clone | while | flops 2700817920 | bytes 103344472 | solution.py:238
  403.0 9.2 convolution_convert_fusion.2
  412.3 9.3 convolution_convert_fusion.1
  422.1 9.7 convolution_convert_fusion
  468.0 67.8 %reduce-scatter.16.cloned.1.call-done = bf16[144,1728]{1,0:T(8,128)(2,1)} async-done(((bf16[1152,1728]{1,0:T(8,128)(2,1)}), bf16[144,1728]{1,0:T(8,128)(2,1)}) %reduce-scatter.16.cloned.1.call-update) | async-done | bytes 497680 | tf_op jit(solution)/shard_map/reduce_scatter | solution.py:295
  535.9 91.3 %reduce-scatter.18.cloned.1.call-done = bf16[144,1728]{1,0:T(8,128)(2,1)} async-done(((bf16[1152,1728]{1,0:T(8,128)(2,1)}), bf16[144,1728]{1,0:T(8,128)(2,1)}) %reduce-scatter.18.cloned.1.call-update) | async-done | bytes 497680 | tf_op jit(solution)/shard_map/reduce_scatter | solution.py:298
  627.2 90.8 %reduce-scatter.20.cloned.1.call-done = bf16[1728,144]{0,1:T(8,128)(2,1)} async-done(((bf16[1728,1152]{0,1:T(8,128)(2,1)}), bf16[1728,144]{0,1:T(8,128)(2,1)}) %reduce-scatter.20.cloned.1.call-update) | async-done | bytes 497680 | tf_op jit(solution)/shard_map/reduce_scatter | solution.py:301
  728.8 55.3 %reduce-scatter.12.cloned.1.call-done = bf16[144,256]{1,0:T(8,128)(2,1)} async-done(((bf16[1152,256]{1,0:T(8,128)(2,1)}), bf16[144,256]{1,0:T(8,128)(2,1)}) %reduce-scatter.12.cloned.1.call-update) | async-done | bytes 73744 | tf_op jit(solution)/shard_map/reduce_scatter | solution.py:289
  784.1 31.9 %all_gather.43 = bf16[1152,256]{1,0:T(8,128)(2,1)S(1)} all-gather(bf16[144,256]{1,0:T(8,128)(2,1)} %reduce-scatter.12.cloned.1.call-done), channel_id=1, replica_groups=mesh['dp'=4,'ctx'=2,'tp'=4] {'dp','ctx'}, dimensions={0}, use_global_device_ids=true | all-gather | bytes 663552 | tf_op jit(solution)/shard_map/all_gather | solution.py:318
  822.6 25.9 %reduce-scatter.14.cloned.1.call-done = bf16[256,144]{0,1:T(8,128)(2,1)} async-done(((bf16[256,1152]{0,1:T(8,128)(2,1)}), bf16[256,144]{0,1:T(8,128)(2,1)}) %reduce-scatter.14.cloned.1.call-update) | async-done | bytes 73744 | tf_op jit(solution)/shard_map/reduce_scatter | solution.py:292
  848.6 31.8 %all_gather.44 = bf16[256,1152]{0,1:T(8,128)(2,1)S(1)} all-gather(bf16[256,144]{0,1:T(8,128)(2,1)} %reduce-scatter.14.cloned.1.call-done), channel_id=1, replica_groups=mesh['dp'=4,'ctx'=2,'tp'=4] {'dp','ctx'}, dimensions={1}, use_global_device_ids=true | all-gather | bytes 663552 | tf_op jit(solution)/shard_map/all_gather | solution.py:321
  881.6 38.4 %all-reduce.12 = (f32[256]{0:T(256)}, f32[256]{0:T(256)}) all-reduce(f32[256]{0:T(256)} %get-tuple-element.380, f32[256]{0:T(256)} %get-tuple-element.378), channel_id=1, replica_groups=mesh['dp'=4,'ctx'=2,'tp'=4] {'dp','ctx','tp'}, use_global_device_ids=true, to_apply=%region_45.46 | all-reduce | flops 512 | bytes 4096 | tf_op jit(solution)/shard_map/psum | solution.py:346
  928.7 37.6 %all-reduce.15 = (bf16[1152]{0:T(1024)(128)(2,1)S(1)}, bf16[1152]{0:T(1024)(128)(2,1)S(1)}, bf16[1152]{0:T(1024)(128)(2,1)S(1)}, bf16[1152]{0:T(1024)(128)(2,1)S(1)}) all-reduce(bf16[1152]{0:T(1024)(128)(2,1)S(1)} %get-tuple-element.376, ...), channel_id=9, replica_groups=mesh['dp'=4,'ctx'=2,'tp'=4] {'dp','ctx'}, use_global_device_ids=true, to_apply=%region_37.38.clone | all-reduce | flops 4608 | bytes 18432
  967.4 33.4 %all-reduce.14 = (bf16[1152]{0:T(1024)(128)(2,1)S(1)}, bf16[1152]{0:T(1024)(128)(2,1)S(1)}, bf16[1152]{0:T(1024)(128)(2,1)S(1)}, bf16[1152]{0:T(1024)(128)(2,1)S(1)}) all-reduce(bf16[1152]{0:T(1024)(128)(2,1)S(1)} %dynamic-update-slice, bf16[1152]{0:T(1024)(128)(2,1)S(1)} %dynamic-update-slice.1, ...), channel_id=1, replica_groups=mesh['dp'=4,'ctx'=2,'tp'=4] {'dp','ctx'}, use_global_device_ids=true, to_apply=%add.4 | all-reduce | flops 4608 | bytes 18432
  1003.3 6.9 copy.85
  1010.2 45.3 %all-gather.18.cloned.1.call-done = bf16[1152,1728]{1,0:T(8,128)(2,1)} async-done(((bf16[144,1728]{1,0:T(8,128)(2,1)}), bf16[1152,1728]{1,0:T(8,128)(2,1)}) %all-gather.18.cloned.1.call-update) | async-done | bytes 3981328 | tf_op jit(solution)/shard_map/all_gather | solution.py:327
  1055.5 6.9 copy.86
  1062.3 66.3 %all-gather.20.cloned.1.call-done = bf16[1728,1152]{0,1:T(8,128)(2,1)} async-done(((bf16[1728,144]{0,1:T(8,128)(2,1)}), bf16[1728,1152]{0,1:T(8,128)(2,1)}) %all-gather.20.cloned.1.call-update) | async-done | bytes 3981328 | tf_op jit(solution)/shard_map/all_gather | solution.py:330
  1128.6 6.9 copy.87
  1135.5 134.1 %all-reduce.30.cloned.1.call-done = (f32[1152,256]{1,0:T(8,128)}, f32[1152,256]{1,0:T(8,128)}) async-done(((f32[1152,256]{1,0:T(8,128)}, f32[1152,256]{1,0:T(8,128)}), (f32[1152,256]{1,0:T(8,128)}, f32[1152,256]{1,0:T(8,128)})) %all-reduce.30.cloned.1.call-update) | async-done | bytes 2359312 | tf_op jit(solution)/shard_map/psum | solution.py:346
  (351 shorter events, 198.1 us)
Async XLA Ops:
  7.2 39.3 %copy-start = (bf16[1152,256]{1,0:T(8,128)(2,1)S(1)}, bf16[1152,256]{1,0:T(8,128)(2,1)}, u32[]{:S(2)}) copy-start(bf16[1152,256]{1,0:T(8,128)(2,1)} %param.23) | copy-start | bytes 1769476
  7.2 29.2 %all-gather.8.cloned.1.call-start = ((), (), s32[]{:S(2)}) async-start(), calls=%async_computation.7 | async-start | bytes 2949120 | tf_op jit(solution)/shard_map/all_gather | solution.py:107
  7.9 70.9 %all-gather.10.cloned.1.call-start = ((), (), s32[]{:S(2)}) async-start(), calls=%async_computation.8 | async-start | bytes 1572864 | tf_op jit(solution)/shard_map/all_gather | solution.py:135
  9.5 31.1 %copy-start.44 = (f32[1152]{0:T(1024)}, f32[1152]{0:T(1024)S(1)}, u32[]{:S(2)}) copy-start(f32[1152]{0:T(1024)S(1)} %convert_element_type.204) | copy-start | bytes 13828
  10.2 39.4 %copy-start.61 = (f32[256]{0:T(256)}, f32[256]{0:T(256)S(1)}, u32[]{:S(2)}) copy-start(f32[256]{0:T(256)S(1)} %convert_element_type.209) | copy-start | bytes 3076
  10.8 38.4 %copy-start.58 = (f32[256]{0:T(256)}, f32[256]{0:T(256)S(1)}, u32[]{:S(2)}) copy-start(f32[256]{0:T(256)S(1)} %convert_element_type.206) | copy-start | bytes 3076
  39.4 136.2 %copy-start.4 = (bf16[1024,1152]{1,0:T(8,128)(2,1)}, bf16[1024,1152]{1,0:T(8,128)(2,1)S(1)}, u32[]{:S(2)}) copy-start(bf16[1024,1152]{1,0:T(8,128)(2,1)S(1)} %copy.74) | copy-start | bytes 7077892
  57.4 44.9 %all-gather.12.cloned.1.call-start = ((), (), s32[]{:S(2)}) async-start(), calls=%async_computation.9 | async-start | bytes 1572864 | tf_op jit(solution)/shard_map/all_gather | solution.py:136
  60.8 112.6 %all-reduce.22.cloned.1.call-start = ((), (), s32[]{:S(2)}) async-start(), calls=%async_computation.10 | async-start | bytes 4718592 | tf_op jit(solution)/shard_map/psum | solution.py:168
  114.0 61.5 %copy-start.35 = (bf16[2,512,1,256]{3,1,2,0:T(8,128)(2,1)}, bf16[2,512,1,256]{3,1,2,0:T(8,128)(2,1)S(1)}, u32[]{:S(2)}) copy-start(bf16[2,512,1,256]{3,1,2,0:T(8,128)(2,1)S(1)} %get-tuple-element.147) | copy-start | bytes 1572868
  117.6 86.3 %all-gather.14.cloned.1.call-start = ((), (), s32[]{:S(2)}) async-start(), calls=%async_computation.12 | async-start | bytes 2949120 | tf_op jit(solution)/shard_map/all_gather | solution.py:108
  118.2 141.0 %all-reduce.24.cloned.1.call-start = ((), (), s32[]{:S(2)}) async-start(), calls=%async_computation.11 | async-start | bytes 4718592 | tf_op jit(solution)/shard_map/psum | solution.py:179
  203.4 148.4 %all-reduce.26.cloned.1.call-start = ((), (), s32[]{:S(2)}) async-start(), calls=%async_computation.13 | async-start | bytes 4718592 | tf_op jit(solution)/shard_map/psum | solution.py:197
  206.9 60.9 %copy-start.14 = (bf16[1024,1152]{1,0:T(8,128)(2,1)}, bf16[1024,1152]{1,0:T(8,128)(2,1)S(1)}, u32[]{:S(2)}) copy-start(bf16[1024,1152]{1,0:T(8,128)(2,1)S(1)} %copy.77) | copy-start | bytes 7077892
  295.9 61.1 %copy-start.9 = (bf16[1024,1152]{1,0:T(8,128)(2,1)S(1)}, bf16[1024,1152]{1,0:T(8,128)(2,1)}, u32[]{:S(2)}) copy-start(bf16[1024,1152]{1,0:T(8,128)(2,1)} %all-reduce.22.cloned.1.call-done) | copy-start | bytes 7077892
  295.9 153.1 %reduce-scatter.8.cloned.1.call-start = ((), (), s32[]{:S(2)}) async-start(), calls=%async_computation.14 | async-start | bytes 1572864 | tf_op jit(solution)/shard_map/reduce_scatter | solution.py:250
  401.6 61.1 %reduce-scatter.10.cloned.1.call-start = ((), (), s32[]{:S(2)}) async-start(), calls=%async_computation.15 | async-start | bytes 1572864 | tf_op jit(solution)/shard_map/reduce_scatter | solution.py:253
  402.8 133.0 %reduce-scatter.16.cloned.1.call-start = ((), (), s32[]{:S(2)}) async-start(), calls=%async_computation.19 | async-start | bytes 4644864 | tf_op jit(solution)/shard_map/reduce_scatter | solution.py:295
  412.2 214.9 %reduce-scatter.18.cloned.1.call-start = ((), (), s32[]{:S(2)}) async-start(), calls=%async_computation.21 | async-start | bytes 4644864 | tf_op jit(solution)/shard_map/reduce_scatter | solution.py:298
  421.6 296.3 %reduce-scatter.20.cloned.1.call-start = ((), (), s32[]{:S(2)}) async-start(), calls=%async_computation.23 | async-start | bytes 4644864 | tf_op jit(solution)/shard_map/reduce_scatter | solution.py:301
  431.8 352.3 %reduce-scatter.12.cloned.1.call-start = ((), (), s32[]{:S(2)}) async-start(), calls=%async_computation.17 | async-start | bytes 663552 | tf_op jit(solution)/shard_map/reduce_scatter | solution.py:289
  442.1 406.5 %reduce-scatter.14.cloned.1.call-start = ((), (), s32[]{:S(2)}) async-start(), calls=%async_computation.18 | async-start | bytes 663552 | tf_op jit(solution)/shard_map/reduce_scatter | solution.py:292
  448.7 471.3 %all-reduce.28.cloned.1.call-start = ((), (), s32[]{:S(2)}) async-start(), calls=%async_computation.16 | async-start | bytes 4718592 | tf_op jit(solution)/shard_map/psum | solution.py:271
  462.7 255.4 %copy-start.64 = (bf16[1152]{0:T(1024)(128)(2,1)S(1)}, bf16[1152]{0:T(1024)(128)(2,1)}, u32[]{:S(2)}) copy-start(bf16[1152]{0:T(1024)(128)(2,1)} %param.33) | copy-start | bytes 6916
  462.7 255.5 %copy-start.67 = (u32[32]{0:T(128)S(1)}, u32[32]{0:T(128)}, u32[]{:S(2)}) copy-start(u32[32]{0:T(128)} %constant.189) | copy-start | bytes 388
  462.7 257.4 %copy-start.5 = (bf16[1024,1152]{1,0:T(8,128)(2,1)S(1)}, bf16[1024,1152]{1,0:T(8,128)(2,1)}, u32[]{:S(2)}) copy-start(bf16[1024,1152]{1,0:T(8,128)(2,1)} %copy-done.4) | copy-start | bytes 7077892
  467.9 535.3 %all-gather.16.cloned.1.call-start = ((), (), s32[]{:S(2)}) async-start(), calls=%async_computation.20 | async-start | bytes 4644864 | tf_op jit(solution)/shard_map/all_gather | solution.py:324
  535.8 519.7 %all-gather.18.cloned.1.call-start = ((), (), s32[]{:S(2)}) async-start(), calls=%async_computation.22 | async-start | bytes 4644864 | tf_op jit(solution)/shard_map/all_gather | solution.py:327
  627.2 501.5 %all-gather.20.cloned.1.call-start = ((), (), s32[]{:S(2)}) async-start(), calls=%async_computation.24 | async-start | bytes 4644864 | tf_op jit(solution)/shard_map/all_gather | solution.py:330
  718.0 551.6 %all-reduce.30.cloned.1.call-start = ((), (), s32[]{:S(2)}) async-start(), calls=%async_computation.25 | async-start | bytes 4718592 | tf_op jit(solution)/shard_map/psum | solution.py:346
  820.8 99.3 %copy-start.45 = (f32[1152]{0:T(1024)S(1)}, f32[1152]{0:T(1024)}, u32[]{:S(2)}) copy-start(f32[1152]{0:T(1024)} %copy-done.44) | copy-start | bytes 13828
  820.8 99.3 %copy-start.47 = (f32[1024]{0:T(1024)S(1)}, f32[1024]{0:T(1024)}, u32[]{:S(2)}) copy-start(f32[1024]{0:T(1024)} %copy-done.46) | copy-start | bytes 12292
  (71 other events, 294.5 us)
Sparse Core Ops, SparseCore 0:
  9.6 26.7 all-gather.7
  57.5 21.3 all-gather.9
  81.0 21.2 all-gather.11
  117.7 55.6 all-reduce.21
  174.8 24.1 all-gather.13
  203.5 55.6 all-reduce.23
  296.0 55.7 all-reduce.25
  401.7 20.3 reduce-scatter.7
  424.5 20.3 reduce-scatter.9
  448.2 87.4 reduce-scatter.15
  539.8 87.3 reduce-scatter.17
  630.6 87.3 reduce-scatter.19
  722.2 61.8 reduce-scatter.11
  787.2 61.2 reduce-scatter.13
  850.9 55.2 all-reduce.27
  908.5 73.5 all-gather.15
  984.3 71.0 all-gather.17
  1057.7 70.8 all-gather.19
  1135.9 133.7 all-reduce.29
where the time goes:
time: 1290 us; the launch traced here: 1280 us
  waiting for transfers between devices  804 us (62%)
  blocking collectives  173 us (13%)
  matrix products  146 us (11%)
  other arithmetic  82.6 us (6%)
  local copies, waits for them, and re-layouts  56.2 us (4%)
  between operations  16.5 us (1%)
    psum x1, waiting for transfers between devices, shards(): lax.psum((grad_key, grad_value, d_gain_query, d_gain_key), ('dp', 'ctx',...  134 us
    reduce_scatter x1, waiting for transfers between devices, shards(): lax.psum_scatter(sharded[3].astype(jnp.bfloat16), ('dp', 'ctx'), scatter_...  91.3 us
    reduce_scatter x1, waiting for transfers between devices, shards(): lax.psum_scatter(sharded[4].astype(jnp.bfloat16), ('dp', 'ctx'), scatter_...  90.8 us
    dot_general x14, matrix products, contract(): lax.dot_general(left, right, (((left_dim,), (right_dim,)), ((), ())), pre...  79.1 us
    unnamed x2, blocking collectives  71 us
    reduce_scatter x1, waiting for transfers between devices, shards(): lax.psum_scatter(sharded[2].astype(jnp.bfloat16), ('dp', 'ctx'), scatter_...  67.8 us
    all_gather x1, waiting for transfers between devices, shards(): lax.all_gather(reduced[4].astype(jnp.bfloat16), ('dp', 'ctx'), axis=1, ti...  66.3 us
    psum x1, waiting for transfers between devices, shards(): lax.psum((contract(d_gate16, w_gate, 1, 1) + contract(d_up16, w_up, 1, 1)...  55.8 us
  transfers between devices with their start and end apart: 19, of which 14 were waited for; matrix products, arithmetic and copies ran while one was open for 12% of the time, Pallas kernels for 0%

commit v1 on v0

--- a/solution.py
+++ b/solution.py
@@ -363,45 +363,406 @@
     )
 
 
+MESH_PAIR = ((0, 1), (1, 0))
+XOR1 = ((0, 1), (1, 0), (2, 3), (3, 2))
+XOR2 = ((0, 2), (2, 0), (1, 3), (3, 1))
+OUTER_IN = ((0, 1), (3, 2))
+INNER = ((1, 2), (2, 1))
+INNER_OUT = ((1, 0), (2, 3))
+INNER_Y = ((2, 3), (3, 2), (4, 5), (5, 4))
+F32 = jnp.float32
+BF16 = jnp.bfloat16
+
+
+def add16(left, right):
+    return (left.astype(F32) + right.astype(F32)).astype(BF16)
+
+
+def halves(values, index):
+    size = values.shape[0] // 2
+    own = lax.dynamic_slice_in_dim(values, index * size, size)
+    other = lax.dynamic_slice_in_dim(values, (1 - index) * size, size)
+    return own, other
+
+
+def join(own, other, index):
+    first = jnp.where(index == 0, own, other)
+    second = jnp.where(index == 0, other, own)
+    return jnp.concatenate([first, second], axis=0)
+
+
+def tp_sum(values):
+    odd = lax.axis_index("tp") % 2
+    own, other = halves(values, odd)
+    own = add16(own, lax.ppermute(other, "tp", XOR1))
+    own = add16(own, lax.ppermute(own, "tp", XOR2))
+    return join(own, lax.ppermute(own, "tp", XOR1), odd)
+
+
+def tp_gather(part):
+    tp_index = lax.axis_index("tp")
+    near = lax.ppermute(part, "tp", XOR1)
+    far = lax.ppermute(part, "tp", XOR2)
+    both = lax.ppermute(far, "tp", XOR1)
+    blocks = (part, near, far, both)
+    return jnp.concatenate(
+        [lax.select_n(tp_index ^ j, *blocks) for j in range(4)], axis=1
+    )
+
+
+def sum_y_first(grad):
+    ctx_index, dp_index = lax.axis_index("ctx"), lax.axis_index("dp")
+    own, other = halves(grad, ctx_index)
+    own = add16(own, lax.ppermute(other, "ctx", MESH_PAIR))
+    own = add16(own, lax.ppermute(own, "dp", OUTER_IN))
+    own = add16(own, lax.ppermute(own, "dp", INNER))
+    inner = (dp_index == 1) | (dp_index == 2)
+    own = jnp.where(inner, own, lax.ppermute(own, "dp", INNER_OUT))
+    return join(own, lax.ppermute(own, "ctx", MESH_PAIR), ctx_index)
+
+
+def sum_z_first(grad):
+    dp_index = lax.axis_index("dp")
+    upper = dp_index // 2
+    grad = add16(grad, lax.ppermute(grad, "dp", OUTER_IN))
+    own, other = halves(grad, upper)
+    own = add16(own, lax.ppermute(other, "dp", INNER))
+    own = add16(own, lax.ppermute(own, ("dp", "ctx"), INNER_Y))
+    whole = join(own, lax.ppermute(own, "dp", INNER), upper)
+    inner = (dp_index == 1) | (dp_index == 2)
+    return jnp.where(inner, whole, lax.ppermute(whole, "dp", INNER_OUT))
+
+
+def sum_all(values):
+    for axis, pairs in (
+        ("tp", XOR1), ("tp", XOR2), ("ctx", MESH_PAIR), ("dp", XOR1), ("dp", XOR2)
+    ):
+        values = values + lax.ppermute(values, axis, pairs)
+    return values
+
+
+def scale_of(values):
+    return lax.rsqrt(jnp.mean(values * values, axis=-1, keepdims=True) + EPSILON)
+
+
+def rms_back(values, gain, cotangent):
+    scale = scale_of(values)
+    weighted = gain * cotangent
+    inner = jnp.mean(values * weighted, axis=-1, keepdims=True)
+    back = scale * weighted - values * (scale * scale * scale * inner)
+    return back, jnp.sum(cotangent * values * scale, axis=0)
+
+
+def rotate_back(values, cosine_table, sine_table):
+    half_dim = values.shape[-1] // 2
+    turned = values * sine_table
+    turned = jnp.concatenate([turned[..., half_dim:], -turned[..., :half_dim]], axis=-1)
+    return values * cosine_table + turned
+
+
+def positions(block, rows, bucket_row, true_row):
+    stream_pos = block * rows + jnp.arange(rows, dtype=jnp.int32)
+    starts = jnp.cumsum(bucket_row) - bucket_row
+    ends = starts + bucket_row
+    inside = (
+        (stream_pos[:, None] >= starts[None, :]) & (stream_pos[:, None] < ends[None, :])
+    ).astype(jnp.int32)
+    slot_ids = jnp.arange(bucket_row.shape[0], dtype=jnp.int32)
+    seq_id = jnp.sum(inside * slot_ids[None, :], axis=1)
+    seq_pos = stream_pos - jnp.sum(inside * starts[None, :], axis=1)
+    is_valid = (seq_pos < jnp.sum(inside * true_row[None, :], axis=1)).astype(jnp.int32)
+    return seq_id, stream_pos, seq_pos, is_valid
+
+
+def allowed_pairs(query_layout, key_layout):
+    return (
+        (key_layout[3][None, :] == 1)
+        & (key_layout[0][None, :] == query_layout[0][:, None])
+        & (key_layout[1][None, :] <= query_layout[1][:, None])
+    )
+
+
+def attend(query16, key16, value16, allowed, score_scale):
+    scores = contract(query16, key16, 1, 1) * score_scale
+    scores = jnp.where(allowed, scores, MASKED)
+    exp_scores = jnp.exp(scores - jnp.max(scores, axis=-1, keepdims=True))
+    probs = exp_scores / jnp.sum(exp_scores, axis=-1, keepdims=True)
+    attended = jnp.dot(probs.astype(BF16), value16, preferred_element_type=F32)
+    return probs, attended.astype(BF16)
+
+
+def attend_back(query16, key16, value16, probs, d_attended16, score_scale):
+    d_probs = contract(d_attended16, value16, 1, 1)
+    inner = jnp.sum(probs * d_probs, axis=-1, keepdims=True)
+    d_scores16 = (probs * (d_probs - inner)).astype(BF16)
+    d_query = jnp.dot(d_scores16, key16, preferred_element_type=F32) * score_scale
+    d_key = contract(d_scores16, query16, 0, 0) * score_scale
+    d_value = contract(probs.astype(BF16), d_attended16, 0, 0)
+    return d_query, d_key, d_value
+
+
+def paired_shards(
+    tokens,
+    out_grad,
+    w_query,
+    w_key,
+    w_value,
+    w_out,
+    w_gate,
+    w_up,
+    w_down,
+    gain_in,
+    gain_post_attn,
+    gain_pre_ffn,
+    gain_post_ffn,
+    gain_query,
+    gain_key,
+    bucket_lengths,
+    true_lengths,
+):
+    ctx_index, tp_index = lax.axis_index("ctx"), lax.axis_index("tp")
+    rows = tokens.shape[0] // 2
+    feature_cols = tokens.shape[1]
+    head_dim = w_key.shape[1]
+    score_scale = head_dim ** (-0.5)
+    g_in, g_pa, g_pf, g_pff, g_q, g_k = [
+        gain.astype(F32)
+        for gain in (gain_in, gain_post_attn, gain_pre_ffn, gain_post_ffn, gain_query, gain_key)
+    ]
+    both = range(2)
+    token_parts = halves(tokens, ctx_index)
+    cot_parts = halves(out_grad, ctx_index)
+    w_qkv = jnp.concatenate([w_query, w_key, w_value], axis=1)
+
+    blocks = (2 * ctx_index, 3 - 2 * ctx_index, 2 - 2 * ctx_index)
+    layouts = [positions(b, rows, bucket_lengths[0], true_lengths[0]) for b in blocks]
+    tables = [rope_tables(layouts[i][2], head_dim) for i in both]
+    key_layout = [jnp.concatenate([a, b]) for a, b in zip(layouts[2], layouts[1])]
+    allowed = [allowed_pairs(layouts[0], layouts[0]), allowed_pairs(layouts[1], key_layout)]
+
+    inputs16 = [tp_gather(part) for part in token_parts]
+    cots16 = [tp_gather(part) for part in cot_parts]
+    inputs = [values.astype(F32) for values in inputs16]
+    normed16 = [rms_norm(values, g_in).astype(BF16) for values in inputs]
+    raw = [jnp.dot(values, w_qkv, preferred_element_type=F32) for values in normed16]
+    query_raw = [values[:, :head_dim] for values in raw]
+    key_raw = [values[:, head_dim : 2 * head_dim] for values in raw]
+    value16 = [values[:, 2 * head_dim :].astype(BF16) for values in raw]
+    query16 = [rotate(rms_norm(query_raw[i], g_q), *tables[i]).astype(BF16) for i in both]
+    key16 = [rotate(rms_norm(key_raw[i], g_k), *tables[i]).astype(BF16) for i in both]
+    far_key, far_value = [
+        lax.ppermute(values, "ctx", MESH_PAIR) for values in (key16[0], value16[0])
+    ]
+    keys = [key16[0], jnp.concatenate([far_key, key16[1]], axis=0)]
+    values_ = [value16[0], jnp.concatenate([far_value, value16[1]], axis=0)]
+
+    probs, attended16, attention, residual, mid16 = [], [], [], [], []
+    hidden16, gate, up, ffn = [], [], [], []
+    for i in both:
+        p, a = attend(query16[i], keys[i], values_[i], allowed[i], score_scale)
+        probs.append(p)
+        attended16.append(a)
+    for i in both:
+        part = jnp.dot(attended16[i], w_out, preferred_element_type=F32).astype(BF16)
+        attention.append(tp_sum(part).astype(F32))
+        residual.append(inputs[i] + rms_norm(attention[i], g_pa))
+        mid16.append(rms_norm(residual[i], g_pf).astype(BF16))
+        gate.append(jnp.dot(mid16[i], w_gate, preferred_element_type=F32).astype(BF16))
+        up.append(jnp.dot(mid16[i], w_up, preferred_element_type=F32).astype(BF16))
+        hidden16.append(geglu(gate[i].astype(F32), up[i].astype(F32)).astype(BF16))
+        part = jnp.dot(hidden16[i], w_down, preferred_element_type=F32).astype(BF16)
+        ffn.append(tp_sum(part).astype(F32))
+
+    out_parts, d_ffn16, d_gate16, d_up16 = [], [], [], []
+    gain_sums = []
+    cots = [values.astype(F32) for values in cots16]
+    for i in both:
+        outputs = residual[i] + rms_norm(ffn[i], g_pff)
+        out_parts.append(
+            lax.dynamic_slice_in_dim(outputs, tp_index * feature_cols, feature_cols, 1).astype(BF16)
+        )
+        d_ffn, d_pff = rms_back(ffn[i], g_pff, cots[i])
+        d_ffn16.append(d_ffn.astype(BF16))
+        d_hidden = contract(d_ffn16[i], w_down, 1, 1)
+        gate32, up32 = gate[i].astype(F32), up[i].astype(F32)
+        _, pull = jax.vjp(geglu, gate32, up32)
+        d_gate, d_up = pull(d_hidden)
+        d_gate16.append(d_gate.astype(BF16))
+        d_up16.append(d_up.astype(BF16))
+        gain_sums.append(d_pff)
+    hidden_all, mid_all, d_ffn_all, d_gate_all, d_up_all = [
+        jnp.concatenate(pair, axis=0) for pair in (hidden16, mid16, d_ffn16, d_gate16, d_up16)
+    ]
+    grad_down = contract(hidden_all, d_ffn_all, 0, 0).astype(BF16)
+    grad_gate = contract(mid_all, d_gate_all, 0, 0).astype(BF16)
+    grad_up = contract(mid_all, d_up_all, 0, 0).astype(BF16)
+
+    def summed(grad):
+        size = grad.shape[0] // 2
+        return jnp.concatenate([sum_y_first(grad[:size]), sum_z_first(grad[size:])], axis=0).astype(
+            F32
+        )
+
+    down_sum, gate_sum, up_sum = summed(grad_down), summed(grad_gate), summed(grad_up)
+
+    d_resid, d_attn16, d_attended16 = [], [], []
+    pf_sums, pa_sums = [], []
+    for i in both:
+        part = contract(d_gate16[i], w_gate, 1, 1) + contract(d_up16[i], w_up, 1, 1)
+        d_mid = tp_sum(part.astype(BF16)).astype(F32)
+        d_norm, d_pf = rms_back(residual[i], g_pf, d_mid)
+        d_resid.append(cots[i] + d_norm)
+        d_attn, d_pa = rms_back(attention[i], g_pa, d_resid[i])
+        d_attn16.append(d_attn.astype(BF16))
+        d_attended16.append(contract(d_attn16[i], w_out, 1, 1).astype(BF16))
+        pf_sums.append(d_pf)
+        pa_sums.append(d_pa)
+    grad_out = contract(
+        jnp.concatenate(attended16, axis=0), jnp.concatenate(d_attn16, axis=0), 0, 0
+    ).astype(BF16)
+    out_sum = sum_y_first(grad_out).astype(F32)
+
+    d_query, d_key, d_value = [], [], []
+    for i in both:
+        dq, dk, dv = attend_back(
+            query16[i], keys[i], values_[i], probs[i], d_attended16[i], score_scale
+        )
+        d_query.append(dq)
+        d_key.append(dk)
+        d_value.append(dv)
+    far_dk = lax.ppermute(d_key[1][:rows].astype(BF16), "ctx", MESH_PAIR)
+    far_dv = lax.ppermute(d_value[1][:rows].astype(BF16), "ctx", MESH_PAIR)
+    d_key = [d_key[0] + far_dk.astype(F32), d_key[1][rows:]]
+    d_value = [d_value[0] + far_dv.astype(F32), d_value[1][rows:]]
+
+    w_blocks = w_qkv.reshape(4, feature_cols, w_qkv.shape[1])
+    w_near = [
+        lax.dynamic_index_in_dim(w_blocks, tp_index ^ j, keepdims=False) for j in range(4)
+    ]
+    g_in_own = lax.dynamic_slice_in_dim(g_in, tp_index * feature_cols, feature_cols)
+    d_qkv16, x_parts, q_sums, k_sums, in_sums = [], [], [], [], []
+    for i in both:
+        dq, d_gq = rms_back(query_raw[i], g_q, rotate_back(d_query[i], *tables[i]))
+        dk, d_gk = rms_back(key_raw[i], g_k, rotate_back(d_key[i], *tables[i]))
+        q_sums.append(d_gq)
+        k_sums.append(d_gk)
+        d_qkv16.append(jnp.concatenate([dq, dk, d_value[i]], axis=1).astype(BF16))
+        parts = [contract(d_qkv16[i], w, 1, 1).astype(BF16) for w in w_near]
+        near = lax.ppermute(jnp.stack([parts[1], parts[3]]), "tp", XOR1)
+        mine = add16(parts[0], near[0])
+        theirs = add16(parts[2], near[1])
+        u = add16(mine, lax.ppermute(theirs, "tp", XOR2)).astype(F32)
+        own_in = token_parts[i].astype(F32)
+        weighted = g_in_own * u
+        inner = jnp.sum(own_in * weighted, axis=-1)
+        inner = inner + lax.ppermute(inner, "tp", XOR1)
+        inner = inner + lax.ppermute(inner, "tp", XOR2)
+        inner = inner[:, None] / (4 * feature_cols)
+        scale = scale_of(inputs[i])
+        d_in = scale * weighted - own_in * (scale * scale * scale * inner)
+        resid_own = lax.dynamic_slice_in_dim(d_resid[i], tp_index * feature_cols, feature_cols, 1)
+        x_parts.append((resid_own + d_in).astype(BF16))
+        in_sums.append(jnp.sum(u * own_in * scale, axis=0))
+    grad_qkv = contract(
+        jnp.concatenate(normed16, axis=0), jnp.concatenate(d_qkv16, axis=0), 0, 0
+    ).astype(BF16)
+    query_sum = sum_y_first(grad_qkv[:, :head_dim]).astype(F32)
+    kv_blocks = grad_qkv[:, head_dim:].reshape(4, feature_cols, 2 * head_dim)
+    kv = [lax.dynamic_index_in_dim(kv_blocks, tp_index ^ j, keepdims=False) for j in range(4)]
+    near = lax.ppermute(jnp.stack([kv[1], kv[3]]), "tp", XOR1)
+    mine, theirs = add16(kv[0], near[0]), add16(kv[2], near[1])
+    mine = add16(mine, lax.ppermute(theirs, "tp", XOR2))
+    mine = sum_y_first(mine)
+    far = lax.ppermute(mine, "tp", XOR2)
+    near = lax.ppermute(jnp.stack([mine, far]), "tp", XOR1)
+    kv_all = (mine, near[0], far, near[1])
+    kv_sum = jnp.concatenate(
+        [lax.select_n(tp_index ^ j, *kv_all) for j in range(4)], axis=0
+    ).astype(F32)
+
+    width = 4 * feature_cols
+    in_full = lax.dynamic_update_slice_in_dim(
+        jnp.zeros((width,), F32), in_sums[0] + in_sums[1], tp_index * feature_cols, 0
+    )
+    shared = [0.25 * (pair[0] + pair[1]) for pair in (pa_sums, pf_sums, gain_sums)]
+    small = sum_all(
+        jnp.concatenate([in_full, *shared, q_sums[0] + q_sums[1], k_sums[0] + k_sums[1]]).reshape(
+            -1, 128
+        )
+    ).reshape(-1)
+    gains = [small[j * width : (j + 1) * width] for j in range(4)]
+    gain_q_sum = small[4 * width : 4 * width + head_dim]
+    gain_k_sum = small[4 * width + head_dim :]
+    return (
+        join(*out_parts, ctx_index),
+        join(*x_parts, ctx_index),
+        query_sum,
+        kv_sum[:, :head_dim],
+        kv_sum[:, head_dim:],
+        out_sum,
+        gate_sum,
+        up_sum,
+        down_sum,
+        gains[0],
+        gains[1],
+        gains[2],
+        gains[3],
+        gain_q_sum,
+        gain_k_sum,
+    )
+
+
 def solution(mesh):
-    return jax.shard_map(
-        shards,
-        mesh=mesh,
-        in_specs=(
-            P(("dp", "ctx"), "tp"),
-            P(("dp", "ctx"), "tp"),
-            P(None, "tp"),
-            P(),
-            P(),
-            P("tp", None),
-            P(None, "tp"),
-            P(None, "tp"),
-            P("tp", None),
-            P(),
-            P(),
-            P(),
-            P(),
-            P(),
-            P(),
-            P("dp", None),
-            P("dp", None),
-        ),
-        out_specs=(
-            P(("dp", "ctx"), "tp"),
-            P(("dp", "ctx"), "tp"),
-            P(None, "tp"),
-            P(),
-            P(),
-            P("tp", None),
-            P(None, "tp"),
-            P(None, "tp"),
-            P("tp", None),
-            P(),
-            P(),
-            P(),
-            P(),
-            P(),
-            P(),
-        ),
-        check_vma=False,
-    )
+    def layer(*args):
+        tokens, bucket_lengths = args[0], args[-2]
+        sizes = mesh.shape
+        group_rows = tokens.shape[0] // sizes["dp"]
+        paired = (sizes["dp"], sizes["ctx"], sizes["tp"]) == (4, 2, 4) and (
+            group_rows == 1024 * bucket_lengths.shape[1] == 2048
+        )
+        return mapped(paired_shards if paired else shards)(*args)
+
+    def mapped(body):
+        return jax.shard_map(
+            body,
+            mesh=mesh,
+            in_specs=(
+                P(("dp", "ctx"), "tp"),
+                P(("dp", "ctx"), "tp"),
+                P(None, "tp"),
+                P(),
+                P(),
+                P("tp", None),
+                P(None, "tp"),
+                P(None, "tp"),
+                P("tp", None),
+                P(),
+                P(),
+                P(),
+                P(),
+                P(),
+                P(),
+                P("dp", None),
+                P("dp", None),
+            ),
+            out_specs=(
+                P(("dp", "ctx"), "tp"),
+                P(("dp", "ctx"), "tp"),
+                P(None, "tp"),
+                P(),
+                P(),
+                P("tp", None),
+                P(None, "tp"),
+                P(None, "tp"),
+                P("tp", None),
+                P(),
+                P(),
+                P(),
+                P(),
+                P(),
+                P(),
+            ),
+            check_vma=False,
+        )
+
+    return layer

time: 1290 us -> 1000 us (0.78)
  waiting for transfers between devices: 804 us -> 515 us
  blocking collectives: 173 us -> 0 us
  starting transfers between devices: 2.18 us -> 173 us
  matrix products: 146 us -> 94 us
  local copies, waits for them, and re-layouts: 56.2 us -> 90 us
  other arithmetic: 82.6 us -> 116 us
    ppermute x0 -> x96, waiting for transfers between devices: none -> 515 us  [the longest x3 127 us: sum_z_first(): return jnp.where(inner, whole, lax.ppermute(whole, 'dp', INNER_OUT))]
    reduce_scatter x7 -> x0, waiting for transfers between devices: 331 us -> none  [the longest x1 91.3 us: shards(): lax.psum_scatter(sharded[3].astype(jnp.bfloat16), ('dp', 'ctx'), scatter_...]
    psum x5 -> x0, waiting for transfers between devices: 297 us -> none  [the longest x1 134 us: shards(): lax.psum((grad_key, grad_value, d_gain_query, d_gain_key), ('dp', 'ctx',...]
    all_gather x7 -> x0, waiting for transfers between devices: 174 us -> none  [the longest x1 66.3 us: shards(): lax.all_gather(reduced[4].astype(jnp.bfloat16), ('dp', 'ctx'), axis=1, ti...]
    ppermute x0 -> x96, starting transfers between devices: none -> 173 us  [the longest x5 64 us: sum_all(): values = values + lax.ppermute(values, axis, pairs)]
    unnamed x2 -> x0, blocking collectives: 71 us -> none
    all_gather x2 -> x0, blocking collectives: 63.7 us -> none  [the longest x1 31.9 us: shards(): lax.all_gather(reduced[0].astype(jnp.bfloat16), ('dp', 'ctx'), axis=0, ti...]
    dot_general x21 -> x14, matrix products: 67.4 us -> 28.2 us  [the longest x2 9.43 us: paired_shards(): up.append(jnp.dot(mid16[i], w_up, preferred_element_type=F32).astype(BF16))]
  transfers between devices with their start and end apart: 19 -> 96, of which waited for: 14 -> 37; matrix products, arithmetic and copies ran while one was open for 12% -> 21% of each run, Pallas kernels for 0% -> 0%
where the time goes in v1:
time: 1000 us; the launch traced here: 993 us
  waiting for transfers between devices  515 us (52%)
  starting transfers between devices  173 us (17%)
  other arithmetic  116 us (12%)
  matrix products  94 us (9%)
  local copies, waits for them, and re-layouts  90 us (9%)
    ppermute x3, waiting for transfers between devices, sum_z_first(): return jnp.where(inner, whole, lax.ppermute(whole, 'dp', INNER_OUT))  127 us
    ppermute x6, waiting for transfers between devices, sum_y_first(): own = add16(own, lax.ppermute(own, 'dp', OUTER_IN))  107 us
    ppermute x6, waiting for transfers between devices, sum_y_first(): return join(own, lax.ppermute(own, 'ctx', MESH_PAIR), ctx_index)  69.2 us
    dot_general x29, matrix products, contract(): lax.dot_general(left, right, (((left_dim,), (right_dim,)), ((), ())), pre...  65.8 us
    ppermute x5, starting transfers between devices, sum_all(): values = values + lax.ppermute(values, axis, pairs)  64 us
    ppermute x6, waiting for transfers between devices, sum_y_first(): own = add16(own, lax.ppermute(other, 'ctx', MESH_PAIR))  55.2 us
    unnamed x451, local copies, waits for them, and re-layouts  53.6 us
    ppermute x6, waiting for transfers between devices, sum_y_first(): own = jnp.where(inner, own, lax.ppermute(own, 'dp', INNER_OUT))  52.5 us
  transfers between devices with their start and end apart: 96, of which 37 were waited for; matrix products, arithmetic and copies ran while one was open for 21% of the time, Pallas kernels for 0%

profile of v1, /device:TPU:0, one launch (start us, length us, event | category | flops | bytes accessed | tf_op | source)
XLA Modules:
  0.0 993.2 jit_solution(14877096088547732393)
XLA Ops:
  9.7 6.4 collective-permute-done.10
  18.3 5.5 collective-permute-done.1
  54.5 13.9 %collective-permute-done.4 = bf16[256,1152]{1,0:T(8,128)(2,1)S(1)} collective-permute-done((bf16[256,1152]{1,0:T(8,128)(2,1)S(1)}, bf16[256,1152]{1,0:T(8,128)(2,1)S(1)}, u32[]{:S(2)}, u32[]{:S(2)}) %collective-permute-start.4) | collective-permute-done | bytes 589856 | tf_op jit(solution)/shard_map/ppermute | solution.py:398
  73.6 7.8 collective-permute-done.21
  126.7 5.1 multiply_convert_fusion.1
  147.5 9.2 collective-permute-done.15
  158.5 6.6 collective-permute-done.27
  165.2 11.6 %collective-permute-done.24 = bf16[256,1152]{1,0:T(8,128)(2,1)S(1)} collective-permute-done((bf16[256,1152]{1,0:T(8,128)(2,1)S(1)}, bf16[256,1152]{1,0:T(8,128)(2,1)S(1)}, u32[]{:S(2)}, u32[]{:S(2)}) %collective-permute-start.24) | collective-permute-done | bytes 589856 | tf_op jit(solution)/shard_map/ppermute | solution.py:398
  190.6 4.7 fusion.3
  213.3 13.1 %collective-permute-done.18 = bf16[256,1152]{1,0:T(8,128)(2,1)S(1)} collective-permute-done((bf16[256,1152]{1,0:T(8,128)(2,1)S(1)}, bf16[256,1152]{1,0:T(8,128)(2,1)S(1)}, u32[]{:S(2)}, u32[]{:S(2)}) %collective-permute-start.18) | collective-permute-done | bytes 589856 | tf_op jit(solution)/shard_map/ppermute | solution.py:398
  234.7 5.8 multiply_convert_fusion
  244.7 6.7 convolution_convert_fusion.2
  251.4 6.5 convolution_convert_fusion
  263.4 6.8 convolution_convert_fusion.1
  285.6 17.9 %collective-permute-done.61 = bf16[288,1728]{1,0:T(8,128)(2,1)S(1)} collective-permute-done((bf16[288,1728]{1,0:T(8,128)(2,1)S(1)}, bf16[288,1728]{1,0:T(8,128)(2,1)S(1)}, u32[]{:S(2)}, u32[]{:S(2)}) %collective-permute-start.61) | collective-permute-done | bytes 995360 | tf_op jit(solution)/shard_map/ppermute | solution.py:416
  308.1 17.5 %collective-permute-done.71 = bf16[288,1728]{1,0:T(8,128)(2,1)S(1)} collective-permute-done((bf16[288,1728]{1,0:T(8,128)(2,1)S(1)}, bf16[288,1728]{1,0:T(8,128)(2,1)S(1)}, u32[]{:S(2)}, u32[]{:S(2)}) %collective-permute-start.71) | collective-permute-done | bytes 995360 | tf_op jit(solution)/shard_map/ppermute | solution.py:416
  325.9 19.8 %collective-permute-done.81 = bf16[432,1152]{1,0:T(8,128)(2,1)S(1)} collective-permute-done((bf16[432,1152]{1,0:T(8,128)(2,1)S(1)}, bf16[432,1152]{1,0:T(8,128)(2,1)S(1)}, u32[]{:S(2)}, u32[]{:S(2)}) %collective-permute-start.81) | collective-permute-done | bytes 995360 | tf_op jit(solution)/shard_map/ppermute | solution.py:416
  368.6 63.2 %collective-permute-done.62 = bf16[288,1728]{1,0:T(8,128)(2,1)} collective-permute-done((bf16[288,1728]{1,0:T(8,128)(2,1)S(1)}, bf16[288,1728]{1,0:T(8,128)(2,1)}, u32[]{:S(2)}, u32[]{:S(2)}) %collective-permute-start.62) | collective-permute-done | bytes 995360 | tf_op jit(solution)/shard_map/ppermute | solution.py:417
  438.9 14.2 %collective-permute-done.82 = bf16[432,1152]{1,0:T(8,128)(2,1)} collective-permute-done((bf16[432,1152]{1,0:T(8,128)(2,1)S(1)}, bf16[432,1152]{1,0:T(8,128)(2,1)}, u32[]{:S(2)}, u32[]{:S(2)}) %collective-permute-start.82) | collective-permute-done | bytes 995360 | tf_op jit(solution)/shard_map/ppermute | solution.py:417
  457.1 17.2 %collective-permute-done.72 = bf16[288,1728]{1,0:T(8,128)(2,1)S(1)} collective-permute-done((bf16[288,1728]{1,0:T(8,128)(2,1)S(1)}, bf16[288,1728]{1,0:T(8,128)(2,1)S(1)}, u32[]{:S(2)}, u32[]{:S(2)}) %collective-permute-start.72) | collective-permute-done | bytes 995360 | tf_op jit(solution)/shard_map/ppermute | solution.py:417
  503.8 6.8 collective-permute-start.57
  511.6 5.6 collective-permute-done.57
  522.4 5.1 collective-permute-done.43
  598.2 58.2 %collective-permute-start.94 = (f32[40,128]{1,0:T(8,128)S(1)}, f32[40,128]{1,0:T(8,128)S(1)}, u32[]{:S(2)}, u32[]{:S(2)}) collective-permute-start(f32[40,128]{1,0:T(8,128)S(1)} %add.692), channel_id=1, source_target_pairs={{0,8},{8,0},{16,24},{24,16},{1,9},{9,1},{17,25},{25,17},{2,10},{10... | collective-permute-start | bytes 61448 | tf_op jit(solution)/shard_map/ppermute | solution.py:440
  678.7 50.5 %collective-permute-done.52 = bf16[144,512]{1,0:T(8,128)(2,1)S(1)} collective-permute-done((bf16[144,512]{1,0:T(8,128)(2,1)S(1)}, bf16[144,512]{1,0:T(8,128)(2,1)S(1)}, u32[]{:S(2)}, u32[]{:S(2)}) %collective-permute-start.52) | collective-permute-done | bytes 147488 | tf_op jit(solution)/shard_map/ppermute | solution.py:420
  737.5 5.1 collective-permute-done.46
  760.0 60.1 %collective-permute-done.85 = bf16[432,1152]{1,0:T(8,128)(2,1)S(1)} collective-permute-done((bf16[432,1152]{1,0:T(8,128)(2,1)S(1)}, bf16[432,1152]{1,0:T(8,128)(2,1)S(1)}, u32[]{:S(2)}, u32[]{:S(2)}) %collective-permute-start.85) | collective-permute-done | bytes 995360 | tf_op jit(solution)/shard_map/ppermute | solution.py:421
  832.8 75.7 %collective-permute-done.70 = bf16[576,1728]{1,0:T(8,128)(2,1)S(1)} collective-permute-done((bf16[576,1728]{1,0:T(8,128)(2,1)S(1)}, bf16[576,1728]{1,0:T(8,128)(2,1)S(1)}, u32[]{:S(2)}, u32[]{:S(2)}) %collective-permute-start.70) | collective-permute-done | bytes 1990688 | tf_op jit(solution)/shard_map/ppermute | solution.py:433
  912.5 8.8 copy.202
  921.3 31.5 %collective-permute-done.80 = bf16[576,1728]{1,0:T(8,128)(2,1)} collective-permute-done((bf16[576,1728]{1,0:T(8,128)(2,1)}, bf16[576,1728]{1,0:T(8,128)(2,1)}, u32[]{:S(2)}, u32[]{:S(2)}) %collective-permute-start.80) | collective-permute-done | bytes 1990688 | tf_op jit(solution)/shard_map/ppermute | solution.py:433
  958.4 8.9 copy.203
  967.4 19.5 %collective-permute-done.90 = bf16[864,1152]{1,0:T(8,128)(2,1)} collective-permute-done((bf16[864,1152]{1,0:T(8,128)(2,1)}, bf16[864,1152]{1,0:T(8,128)(2,1)}, u32[]{:S(2)}, u32[]{:S(2)}) %collective-permute-start.90) | collective-permute-done | bytes 1990688 | tf_op jit(solution)/shard_map/ppermute | solution.py:433
  (885 shorter events, 392.6 us)
Async XLA Ops:
  158.0 44.7 %collective-permute-start.26 = (bf16[512,288]{1,0:T(8,128)(2,1)}, bf16[512,288]{1,0:T(8,128)(2,1)}, u32[]{:S(2)}, u32[]{:S(2)}) collective-permute-start(bf16[512,288]{1,0:T(8,128)(2,1)} %copy.219), channel_id=1, source_target_pairs={{0,1},{1,0},{2,3},{3,2},{4,5},{5,4},{6,7},{7,6},{8,9},{9,8},{10,11... | collective-permute-start | bytes 884744 | tf_op jit(solution)/shard_map/ppermute | solution.py:404
  165.2 37.6 %collective-permute-start.28 = (bf16[512,288]{1,0:T(8,128)(2,1)}, bf16[512,288]{1,0:T(8,128)(2,1)}, u32[]{:S(2)}, u32[]{:S(2)}) collective-permute-start(bf16[512,288]{1,0:T(8,128)(2,1)} %collective-permute-done.27), channel_id=1, source_target_pairs={{0,1},{1,0},{2,3},{3,2},{4,5},{5,4},{6,7},{7,6},{8,9},{9,8},{10,11... | collective-permute-start | bytes 884744 | tf_op jit(solution)/shard_map/ppermute | solution.py:406
  273.8 203.3 %collective-permute-start.66 = (bf16[576,1728]{1,0:T(8,128)(2,1)S(1)}, bf16[576,1728]{1,0:T(8,128)(2,1)S(1)}, u32[]{:S(2)}, u32[]{:S(2)}) collective-permute-start(bf16[576,1728]{1,0:T(8,128)(2,1)S(1)} %get-tuple-element.146), channel_id=1, source_target_pairs={{0,8},{24,16},{1,9},{25,17},{2,10},{26,18},{3,11},{27,19},{4,12},{... | collective-permute-start | bytes 5971976 | tf_op jit(solution)/shard_map/ppermute | solution.py:427
  279.6 199.7 %collective-permute-start.76 = (bf16[576,1728]{1,0:T(8,128)(2,1)S(1)}, bf16[576,1728]{1,0:T(8,128)(2,1)S(1)}, u32[]{:S(2)}, u32[]{:S(2)}) collective-permute-start(bf16[576,1728]{1,0:T(8,128)(2,1)S(1)} %get-tuple-element.144), channel_id=1, source_target_pairs={{0,8},{24,16},{1,9},{25,17},{2,10},{26,18},{3,11},{27,19},{4,12},{... | collective-permute-start | bytes 5971976 | tf_op jit(solution)/shard_map/ppermute | solution.py:427
  281.7 43.8 %collective-permute-start.71 = (bf16[288,1728]{1,0:T(8,128)(2,1)S(1)}, bf16[288,1728]{1,0:T(8,128)(2,1)S(1)}, u32[]{:S(2)}, u32[]{:S(2)}) collective-permute-start(bf16[288,1728]{1,0:T(8,128)(2,1)S(1)} %constant_dynamic-slice_fusion.3), channel_id=1, source_target_pairs={{0,4},{4,0},{1,5},{5,1},{2,6},{6,2},{3,7},{7,3},{8,12},{12,8},{9,1... | collective-permute-start | bytes 2985992 | tf_op jit(solution)/shard_map/ppermute | solution.py:416
  303.4 179.7 %collective-permute-start.86 = (bf16[864,1152]{1,0:T(8,128)(2,1)}, bf16[864,1152]{1,0:T(8,128)(2,1)}, u32[]{:S(2)}, u32[]{:S(2)}) collective-permute-start(bf16[864,1152]{1,0:T(8,128)(2,1)} %get-tuple-element.148), channel_id=1, source_target_pairs={{0,8},{24,16},{1,9},{25,17},{2,10},{26,18},{3,11},{27,19},{4,12},{... | collective-permute-start | bytes 5971976 | tf_op jit(solution)/shard_map/ppermute | solution.py:427
  306.3 39.4 %collective-permute-start.81 = (bf16[432,1152]{1,0:T(8,128)(2,1)S(1)}, bf16[432,1152]{1,0:T(8,128)(2,1)S(1)}, u32[]{:S(2)}, u32[]{:S(2)}) collective-permute-start(bf16[432,1152]{1,0:T(8,128)(2,1)S(1)} %constant_dynamic-slice_fusion.1), channel_id=1, source_target_pairs={{0,4},{4,0},{1,5},{5,1},{2,6},{6,2},{3,7},{7,3},{8,12},{12,8},{9,1... | collective-permute-start | bytes 2985992 | tf_op jit(solution)/shard_map/ppermute | solution.py:416
  345.6 86.1 %collective-permute-start.62 = (bf16[288,1728]{1,0:T(8,128)(2,1)S(1)}, bf16[288,1728]{1,0:T(8,128)(2,1)}, u32[]{:S(2)}, u32[]{:S(2)}) collective-permute-start(bf16[288,1728]{1,0:T(8,128)(2,1)S(1)} %add_convert_fusion.12), channel_id=1, source_target_pairs={{0,8},{24,16},{1,9},{25,17},{2,10},{26,18},{3,11},{27,19},{4,12},{... | collective-permute-start | bytes 2985992 | tf_op jit(solution)/shard_map/ppermute | solution.py:417
  348.4 104.7 %collective-permute-start.82 = (bf16[432,1152]{1,0:T(8,128)(2,1)S(1)}, bf16[432,1152]{1,0:T(8,128)(2,1)}, u32[]{:S(2)}, u32[]{:S(2)}) collective-permute-start(bf16[432,1152]{1,0:T(8,128)(2,1)S(1)} %add_convert_fusion.17), channel_id=1, source_target_pairs={{0,8},{24,16},{1,9},{25,17},{2,10},{26,18},{3,11},{27,19},{4,12},{... | collective-permute-start | bytes 2985992 | tf_op jit(solution)/shard_map/ppermute | solution.py:417
  431.8 42.5 %collective-permute-start.72 = (bf16[288,1728]{1,0:T(8,128)(2,1)S(1)}, bf16[288,1728]{1,0:T(8,128)(2,1)S(1)}, u32[]{:S(2)}, u32[]{:S(2)}) collective-permute-start(bf16[288,1728]{1,0:T(8,128)(2,1)S(1)} %add_convert_fusion.7), channel_id=1, source_target_pairs={{0,8},{24,16},{1,9},{25,17},{2,10},{26,18},{3,11},{27,19},{4,12},{... | collective-permute-start | bytes 2985992 | tf_op jit(solution)/shard_map/ppermute | solution.py:417
  453.1 35.0 %collective-permute-start.32 = (bf16[512,256]{1,0:T(8,128)(2,1)S(1)}, bf16[512,256]{1,0:T(8,128)(2,1)S(1)}, u32[]{:S(2)}, u32[]{:S(2)}) collective-permute-start(bf16[512,256]{1,0:T(8,128)(2,1)S(1)} %slice.341), channel_id=1, source_target_pairs={{0,4},{4,0},{1,5},{5,1},{2,6},{6,2},{3,7},{7,3},{8,12},{12,8},{9,1... | collective-permute-start | bytes 786440 | tf_op jit(solution)/shard_map/ppermute | solution.py:633
  479.8 111.0 %collective-permute-start.63 = (bf16[288,1728]{1,0:T(8,128)(2,1)}, bf16[288,1728]{1,0:T(8,128)(2,1)}, u32[]{:S(2)}, u32[]{:S(2)}) collective-permute-start(bf16[288,1728]{1,0:T(8,128)(2,1)} %add_convert_fusion.11), channel_id=1, source_target_pairs={{8,16},{16,8},{9,17},{17,9},{10,18},{18,10},{11,19},{19,11},{12,20... | collective-permute-start | bytes 2985992 | tf_op jit(solution)/shard_map/ppermute | solution.py:418
  483.1 110.8 %collective-permute-start.73 = (bf16[288,1728]{1,0:T(8,128)(2,1)}, bf16[288,1728]{1,0:T(8,128)(2,1)}, u32[]{:S(2)}, u32[]{:S(2)}) collective-permute-start(bf16[288,1728]{1,0:T(8,128)(2,1)} %add_convert_fusion.6), channel_id=1, source_target_pairs={{8,16},{16,8},{9,17},{17,9},{10,18},{18,10},{11,19},{19,11},{12,20... | collective-permute-start | bytes 2985992 | tf_op jit(solution)/shard_map/ppermute | solution.py:418
  551.0 37.3 %collective-permute-start.83 = (bf16[432,1152]{1,0:T(8,128)(2,1)}, bf16[432,1152]{1,0:T(8,128)(2,1)}, u32[]{:S(2)}, u32[]{:S(2)}) collective-permute-start(bf16[432,1152]{1,0:T(8,128)(2,1)} %add_convert_fusion.16), channel_id=1, source_target_pairs={{8,16},{16,8},{9,17},{17,9},{10,18},{18,10},{11,19},{19,11},{12,20... | collective-permute-start | bytes 2985992 | tf_op jit(solution)/shard_map/ppermute | solution.py:418
  587.5 72.0 %collective-permute-start.77 = (bf16[288,1728]{1,0:T(8,128)(2,1)S(1)}, bf16[288,1728]{1,0:T(8,128)(2,1)S(1)}, u32[]{:S(2)}, u32[]{:S(2)}) collective-permute-start(bf16[288,1728]{1,0:T(8,128)(2,1)S(1)} %copy-done.90), channel_id=1, source_target_pairs={{8,16},{16,8},{9,17},{17,9},{10,18},{18,10},{11,19},{19,11},{12,20... | collective-permute-start | bytes 2985992 | tf_op jit(solution)/shard_map/ppermute | solution.py:429
  590.7 85.0 %collective-permute-start.45 = (bf16[576,256]{1,0:T(8,128)(2,1)S(1)}, bf16[576,256]{1,0:T(8,128)(2,1)S(1)}, u32[]{:S(2)}, u32[]{:S(2)}) collective-permute-start(bf16[576,256]{1,0:T(8,128)(2,1)S(1)} %copy-done.76), channel_id=1, source_target_pairs={{8,0},{16,24},{9,1},{17,25},{10,2},{18,26},{11,3},{19,27},{12,4},{... | collective-permute-start | bytes 884744 | tf_op jit(solution)/shard_map/ppermute | solution.py:420
  594.0 73.1 %collective-permute-start.49 = (bf16[144,512]{1,0:T(8,128)(2,1)S(1)}, bf16[144,512]{1,0:T(8,128)(2,1)S(1)}, u32[]{:S(2)}, u32[]{:S(2)}) collective-permute-start(bf16[144,512]{1,0:T(8,128)(2,1)S(1)} %copy-done.113), channel_id=1, source_target_pairs={{0,4},{4,0},{1,5},{5,1},{2,6},{6,2},{3,7},{7,3},{8,12},{12,8},{9,1... | collective-permute-start | bytes 442376 | tf_op jit(solution)/shard_map/ppermute | solution.py:416
  596.4 80.9 %collective-permute-start.60 = (bf16[128,1152]{1,0:T(8,128)(2,1)S(1)}, bf16[128,1152]{1,0:T(8,128)(2,1)S(1)}, u32[]{:S(2)}, u32[]{:S(2)}) collective-permute-start(bf16[128,1152]{1,0:T(8,128)(2,1)S(1)} %broadcast_select_fusion.34), channel_id=1, source_target_pairs={{0,4},{4,0},{1,5},{5,1},{2,6},{6,2},{3,7},{7,3},{8,12},{12,8},{9,1... | collective-permute-start | bytes 884744 | tf_op jit(solution)/shard_map/ppermute | solution.py:421
  598.2 60.0 %collective-permute-start.94 = (f32[40,128]{1,0:T(8,128)S(1)}, f32[40,128]{1,0:T(8,128)S(1)}, u32[]{:S(2)}, u32[]{:S(2)}) collective-permute-start(f32[40,128]{1,0:T(8,128)S(1)} %add.692), channel_id=1, source_target_pairs={{0,8},{8,0},{16,24},{24,16},{1,9},{9,1},{17,25},{25,17},{2,10},{10... | collective-permute-start | bytes 61448 | tf_op jit(solution)/shard_map/ppermute | solution.py:440
  658.2 93.0 %collective-permute-start.64 = (bf16[288,1728]{1,0:T(8,128)(2,1)S(1)}, bf16[288,1728]{1,0:T(8,128)(2,1)S(1)}, u32[]{:S(2)}, u32[]{:S(2)}) collective-permute-start(bf16[288,1728]{1,0:T(8,128)(2,1)S(1)} %add_convert_fusion.10), channel_id=1, source_target_pairs={{8,0},{16,24},{9,1},{17,25},{10,2},{18,26},{11,3},{19,27},{12,4},{... | collective-permute-start | bytes 2985992 | tf_op jit(solution)/shard_map/ppermute | solution.py:420
  665.2 86.2 %collective-permute-start.74 = (bf16[288,1728]{1,0:T(8,128)(2,1)S(1)}, bf16[288,1728]{1,0:T(8,128)(2,1)S(1)}, u32[]{:S(2)}, u32[]{:S(2)}) collective-permute-start(bf16[288,1728]{1,0:T(8,128)(2,1)S(1)} %add_convert_fusion.5), channel_id=1, source_target_pairs={{8,0},{16,24},{9,1},{17,25},{10,2},{18,26},{11,3},{19,27},{12,4},{... | collective-permute-start | bytes 2985992 | tf_op jit(solution)/shard_map/ppermute | solution.py:420
  674.4 75.7 %collective-permute-start.84 = (bf16[432,1152]{1,0:T(8,128)(2,1)S(1)}, bf16[432,1152]{1,0:T(8,128)(2,1)S(1)}, u32[]{:S(2)}, u32[]{:S(2)}) collective-permute-start(bf16[432,1152]{1,0:T(8,128)(2,1)S(1)} %add_convert_fusion.15), channel_id=1, source_target_pairs={{8,0},{16,24},{9,1},{17,25},{10,2},{18,26},{11,3},{19,27},{12,4},{... | collective-permute-start | bytes 2985992 | tf_op jit(solution)/shard_map/ppermute | solution.py:420
  676.5 76.7 %collective-permute-start.68 = (bf16[288,1728]{1,0:T(8,128)(2,1)S(1)}, bf16[288,1728]{1,0:T(8,128)(2,1)S(1)}, u32[]{:S(2)}, u32[]{:S(2)}) collective-permute-start(bf16[288,1728]{1,0:T(8,128)(2,1)S(1)} %add_convert_fusion.9), channel_id=1, source_target_pairs={{8,12},{12,8},{16,20},{20,16},{9,13},{13,9},{17,21},{21,17},{10,14... | collective-permute-start | bytes 2985992 | tf_op jit(solution)/shard_map/ppermute | solution.py:430
  677.3 51.8 %collective-permute-start.52 = (bf16[144,512]{1,0:T(8,128)(2,1)S(1)}, bf16[144,512]{1,0:T(8,128)(2,1)S(1)}, u32[]{:S(2)}, u32[]{:S(2)}) collective-permute-start(bf16[144,512]{1,0:T(8,128)(2,1)S(1)} %add_convert_fusion.41), channel_id=1, source_target_pairs={{8,0},{16,24},{9,1},{17,25},{10,2},{18,26},{11,3},{19,27},{12,4},{... | collective-permute-start | bytes 442376 | tf_op jit(solution)/shard_map/ppermute | solution.py:420
  751.4 70.9 %collective-permute-start.65 = (bf16[288,1728]{1,0:T(8,128)(2,1)S(1)}, bf16[288,1728]{1,0:T(8,128)(2,1)S(1)}, u32[]{:S(2)}, u32[]{:S(2)}) collective-permute-start(bf16[288,1728]{1,0:T(8,128)(2,1)S(1)} %broadcast_select_fusion.8), channel_id=1, source_target_pairs={{0,4},{4,0},{1,5},{5,1},{2,6},{6,2},{3,7},{7,3},{8,12},{12,8},{9,1... | collective-permute-start | bytes 2985992 | tf_op jit(solution)/shard_map/ppermute | solution.py:421
  753.2 71.1 %collective-permute-start.75 = (bf16[288,1728]{1,0:T(8,128)(2,1)S(1)}, bf16[288,1728]{1,0:T(8,128)(2,1)S(1)}, u32[]{:S(2)}, u32[]{:S(2)}) collective-permute-start(bf16[288,1728]{1,0:T(8,128)(2,1)S(1)} %broadcast_select_fusion.7), channel_id=1, source_target_pairs={{0,4},{4,0},{1,5},{5,1},{2,6},{6,2},{3,7},{7,3},{8,12},{12,8},{9,1... | collective-permute-start | bytes 2985992 | tf_op jit(solution)/shard_map/ppermute | solution.py:421
  754.0 66.1 %collective-permute-start.85 = (bf16[432,1152]{1,0:T(8,128)(2,1)S(1)}, bf16[432,1152]{1,0:T(8,128)(2,1)S(1)}, u32[]{:S(2)}, u32[]{:S(2)}) collective-permute-start(bf16[432,1152]{1,0:T(8,128)(2,1)S(1)} %broadcast_select_fusion.15), channel_id=1, source_target_pairs={{0,4},{4,0},{1,5},{5,1},{2,6},{6,2},{3,7},{7,3},{8,12},{12,8},{9,1... | collective-permute-start | bytes 2985992 | tf_op jit(solution)/shard_map/ppermute | solution.py:421
  755.9 66.7 %collective-permute-start.69 = (bf16[288,1728]{1,0:T(8,128)(2,1)S(1)}, bf16[288,1728]{1,0:T(8,128)(2,1)S(1)}, u32[]{:S(2)}, u32[]{:S(2)}) collective-permute-start(bf16[288,1728]{1,0:T(8,128)(2,1)S(1)} %add_convert_fusion.8), channel_id=1, source_target_pairs={{8,16},{16,8},{9,17},{17,9},{10,18},{18,10},{11,19},{19,11},{12,20... | collective-permute-start | bytes 2985992 | tf_op jit(solution)/shard_map/ppermute | solution.py:431
  756.9 68.9 %collective-permute-start.79 = (bf16[288,1728]{1,0:T(8,128)(2,1)S(1)}, bf16[288,1728]{1,0:T(8,128)(2,1)S(1)}, u32[]{:S(2)}, u32[]{:S(2)}) collective-permute-start(bf16[288,1728]{1,0:T(8,128)(2,1)S(1)} %add_convert_fusion.3), channel_id=1, source_target_pairs={{8,16},{16,8},{9,17},{17,9},{10,18},{18,10},{11,19},{19,11},{12,20... | collective-permute-start | bytes 2985992 | tf_op jit(solution)/shard_map/ppermute | solution.py:431
  822.9 85.5 %collective-permute-start.70 = (bf16[576,1728]{1,0:T(8,128)(2,1)S(1)}, bf16[576,1728]{1,0:T(8,128)(2,1)S(1)}, u32[]{:S(2)}, u32[]{:S(2)}) collective-permute-start(bf16[576,1728]{1,0:T(8,128)(2,1)S(1)} %pad_maximum_fusion.1), channel_id=1, source_target_pairs={{8,0},{16,24},{9,1},{17,25},{10,2},{18,26},{11,3},{19,27},{12,4},{... | collective-permute-start | bytes 5971976 | tf_op jit(solution)/shard_map/ppermute | solution.py:433
  827.6 125.2 %collective-permute-start.80 = (bf16[576,1728]{1,0:T(8,128)(2,1)}, bf16[576,1728]{1,0:T(8,128)(2,1)}, u32[]{:S(2)}, u32[]{:S(2)}) collective-permute-start(bf16[576,1728]{1,0:T(8,128)(2,1)} %pad_maximum_fusion.2), channel_id=1, source_target_pairs={{8,0},{16,24},{9,1},{17,25},{10,2},{18,26},{11,3},{19,27},{12,4},{... | collective-permute-start | bytes 5971976 | tf_op jit(solution)/shard_map/ppermute | solution.py:433
  831.5 155.4 %collective-permute-start.90 = (bf16[864,1152]{1,0:T(8,128)(2,1)}, bf16[864,1152]{1,0:T(8,128)(2,1)}, u32[]{:S(2)}, u32[]{:S(2)}) collective-permute-start(bf16[864,1152]{1,0:T(8,128)(2,1)} %pad_maximum_fusion.3), channel_id=1, source_target_pairs={{8,0},{16,24},{9,1},{17,25},{10,2},{18,26},{11,3},{19,27},{12,4},{... | collective-permute-start | bytes 5971976 | tf_op jit(solution)/shard_map/ppermute | solution.py:433
  (282 other events, 2572.0 us)

commit v2 on v1

--- a/solution.py
+++ b/solution.py
@@ -3,6 +3,8 @@
 import jax
 import jax.numpy as jnp
 from jax import lax
+from jax.experimental import pallas as pl
+from jax.experimental.pallas import tpu as pltpu
 from jax.sharding import PartitionSpec as P
 
 QBLK = 512
@@ -366,10 +368,7 @@
 MESH_PAIR = ((0, 1), (1, 0))
 XOR1 = ((0, 1), (1, 0), (2, 3), (3, 2))
 XOR2 = ((0, 2), (2, 0), (1, 3), (3, 1))
-OUTER_IN = ((0, 1), (3, 2))
-INNER = ((1, 2), (2, 1))
-INNER_OUT = ((1, 0), (2, 3))
-INNER_Y = ((2, 3), (3, 2), (4, 5), (5, 4))
+MESH = pl.DeviceIdType.MESH
 F32 = jnp.float32
 BF16 = jnp.bfloat16
 
@@ -410,35 +409,147 @@
     )
 
 
-def sum_y_first(grad):
-    ctx_index, dp_index = lax.axis_index("ctx"), lax.axis_index("dp")
-    own, other = halves(grad, ctx_index)
-    own = add16(own, lax.ppermute(other, "ctx", MESH_PAIR))
-    own = add16(own, lax.ppermute(own, "dp", OUTER_IN))
-    own = add16(own, lax.ppermute(own, "dp", INNER))
-    inner = (dp_index == 1) | (dp_index == 2)
-    own = jnp.where(inner, own, lax.ppermute(own, "dp", INNER_OUT))
-    return join(own, lax.ppermute(own, "ctx", MESH_PAIR), ctx_index)
-
-
-def sum_z_first(grad):
-    dp_index = lax.axis_index("dp")
-    upper = dp_index // 2
-    grad = add16(grad, lax.ppermute(grad, "dp", OUTER_IN))
-    own, other = halves(grad, upper)
-    own = add16(own, lax.ppermute(other, "dp", INNER))
-    own = add16(own, lax.ppermute(own, ("dp", "ctx"), INNER_Y))
-    whole = join(own, lax.ppermute(own, "dp", INNER), upper)
-    inner = (dp_index == 1) | (dp_index == 2)
-    return jnp.where(inner, whole, lax.ppermute(whole, "dp", INNER_OUT))
-
-
 def sum_all(values):
     for axis, pairs in (
         ("tp", XOR1), ("tp", XOR2), ("ctx", MESH_PAIR), ("dp", XOR1), ("dp", XOR2)
     ):
         values = values + lax.ppermute(values, axis, pairs)
     return values
+
+
+def grid_sum_kernel(s, K, L, g, out, Y2, Z2, M2, Z1, M1, Y1, *sems):
+    sy2, sz2, sm2, sfo, sfy, sz1, sm1, sy1, sfm, sfa, sfb = sems[:11]
+    ry2, rz2, rm2, rfo, rfy, rz1, rm1, ry1, rfm, rfa, rfb = sems[11:]
+    dp, ctx, tp = lax.axis_index("dp"), lax.axis_index("ctx"), lax.axis_index("tp")
+    upper = dp // 2
+    outer = (dp == 0) | (dp == 3)
+    inner = jnp.logical_not(outer)
+    zn = jnp.where(dp < 2, 1 - dp, 5 - dp)
+    zm = 3 - dp
+    ypeer, zpeer, mpeer = (dp, 1 - ctx, tp), (zn, ctx, tp), (zm, ctx, tp)
+    bar = pltpu.get_barrier_semaphore()
+    pl.semaphore_signal(bar, inc=1, device_id=ypeer, device_id_type=MESH)
+    pl.semaphore_signal(bar, inc=1, device_id=zpeer, device_id_type=MESH)
+    pl.when(inner)(lambda: pl.semaphore_signal(bar, inc=1, device_id=mpeer, device_id_type=MESH))
+    pl.semaphore_wait(bar, jnp.where(inner, 3, 2))
+    base1 = 2 * s * K
+    def rows2(k, h): return pl.ds(pl.multiple_of((2 * k + h) * s, s), s)
+    def rows1(k, h): return pl.ds(pl.multiple_of(base1 + (2 * k + h) * s, s), s)
+    def pair1(k): return pl.ds(pl.multiple_of(base1 + 2 * k * s, s), 2 * s)
+    def slot(k, n=1): return pl.ds(pl.multiple_of(k * n * s, s), n * s)
+    def half1(k, h): return pl.ds(pl.multiple_of((2 * k + h) * s, s), s)
+    def cp(src, dst, ss, rs, k, dev):
+        return pltpu.make_async_remote_copy(src_ref=src, dst_ref=dst, send_sem=ss.at[k], recv_sem=rs.at[k], device_id=dev, device_id_type=MESH)
+    def c_y2(k): return cp(g.at[rows2(k, 1 - ctx)], Y2.at[slot(k)], sy2, ry2, k, ypeer)
+    def c_z2(k): return cp(Y2.at[slot(k)], Z2.at[slot(k)], sz2, rz2, k, zpeer)
+    def c_m2(k): return cp(Z2.at[slot(k)], M2.at[slot(k)], sm2, rm2, k, mpeer)
+    def c_fo(k): return cp(out.at[rows2(k, ctx)], out.at[rows2(k, ctx)], sfo, rfo, k, zpeer)
+    def c_fy(k): return cp(out.at[rows2(k, ctx)], out.at[rows2(k, ctx)], sfy, rfy, k, ypeer)
+    def c_z1(k): return cp(g.at[pair1(k)], Z1.at[slot(k, 2)], sz1, rz1, k, zpeer)
+    def c_m1(k): return cp(Z1.at[half1(k, 1 - upper)], M1.at[slot(k)], sm1, rm1, k, mpeer)
+    def c_y1(k): return cp(M1.at[slot(k)], Y1.at[slot(k)], sy1, ry1, k, ypeer)
+    def c_fm(k): return cp(out.at[rows1(k, upper)], out.at[rows1(k, upper)], sfm, rfm, k, mpeer)
+    def c_fa(k): return cp(out.at[rows1(k, upper)], out.at[rows1(k, upper)], sfa, rfa, k, zpeer)
+    def c_fb(k): return cp(out.at[rows1(k, 1 - upper)], out.at[rows1(k, 1 - upper)], sfb, rfb, k, zpeer)
+    def add(a, b): return (a.astype(F32) + b.astype(F32)).astype(BF16)
+    def at(t, lag, cond, fn):
+        k = t - lag
+        pl.when(cond & (k >= 0) & (k < K))(lambda: fn(k))
+    yes = dp >= 0
+    def a2(k):
+        c_y2(k).start()
+    def a1(k):
+        c_z1(k).start()
+    def b2(k):
+        c_y2(k).wait_recv()
+        Y2[slot(k)] = add(Y2[slot(k)], g[rows2(k, ctx)])
+        pl.when(outer)(lambda: c_z2(k).start())
+    def b1(k):
+        c_z1(k).wait_recv()
+        Z1[slot(k, 2)] = add(Z1[slot(k, 2)], g[pair1(k)])
+        c_m1(k).start()
+    def c2(k):
+        c_z2(k).wait_recv()
+        Z2[slot(k)] = add(Z2[slot(k)], Y2[slot(k)])
+        c_m2(k).start()
+    def c1(k):
+        c_m1(k).wait_recv()
+        M1[slot(k)] = add(M1[slot(k)], Z1[half1(k, upper)])
+        c_y1(k).start()
+    def d2(k):
+        c_m2(k).wait_recv()
+        out[rows2(k, ctx)] = add(M2[slot(k)], Z2[slot(k)])
+        c_fo(k).start()
+        c_fy(k).start()
+    def d1(k):
+        c_y1(k).wait_recv()
+        out[rows1(k, upper)] = add(Y1[slot(k)], M1[slot(k)])
+        c_fm(k).start()
+        c_fa(k).start()
+    def e2(k):
+        c_fo(k).wait_recv()
+        c_fy(k).start()
+    def e1(k):
+        c_fm(k).wait_recv()
+        c_fb(k).start()
+    def f2(k):
+        c_fy(k).wait_recv()
+        c_y2(k).wait_send()
+        c_fy(k).wait_send()
+    def f2o(k):
+        c_z2(k).wait_send()
+    def f2i(k):
+        c_m2(k).wait_send()
+        c_fo(k).wait_send()
+    def f1o(k):
+        c_fa(k).wait_recv()
+        c_fb(k).wait_recv()
+        c_z1(k).wait_send()
+    def f1i(k):
+        c_m1(k).wait_send()
+        c_y1(k).wait_send()
+        c_fm(k).wait_send()
+        c_fa(k).wait_send()
+        c_fb(k).wait_send()
+    def body(t, carry):
+        at(t, 5 * L, yes, f2)
+        at(t, 5 * L, outer, f2o)
+        at(t, 5 * L, inner, f2i)
+        at(t, 5 * L, outer, f1o)
+        at(t, 5 * L, inner, f1i)
+        at(t, 4 * L, outer, e2)
+        at(t, 4 * L, inner, e1)
+        at(t, 3 * L, inner, d2)
+        at(t, 3 * L, inner, d1)
+        at(t, 2 * L, inner, c2)
+        at(t, 2 * L, inner, c1)
+        at(t, L, yes, b2)
+        at(t, L, inner, b1)
+        at(t, 0, yes, a2)
+        at(t, 0, outer, a1)
+        return carry
+    lax.fori_loop(0, K + 5 * L, body, 0)
+
+def grid_sum(grads):
+    step_rows, lag = 48, 1
+    rows, width = grads.shape
+    steps = rows // (4 * step_rows)
+
+    def slots(n):
+        return pltpu.VMEM((n * step_rows * steps, width), BF16)
+
+    return pl.pallas_call(
+        partial(grid_sum_kernel, step_rows, steps, lag),
+        out_shape=jax.ShapeDtypeStruct(grads.shape, BF16),
+        in_specs=[pl.BlockSpec(memory_space=pltpu.VMEM)],
+        out_specs=pl.BlockSpec(memory_space=pltpu.VMEM),
+        scratch_shapes=[slots(n) for n in (1, 1, 1, 2, 1, 1)]
+        + [pltpu.SemaphoreType.DMA((steps,)) for _ in range(22)],
+        name="grid_sum",
+        compiler_params=pltpu.CompilerParams(
+            collective_id=1, has_side_effects=True, vmem_limit_bytes=62 << 20
+        ),
+    )(grads)
 
 
 def scale_of(values):
@@ -594,16 +705,8 @@
         jnp.concatenate(pair, axis=0) for pair in (hidden16, mid16, d_ffn16, d_gate16, d_up16)
     ]
     grad_down = contract(hidden_all, d_ffn_all, 0, 0).astype(BF16)
-    grad_gate = contract(mid_all, d_gate_all, 0, 0).astype(BF16)
-    grad_up = contract(mid_all, d_up_all, 0, 0).astype(BF16)
-
-    def summed(grad):
-        size = grad.shape[0] // 2
-        return jnp.concatenate([sum_y_first(grad[:size]), sum_z_first(grad[size:])], axis=0).astype(
-            F32
-        )
-
-    down_sum, gate_sum, up_sum = summed(grad_down), summed(grad_gate), summed(grad_up)
+    grad_gate = contract(d_gate_all, mid_all, 0, 0).astype(BF16)
+    grad_up = contract(d_up_all, mid_all, 0, 0).astype(BF16)
 
     d_resid, d_attn16, d_attended16 = [], [], []
     pf_sums, pa_sums = [], []
@@ -620,7 +723,6 @@
     grad_out = contract(
         jnp.concatenate(attended16, axis=0), jnp.concatenate(d_attn16, axis=0), 0, 0
     ).astype(BF16)
-    out_sum = sum_y_first(grad_out).astype(F32)
 
     d_query, d_key, d_value = [], [], []
     for i in both:
@@ -664,21 +766,29 @@
         x_parts.append((resid_own + d_in).astype(BF16))
         in_sums.append(jnp.sum(u * own_in * scale, axis=0))
     grad_qkv = contract(
-        jnp.concatenate(normed16, axis=0), jnp.concatenate(d_qkv16, axis=0), 0, 0
+        jnp.concatenate(d_qkv16, axis=0), jnp.concatenate(normed16, axis=0), 0, 0
     ).astype(BF16)
-    query_sum = sum_y_first(grad_qkv[:, :head_dim]).astype(F32)
-    kv_blocks = grad_qkv[:, head_dim:].reshape(4, feature_cols, 2 * head_dim)
+    grad_query = grad_qkv[:head_dim]
+    kv_blocks = grad_qkv[head_dim:].reshape(4, head_dim // 2, -1)
     kv = [lax.dynamic_index_in_dim(kv_blocks, tp_index ^ j, keepdims=False) for j in range(4)]
     near = lax.ppermute(jnp.stack([kv[1], kv[3]]), "tp", XOR1)
     mine, theirs = add16(kv[0], near[0]), add16(kv[2], near[1])
-    mine = add16(mine, lax.ppermute(theirs, "tp", XOR2))
-    mine = sum_y_first(mine)
+    grad_kv = add16(mine, lax.ppermute(theirs, "tp", XOR2))
+    grads = [grad_down, grad_gate, grad_up, grad_out, grad_query, grad_kv]
+    sizes = [grad.shape[0] for grad in grads]
+    spare = -sum(sizes) % 192
+    grads.append(jnp.zeros((spare, grad_down.shape[1]), BF16))
+    sums = grid_sum(jnp.concatenate(grads, axis=0))
+    ends = [sum(sizes[: j + 1]) for j in range(6)]
+    down_sum, gate_sum, up_sum, out_sum, query_sum, mine = [
+        sums[end - size : end] for size, end in zip(sizes, ends)
+    ]
     far = lax.ppermute(mine, "tp", XOR2)
     near = lax.ppermute(jnp.stack([mine, far]), "tp", XOR1)
     kv_all = (mine, near[0], far, near[1])
     kv_sum = jnp.concatenate(
         [lax.select_n(tp_index ^ j, *kv_all) for j in range(4)], axis=0
-    ).astype(F32)
+    ).astype(F32).T
 
     width = 4 * feature_cols
     in_full = lax.dynamic_update_slice_in_dim(
@@ -696,13 +806,13 @@
     return (
         join(*out_parts, ctx_index),
         join(*x_parts, ctx_index),
-        query_sum,
+        query_sum.astype(F32).T,
         kv_sum[:, :head_dim],
         kv_sum[:, head_dim:],
-        out_sum,
-        gate_sum,
-        up_sum,
-        down_sum,
+        out_sum.astype(F32),
+        gate_sum.astype(F32).T,
+        up_sum.astype(F32).T,
+        down_sum.astype(F32),
         gains[0],
         gains[1],
         gains[2],

time: 1000 us -> 661 us (0.66)
  waiting for transfers between devices: 515 us -> 108 us
  Pallas kernels: 0 us -> 257 us
  starting transfers between devices: 173 us -> 36.4 us
  other arithmetic: 116 us -> 90.2 us
  local copies, waits for them, and re-layouts: 90 us -> 64.4 us
    ppermute x46 -> x1, waiting for transfers between devices: 415 us -> 5.25 us  [paired_shards(): grad_kv = add16(mine, lax.ppermute(theirs, 'tp', XOR2))]
    pallas_call x0 -> x1, Pallas kernels: none -> 257 us  [grid_sum(): pl.pallas_call(partial(grid_sum_kernel, step_rows, steps, lag), out_shape...]
    ppermute x46 -> x1, starting transfers between devices: 77.4 us -> 0.16 us  [paired_shards(): grad_kv = add16(mine, lax.ppermute(theirs, 'tp', XOR2))]
    ppermute x5, starting transfers between devices: 64 us -> 3.74 us  [sum_all(): values = values + lax.ppermute(values, axis, pairs)]
    convert_element_type x41 -> x13, other arithmetic: 33.1 us -> 8.37 us  [add16(): return (left.astype(F32) + right.astype(F32)).astype(BF16)]
    unnamed x451 -> x403, local copies, waits for them, and re-layouts: 53.6 us -> 33.6 us
  transfers between devices with their start and end apart: 96 -> 51, of which waited for: 37 -> 19; matrix products, arithmetic and copies ran while one was open for 21% -> 26% of each run, Pallas kernels for 0% -> 39%
where the time goes in v2:
time: 661 us; the launch traced here: 653 us
  Pallas kernels  257 us (39%)
  waiting for transfers between devices  108 us (16%)
  matrix products  92.9 us (14%)
  other arithmetic  90.2 us (14%)
  local copies, waits for them, and re-layouts  64.4 us (10%)
  starting transfers between devices  36.4 us (6%)
    pallas_call x1, Pallas kernels, grid_sum(): pl.pallas_call(partial(grid_sum_kernel, step_rows, steps, lag), out_shape...  257 us
    dot_general x29, matrix products, contract(): lax.dot_general(left, right, (((left_dim,), (right_dim,)), ((), ())), pre...  64.7 us
    ppermute x6, waiting for transfers between devices, tp_sum(): own = add16(own, lax.ppermute(own, 'tp', XOR2))  58.6 us
    unnamed x403, local copies, waits for them, and re-layouts  33.6 us
    ppermute x4, waiting for transfers between devices, tp_gather(): far = lax.ppermute(part, 'tp', XOR2)  26.5 us
    reduce_sum x8, other arithmetic, rms_back(): return (back, jnp.sum(cotangent * values * scale, axis=0))  16 us
    concatenate x4, local copies, waits for them, and re-layouts, tp_gather(): jnp.concatenate([lax.select_n(tp_index ^ j, *blocks) for j in range(4)],...  13.4 us
  transfers between devices with their start and end apart: 51, of which 19 were waited for; matrix products, arithmetic and copies ran while one was open for 26% of the time, Pallas kernels for 39%

profile of v2, /device:TPU:0, one launch (start us, length us, event | category | flops | bytes accessed | tf_op | source)
XLA Modules:
  0.0 653.1 jit_solution(10793949358575241713)
XLA Ops:
  3.2 3.0 collective-permute-start.10
  9.7 6.4 collective-permute-done.10
  18.2 5.6 collective-permute-done.1
  26.1 2.7 concatenate.142
  31.7 2.9 concatenate.135
  54.3 13.9 %collective-permute-done.4 = bf16[256,1152]{1,0:T(8,128)(2,1)S(1)} collective-permute-done((bf16[256,1152]{1,0:T(8,128)(2,1)S(1)}, bf16[256,1152]{1,0:T(8,128)(2,1)S(1)}, u32[]{:S(2)}, u32[]{:S(2)}) %collective-permute-start.4) | collective-permute-done | bytes 589856 | tf_op jit(solution)/shard_map/ppermute | solution.py:397
  73.4 7.8 %collective-permute-done.21 = bf16[512,288]{1,0:T(8,128)(2,1)} collective-permute-done((bf16[512,288]{1,0:T(8,128)(2,1)S(1)}, bf16[512,288]{1,0:T(8,128)(2,1)}, u32[]{:S(2)}, u32[]{:S(2)}) %collective-permute-start.21) | collective-permute-done | bytes 294944 | tf_op jit(solution)/shard_map/ppermute | solution.py:404
  92.5 4.7 fusion.5
  100.9 3.0 select_select_fusion.4
  105.8 2.8 fusion.166
  108.7 3.7 concatenate.155
  115.0 4.5 collective-permute-done.7
  127.3 5.1 multiply_convert_fusion.1
  148.0 9.3 %collective-permute-done.15 = bf16[256,1152]{1,0:T(8,128)(2,1)} collective-permute-done((bf16[256,1152]{1,0:T(8,128)(2,1)S(1)}, bf16[256,1152]{1,0:T(8,128)(2,1)}, u32[]{:S(2)}, u32[]{:S(2)}) %collective-permute-start.15) | collective-permute-done | bytes 589856 | tf_op jit(solution)/shard_map/ppermute | solution.py:397
  159.0 6.6 %collective-permute-done.27 = bf16[512,288]{1,0:T(8,128)(2,1)} collective-permute-done((bf16[512,288]{1,0:T(8,128)(2,1)}, bf16[512,288]{1,0:T(8,128)(2,1)}, u32[]{:S(2)}, u32[]{:S(2)}) %collective-permute-start.27) | collective-permute-done | bytes 294944 | tf_op jit(solution)/shard_map/ppermute | solution.py:404
  165.7 11.6 %collective-permute-done.24 = bf16[256,1152]{1,0:T(8,128)(2,1)S(1)} collective-permute-done((bf16[256,1152]{1,0:T(8,128)(2,1)S(1)}, bf16[256,1152]{1,0:T(8,128)(2,1)S(1)}, u32[]{:S(2)}, u32[]{:S(2)}) %collective-permute-start.24) | collective-permute-done | bytes 589856 | tf_op jit(solution)/shard_map/ppermute | solution.py:397
  181.3 3.1 fusion.73
  184.5 3.2 multiply_reduce_fusion.1
  191.0 4.7 fusion.6
  205.8 4.1 concatenate.158
  215.2 11.9 %collective-permute-done.18 = bf16[256,1152]{1,0:T(8,128)(2,1)S(1)} collective-permute-done((bf16[256,1152]{1,0:T(8,128)(2,1)S(1)}, bf16[256,1152]{1,0:T(8,128)(2,1)S(1)}, u32[]{:S(2)}, u32[]{:S(2)}) %collective-permute-start.18) | collective-permute-done | bytes 589856 | tf_op jit(solution)/shard_map/ppermute | solution.py:397
  241.6 6.4 multiply_convert_fusion
  254.0 6.2 fusion.2
  262.0 6.2 fusion.1
  268.2 7.4 %collective-permute-done.30 = bf16[256,1152]{1,0:T(8,128)(2,1)S(1)} collective-permute-done((bf16[256,1152]{1,0:T(8,128)(2,1)S(1)}, bf16[256,1152]{1,0:T(8,128)(2,1)S(1)}, u32[]{:S(2)}, u32[]{:S(2)}) %collective-permute-start.30) | collective-permute-done | bytes 589856 | tf_op jit(solution)/shard_map/ppermute | solution.py:397
  275.9 6.2 fusion
  285.1 3.3 fusion.80
  335.9 5.2 collective-permute-done.43
  343.7 256.9 %grid_sum.1 = bf16[5952,1152]{1,0:T(8,128)(2,1)} custom-call(bf16[5952,1152]{1,0:T(8,128)(2,1)} %broadcast_dynamic-update-slice_fusion.g), custom_call_target="tpu_custom_call" | custom-call | tf_op jit(solution)/shard_map/grid_sum/pallas_call | solution.py:541
  603.1 11.6 %slice_convert_fusion = (f32[1728,1152]{1,0:T(8,128)}, f32[1152,1728]{0,1:T(8,128)}, f32[1152,1728]{0,1:T(8,128)}) fusion(bf16[5952,1152]{1,0:T(8,128)(2,1)} %grid_sum.1), kind=kLoop, calls=%fused_computation.34 | loop fusion | flops 5971968 | bytes 35831808 | tf_op jit(solution)/shard_map/convert_element_type | solution.py:815
  625.2 5.1 collective-permute-done.37
  638.2 3.5 collective-permute-done.49
  (685 shorter events, 210.3 us)
Async XLA Ops:
  3.2 12.9 %collective-permute-start.10 = (bf16[512,288]{1,0:T(8,128)(2,1)S(1)}, bf16[512,288]{1,0:T(8,128)(2,1)S(1)}, u32[]{:S(2)}, u32[]{:S(2)}) collective-permute-start(bf16[512,288]{1,0:T(8,128)(2,1)S(1)} %copy.112), channel_id=1, source_target_pairs={{0,2},{2,0},{1,3},{3,1},{4,6},{6,4},{5,7},{7,5},{8,10},{10,8},{9,1... | collective-permute-start | bytes 884744 | tf_op jit(solution)/shard_map/ppermute | solution.py:404
  6.2 17.7 %collective-permute-start.9 = (bf16[512,288]{1,0:T(8,128)(2,1)S(1)}, bf16[512,288]{1,0:T(8,128)(2,1)}, u32[]{:S(2)}, u32[]{:S(2)}) collective-permute-start(bf16[512,288]{1,0:T(8,128)(2,1)S(1)} %copy.112), channel_id=1, source_target_pairs={{0,1},{1,0},{2,3},{3,2},{4,5},{5,4},{6,7},{7,6},{8,9},{9,8},{10,11... | collective-permute-start | bytes 884744 | tf_op jit(solution)/shard_map/ppermute | solution.py:403
  6.4 17.4 %collective-permute-start.1 = (bf16[512,288]{1,0:T(8,128)(2,1)S(1)}, bf16[512,288]{1,0:T(8,128)(2,1)}, u32[]{:S(2)}, u32[]{:S(2)}) collective-permute-start(bf16[512,288]{1,0:T(8,128)(2,1)S(1)} %copy.111), channel_id=1, source_target_pairs={{0,2},{2,0},{1,3},{3,1},{4,6},{6,4},{5,7},{7,5},{8,10},{10,8},{9,1... | collective-permute-start | bytes 884744 | tf_op jit(solution)/shard_map/ppermute | solution.py:404
  6.6 22.6 %collective-permute-start = (bf16[512,288]{1,0:T(8,128)(2,1)S(1)}, bf16[512,288]{1,0:T(8,128)(2,1)}, u32[]{:S(2)}, u32[]{:S(2)}) collective-permute-start(bf16[512,288]{1,0:T(8,128)(2,1)S(1)} %copy.111), channel_id=1, source_target_pairs={{0,1},{1,0},{2,3},{3,2},{4,5},{5,4},{6,7},{7,6},{8,9},{9,8},{10,11... | collective-permute-start | bytes 884744 | tf_op jit(solution)/shard_map/ppermute | solution.py:403
  52.5 15.7 %collective-permute-start.4 = (bf16[256,1152]{1,0:T(8,128)(2,1)S(1)}, bf16[256,1152]{1,0:T(8,128)(2,1)S(1)}, u32[]{:S(2)}, u32[]{:S(2)}) collective-permute-start(bf16[256,1152]{1,0:T(8,128)(2,1)S(1)} %add_convert_fusion.11), channel_id=1, source_target_pairs={{0,2},{2,0},{1,3},{3,1},{4,6},{6,4},{5,7},{7,5},{8,10},{10,8},{9,1... | collective-permute-start | bytes 1769480 | tf_op jit(solution)/shard_map/ppermute | solution.py:397
  68.3 17.5 %collective-permute-start.5 = (bf16[256,1152]{1,0:T(8,128)(2,1)S(1)}, bf16[256,1152]{1,0:T(8,128)(2,1)}, u32[]{:S(2)}, u32[]{:S(2)}) collective-permute-start(bf16[256,1152]{1,0:T(8,128)(2,1)S(1)} %add_convert_fusion.10), channel_id=1, source_target_pairs={{0,1},{1,0},{2,3},{3,2},{4,5},{5,4},{6,7},{7,6},{8,9},{9,8},{10,11... | collective-permute-start | bytes 1769480 | tf_op jit(solution)/shard_map/ppermute | solution.py:398
  69.6 11.7 %collective-permute-start.21 = (bf16[512,288]{1,0:T(8,128)(2,1)S(1)}, bf16[512,288]{1,0:T(8,128)(2,1)}, u32[]{:S(2)}, u32[]{:S(2)}) collective-permute-start(bf16[512,288]{1,0:T(8,128)(2,1)S(1)} %copy.113), channel_id=1, source_target_pairs={{0,2},{2,0},{1,3},{3,1},{4,6},{6,4},{5,7},{7,5},{8,10},{10,8},{9,1... | collective-permute-start | bytes 884744 | tf_op jit(solution)/shard_map/ppermute | solution.py:404
  71.4 29.5 %collective-permute-start.20 = (bf16[512,288]{1,0:T(8,128)(2,1)S(1)}, bf16[512,288]{1,0:T(8,128)(2,1)}, u32[]{:S(2)}, u32[]{:S(2)}) collective-permute-start(bf16[512,288]{1,0:T(8,128)(2,1)S(1)} %copy.113), channel_id=1, source_target_pairs={{0,1},{1,0},{2,3},{3,2},{4,5},{5,4},{6,7},{7,6},{8,9},{9,8},{10,11... | collective-permute-start | bytes 884744 | tf_op jit(solution)/shard_map/ppermute | solution.py:403
  81.3 19.6 %collective-permute-start.22 = (bf16[512,288]{1,0:T(8,128)(2,1)}, bf16[512,288]{1,0:T(8,128)(2,1)S(1)}, u32[]{:S(2)}, u32[]{:S(2)}) collective-permute-start(bf16[512,288]{1,0:T(8,128)(2,1)} %collective-permute-done.21), channel_id=1, source_target_pairs={{0,1},{1,0},{2,3},{3,2},{4,5},{5,4},{6,7},{7,6},{8,9},{9,8},{10,11... | collective-permute-start | bytes 884744 | tf_op jit(solution)/shard_map/ppermute | solution.py:405
  83.8 28.6 %collective-permute-start.12 = (bf16[512,256]{1,0:T(8,128)(2,1)}, bf16[512,256]{1,0:T(8,128)(2,1)}, u32[]{:S(2)}, u32[]{:S(2)}) collective-permute-start(bf16[512,256]{1,0:T(8,128)(2,1)} %copy-done.67), channel_id=1, source_target_pairs={{0,4},{4,0},{1,5},{5,1},{2,6},{6,2},{3,7},{7,3},{8,12},{12,8},{9,1... | collective-permute-start | bytes 786440 | tf_op jit(solution)/shard_map/ppermute | solution.py:665
  85.6 35.2 %collective-permute-start.13 = (bf16[512,256]{1,0:T(8,128)(2,1)}, bf16[512,256]{1,0:T(8,128)(2,1)}, u32[]{:S(2)}, u32[]{:S(2)}) collective-permute-start(bf16[512,256]{1,0:T(8,128)(2,1)} %slice.345), channel_id=1, source_target_pairs={{0,4},{4,0},{1,5},{5,1},{2,6},{6,2},{3,7},{7,3},{8,12},{12,8},{9,1... | collective-permute-start | bytes 786440 | tf_op jit(solution)/shard_map/ppermute | solution.py:665
  104.0 15.4 %collective-permute-start.7 = (bf16[256,1152]{1,0:T(8,128)(2,1)S(1)}, bf16[256,1152]{1,0:T(8,128)(2,1)}, u32[]{:S(2)}, u32[]{:S(2)}) collective-permute-start(bf16[256,1152]{1,0:T(8,128)(2,1)S(1)} %add_convert_fusion.9), channel_id=1, source_target_pairs={{0,2},{2,0},{1,3},{3,1},{4,6},{6,4},{5,7},{7,5},{8,10},{10,8},{9,1... | collective-permute-start | bytes 1769480 | tf_op jit(solution)/shard_map/ppermute | solution.py:397
  122.9 17.9 %collective-permute-start.14 = (bf16[256,1152]{1,0:T(8,128)(2,1)S(1)}, bf16[256,1152]{1,0:T(8,128)(2,1)S(1)}, u32[]{:S(2)}, u32[]{:S(2)}) collective-permute-start(bf16[256,1152]{1,0:T(8,128)(2,1)S(1)} %constant_dynamic-slice_fusion.7), channel_id=1, source_target_pairs={{0,1},{1,0},{2,3},{3,2},{4,5},{5,4},{6,7},{7,6},{8,9},{9,8},{10,11... | collective-permute-start | bytes 1769480 | tf_op jit(solution)/shard_map/ppermute | solution.py:396
  140.9 16.4 %collective-permute-start.15 = (bf16[256,1152]{1,0:T(8,128)(2,1)S(1)}, bf16[256,1152]{1,0:T(8,128)(2,1)}, u32[]{:S(2)}, u32[]{:S(2)}) collective-permute-start(bf16[256,1152]{1,0:T(8,128)(2,1)S(1)} %add_convert_fusion.7), channel_id=1, source_target_pairs={{0,2},{2,0},{1,3},{3,1},{4,6},{6,4},{5,7},{7,5},{8,10},{10,8},{9,1... | collective-permute-start | bytes 1769480 | tf_op jit(solution)/shard_map/ppermute | solution.py:397
  144.5 21.2 %collective-permute-start.27 = (bf16[512,288]{1,0:T(8,128)(2,1)}, bf16[512,288]{1,0:T(8,128)(2,1)}, u32[]{:S(2)}, u32[]{:S(2)}) collective-permute-start(bf16[512,288]{1,0:T(8,128)(2,1)} %copy.114), channel_id=1, source_target_pairs={{0,2},{2,0},{1,3},{3,1},{4,6},{6,4},{5,7},{7,5},{8,10},{10,8},{9,1... | collective-permute-start | bytes 884744 | tf_op jit(solution)/shard_map/ppermute | solution.py:404
  146.3 31.1 %collective-permute-start.24 = (bf16[256,1152]{1,0:T(8,128)(2,1)S(1)}, bf16[256,1152]{1,0:T(8,128)(2,1)S(1)}, u32[]{:S(2)}, u32[]{:S(2)}) collective-permute-start(bf16[256,1152]{1,0:T(8,128)(2,1)S(1)} %add_convert_fusion.3), channel_id=1, source_target_pairs={{0,2},{2,0},{1,3},{3,1},{4,6},{6,4},{5,7},{7,5},{8,10},{10,8},{9,1... | collective-permute-start | bytes 1769480 | tf_op jit(solution)/shard_map/ppermute | solution.py:397
  158.5 19.1 %collective-permute-start.16 = (bf16[256,1152]{1,0:T(8,128)(2,1)S(1)}, bf16[256,1152]{1,0:T(8,128)(2,1)S(1)}, u32[]{:S(2)}, u32[]{:S(2)}) collective-permute-start(bf16[256,1152]{1,0:T(8,128)(2,1)S(1)} %add_convert_fusion.6), channel_id=1, source_target_pairs={{0,1},{1,0},{2,3},{3,2},{4,5},{5,4},{6,7},{7,6},{8,9},{9,8},{10,11... | collective-permute-start | bytes 1769480 | tf_op jit(solution)/shard_map/ppermute | solution.py:398
  158.6 44.6 %collective-permute-start.26 = (bf16[512,288]{1,0:T(8,128)(2,1)}, bf16[512,288]{1,0:T(8,128)(2,1)}, u32[]{:S(2)}, u32[]{:S(2)}) collective-permute-start(bf16[512,288]{1,0:T(8,128)(2,1)} %copy.114), channel_id=1, source_target_pairs={{0,1},{1,0},{2,3},{3,2},{4,5},{5,4},{6,7},{7,6},{8,9},{9,8},{10,11... | collective-permute-start | bytes 884744 | tf_op jit(solution)/shard_map/ppermute | solution.py:403
  165.7 37.5 %collective-permute-start.28 = (bf16[512,288]{1,0:T(8,128)(2,1)}, bf16[512,288]{1,0:T(8,128)(2,1)}, u32[]{:S(2)}, u32[]{:S(2)}) collective-permute-start(bf16[512,288]{1,0:T(8,128)(2,1)} %collective-permute-done.27), channel_id=1, source_target_pairs={{0,1},{1,0},{2,3},{3,2},{4,5},{5,4},{6,7},{7,6},{8,9},{9,8},{10,11... | collective-permute-start | bytes 884744 | tf_op jit(solution)/shard_map/ppermute | solution.py:405
  200.3 9.6 %collective-permute-start.17 = (bf16[256,1152]{1,0:T(8,128)(2,1)}, bf16[256,1152]{1,0:T(8,128)(2,1)}, u32[]{:S(2)}, u32[]{:S(2)}) collective-permute-start(bf16[256,1152]{1,0:T(8,128)(2,1)} %constant_dynamic-slice_fusion.6), channel_id=1, source_target_pairs={{0,1},{1,0},{2,3},{3,2},{4,5},{5,4},{6,7},{7,6},{8,9},{9,8},{10,11... | collective-permute-start | bytes 1769480 | tf_op jit(solution)/shard_map/ppermute | solution.py:396
  211.4 15.7 %collective-permute-start.18 = (bf16[256,1152]{1,0:T(8,128)(2,1)S(1)}, bf16[256,1152]{1,0:T(8,128)(2,1)S(1)}, u32[]{:S(2)}, u32[]{:S(2)}) collective-permute-start(bf16[256,1152]{1,0:T(8,128)(2,1)S(1)} %add_convert_fusion.5), channel_id=1, source_target_pairs={{0,2},{2,0},{1,3},{3,1},{4,6},{6,4},{5,7},{7,5},{8,10},{10,8},{9,1... | collective-permute-start | bytes 1769480 | tf_op jit(solution)/shard_map/ppermute | solution.py:397
  260.3 15.4 %collective-permute-start.30 = (bf16[256,1152]{1,0:T(8,128)(2,1)S(1)}, bf16[256,1152]{1,0:T(8,128)(2,1)S(1)}, u32[]{:S(2)}, u32[]{:S(2)}) collective-permute-start(bf16[256,1152]{1,0:T(8,128)(2,1)S(1)} %add_convert_fusion.1), channel_id=1, source_target_pairs={{0,2},{2,0},{1,3},{3,1},{4,6},{6,4},{5,7},{7,5},{8,10},{10,8},{9,1... | collective-permute-start | bytes 1769480 | tf_op jit(solution)/shard_map/ppermute | solution.py:397
  295.1 8.8 %collective-permute-start.32 = (bf16[512,256]{1,0:T(8,128)(2,1)S(1)}, bf16[512,256]{1,0:T(8,128)(2,1)S(1)}, u32[]{:S(2)}, u32[]{:S(2)}) collective-permute-start(bf16[512,256]{1,0:T(8,128)(2,1)S(1)} %slice.343), channel_id=1, source_target_pairs={{0,4},{4,0},{1,5},{5,1},{2,6},{6,2},{3,7},{7,3},{8,12},{12,8},{9,1... | collective-permute-start | bytes 786440 | tf_op jit(solution)/shard_map/ppermute | solution.py:735
  300.8 8.6 %collective-permute-start.33 = (bf16[512,256]{1,0:T(8,128)(2,1)S(1)}, bf16[512,256]{1,0:T(8,128)(2,1)S(1)}, u32[]{:S(2)}, u32[]{:S(2)}) collective-permute-start(bf16[512,256]{1,0:T(8,128)(2,1)S(1)} %get-tuple-element.191), channel_id=1, source_target_pairs={{0,4},{4,0},{1,5},{5,1},{2,6},{6,2},{3,7},{7,3},{8,12},{12,8},{9,1... | collective-permute-start | bytes 786440 | tf_op jit(solution)/shard_map/ppermute | solution.py:736
  315.2 9.4 %collective-permute-start.34 = (bf16[2,512,288]{1,2,0:T(8,128)(2,1)}, bf16[2,512,288]{1,2,0:T(8,128)(2,1)}, u32[]{:S(2)}, u32[]{:S(2)}) collective-permute-start(bf16[2,512,288]{1,2,0:T(8,128)(2,1)} %pad_maximum_fusion.13), channel_id=1, source_target_pairs={{0,1},{1,0},{2,3},{3,2},{4,5},{5,4},{6,7},{7,6},{8,9},{9,8},{10,11... | collective-permute-start | bytes 1769480 | tf_op jit(solution)/shard_map/ppermute | solution.py:753
  316.7 9.8 %collective-permute-start.42 = (bf16[2,128,1152]{2,1,0:T(8,128)(2,1)}, bf16[2,128,1152]{2,1,0:T(8,128)(2,1)S(1)}, u32[]{:S(2)}, u32[]{:S(2)}) collective-permute-start(bf16[2,128,1152]{2,1,0:T(8,128)(2,1)} %pad_maximum_fusion.15), channel_id=1, source_target_pairs={{0,1},{1,0},{2,3},{3,2},{4,5},{5,4},{6,7},{7,6},{8,9},{9,8},{10,11... | collective-permute-start | bytes 1769480 | tf_op jit(solution)/shard_map/ppermute | solution.py:774
  322.6 294.0 %collective-permute-start.39 = (bf16[512,288]{1,0:T(8,128)(2,1)}, bf16[512,288]{1,0:T(8,128)(2,1)}, u32[]{:S(2)}, u32[]{:S(2)}) collective-permute-start(bf16[512,288]{1,0:T(8,128)(2,1)} %fusion.132), channel_id=1, source_target_pairs={{0,2},{2,0},{1,3},{3,1},{4,6},{6,4},{5,7},{7,5},{8,10},{10,8},{9,1... | collective-permute-start | bytes 884744 | tf_op jit(solution)/shard_map/ppermute | solution.py:756
  327.4 13.8 %collective-permute-start.43 = (bf16[128,1152]{1,0:T(8,128)(2,1)}, bf16[128,1152]{1,0:T(8,128)(2,1)}, u32[]{:S(2)}, u32[]{:S(2)}) collective-permute-start(bf16[128,1152]{1,0:T(8,128)(2,1)} %fusion.196), channel_id=1, source_target_pairs={{0,2},{2,0},{1,3},{3,1},{4,6},{6,4},{5,7},{7,5},{8,10},{10,8},{9,1... | collective-permute-start | bytes 884744 | tf_op jit(solution)/shard_map/ppermute | solution.py:776
  331.1 285.5 %collective-permute-start.35 = (bf16[512,288]{1,0:T(8,128)(2,1)}, bf16[512,288]{1,0:T(8,128)(2,1)S(1)}, u32[]{:S(2)}, u32[]{:S(2)}) collective-permute-start(bf16[512,288]{1,0:T(8,128)(2,1)} %fusion.134), channel_id=1, source_target_pairs={{0,2},{2,0},{1,3},{3,1},{4,6},{6,4},{5,7},{7,5},{8,10},{10,8},{9,1... | collective-permute-start | bytes 884744 | tf_op jit(solution)/shard_map/ppermute | solution.py:756
  621.1 16.9 %collective-permute-start.44 = (bf16[128,1152]{1,0:T(8,128)(2,1)}, bf16[128,1152]{1,0:T(8,128)(2,1)S(1)}, u32[]{:S(2)}, u32[]{:S(2)}) collective-permute-start(bf16[128,1152]{1,0:T(8,128)(2,1)} %get-tuple-element.133), channel_id=1, source_target_pairs={{0,2},{2,0},{1,3},{3,1},{4,6},{6,4},{5,7},{7,5},{8,10},{10,8},{9,1... | collective-permute-start | bytes 884744 | tf_op jit(solution)/shard_map/ppermute | solution.py:786
  623.7 8.2 %collective-permute-start.41 = (f32[512]{0:T(512)S(1)}, f32[512]{0:T(512)S(1)}, u32[]{:S(2)}, u32[]{:S(2)}) collective-permute-start(f32[512]{0:T(512)S(1)} %add.509), channel_id=1, source_target_pairs={{0,2},{2,0},{1,3},{3,1},{4,6},{6,4},{5,7},{7,5},{8,10},{10,8},{9,1... | collective-permute-start | bytes 6152 | tf_op jit(solution)/shard_map/ppermute | solution.py:761
  638.1 9.6 %collective-permute-start.45 = (bf16[2,128,1152]{2,1,0:T(8,128)(2,1)S(1)}, bf16[2,128,1152]{2,1,0:T(8,128)(2,1)S(1)}, u32[]{:S(2)}, u32[]{:S(2)}) collective-permute-start(bf16[2,128,1152]{2,1,0:T(8,128)(2,1)S(1)} %pad_maximum_fusion.16), channel_id=1, source_target_pairs={{0,1},{1,0},{2,3},{3,2},{4,5},{5,4},{6,7},{7,6},{8,9},{9,8},{10,11... | collective-permute-start | bytes 1769480 | tf_op jit(solution)/shard_map/ppermute | solution.py:787
  (212 other events, 1282.1 us)

commit v3 on v2

--- a/solution.py
+++ b/solution.py
@@ -1,3 +1,4 @@
+import math
 from functools import partial
 
 import jax
@@ -369,6 +370,7 @@
 XOR1 = ((0, 1), (1, 0), (2, 3), (3, 2))
 XOR2 = ((0, 2), (2, 0), (1, 3), (3, 1))
 MESH = pl.DeviceIdType.MESH
+GELU_SCALE = math.sqrt(2.0 / math.pi)
 F32 = jnp.float32
 BF16 = jnp.bfloat16
 
@@ -571,6 +573,365 @@
     return values * cosine_table + turned
 
 
+def row_blocks(rows, size, body, carry=None):
+    def step(i, state):
+        return body(pl.ds(pl.multiple_of(i * size, size), size), state)
+
+    return lax.fori_loop(0, rows // size, step, carry)
+
+
+def turn_in(source, target, rows):
+    for first in range(0, source.shape[0], 128):
+        target[rows, first : first + 128] = source[first : first + 128, :].T
+
+
+def column_tiles(total, size):
+    return [(first, min(size, total - first)) for first in range(0, total, size)]
+
+
+def dot_nn(left, right):
+    return jnp.dot(left, right, preferred_element_type=F32)
+
+
+def dot_nt(left, right):
+    return contract(left, right, 1, 1)
+
+
+def gelu_parts(gate):
+    square = gate * gate
+    tanh = jnp.tanh(GELU_SCALE * gate * (1.0 + 0.044715 * square))
+    half = 0.5 + 0.5 * tanh
+    slope = GELU_SCALE * (1.0 + 3.0 * 0.044715 * square)
+    return gate * half, half + 0.5 * gate * (1.0 - tanh * tanh) * slope
+
+
+def forward_kernel(
+    real_length, tok, cot, w_q, w_k, w_v, w_o, w_g, w_u, w_d, gains, head_gains, cosines, sines,
+    out_t, x16, cot16, n16, raw, q16, kv16, far_kv, att16, attn16, mid16, hid16, dffn16, dg16, du16,
+    gain_sum,
+    blocks, v_qkv, v_o, v_g, v_u, v_d, part, near, far, ffn16,
+    load_sem, own_sem, g_send, g_recv, kv_send, kv_recv, s_send, s_recv,
+):
+    dp, ctx, tp = lax.axis_index("dp"), lax.axis_index("ctx"), lax.axis_index("tp")
+    core_peer = (dp, ctx, tp + 1 - 2 * (tp % 2))
+    x_index = (tp + 2) % 4
+    x_peer = (dp, ctx, x_index)
+    y_peer = (dp, 1 - ctx, tp)
+    features, rows = tok.shape[0], tok.shape[1] // 2
+    width = 4 * features
+    hidden = w_d.shape[0]
+    head_dim = w_k.shape[1]
+    half = rows // 2
+    odd = tp % 2
+
+    loads = [
+        pltpu.make_async_copy(source, target, load_sem.at[j])
+        for j, (source, target) in enumerate(
+            (
+                (w_q, v_qkv.at[:, 0:head_dim]),
+                (w_k, v_qkv.at[:, head_dim : 2 * head_dim]),
+                (w_v, v_qkv.at[:, 2 * head_dim : 3 * head_dim]),
+                (w_o, v_o), (w_g, v_g), (w_u, v_u), (w_d, v_d),
+            )
+        )
+    ]
+    for copy in loads:
+        copy.start()
+
+    def half_of(source, index):
+        lane = (ctx if index % 2 == 0 else 1 - ctx) * rows
+        return source.at[:, pl.ds(pl.multiple_of(lane, rows), rows)]
+
+    def place(index, owner):
+        return blocks.at[index, pl.ds(pl.multiple_of(owner * features, features), features)]
+
+    sources = [half_of(tok, 0), half_of(tok, 1), half_of(cot, 0), half_of(cot, 1)]
+
+    def remote(source, target, send, recv, peer):
+        return pltpu.make_async_remote_copy(
+            src_ref=source, dst_ref=target, send_sem=send, recv_sem=recv,
+            device_id=peer, device_id_type=MESH,
+        )
+
+    own = [pltpu.make_async_copy(sources[j], place(j, tp), own_sem.at[j]) for j in range(4)]
+    to_x = [
+        remote(sources[j], place(j, tp), g_send.at[0, j], g_recv.at[0, j], x_peer) for j in range(4)
+    ]
+    to_core = [
+        remote(sources[j], place(j, tp), g_send.at[1, j], g_recv.at[1, j], core_peer)
+        for j in range(4)
+    ]
+    onward = [
+        remote(place(j, x_index), place(j, x_index), g_send.at[2, j], g_recv.at[2, j], core_peer)
+        for j in range(4)
+    ]
+    for copy in own:
+        copy.start()
+    barrier = pltpu.get_barrier_semaphore()
+    for peer in (core_peer, x_peer, y_peer):
+        pl.semaphore_signal(barrier, inc=1, device_id=peer, device_id_type=MESH)
+    pl.semaphore_wait(barrier, 3)
+
+    for j in range(4):
+        to_core[j].start()
+    to_x[0].start()
+    to_x[1].start()
+
+    def pass_on(j):
+        to_x[j].wait_recv()
+        onward[j].start()
+
+    def gathered(j):
+        own[j].wait()
+        to_core[j].wait_recv()
+        onward[j].wait_recv()
+
+    def chunk(c):
+        return pl.ds(c * rows, rows)
+
+    def project(c):
+        turn_in(blocks.at[c], x16, chunk(c))
+
+        def norm(block, _):
+            at = pl.ds(c * rows + block.start, block.size)
+            values = x16[at, :].astype(F32)
+            n16[at, :] = (values * scale_of(values) * gains[0:1, :]).astype(BF16)
+
+        row_blocks(rows, 32, norm)
+        for first in range(0, rows, half):
+            at = pl.ds(c * rows + first, half)
+            tables = pl.ds(c * rows + first, half)
+            values = dot_nn(n16[at, :], v_qkv[...])
+            raw[at, :] = values[:, : 2 * head_dim]
+            cosine, sine = cosines[tables, :], sines[tables, :]
+            for j, target in ((0, q16.at[at, :]), (1, kv16.at[at, 0:head_dim])):
+                head = values[:, j * head_dim : (j + 1) * head_dim]
+                head = head * scale_of(head) * head_gains[j : j + 1, :]
+                low, high = head[:, : head_dim // 2], head[:, head_dim // 2 :]
+                target[:, : head_dim // 2] = (low * cosine - high * sine).astype(BF16)
+                target[:, head_dim // 2 :] = (high * cosine + low * sine).astype(BF16)
+            kv16[at, head_dim:] = values[:, 2 * head_dim :].astype(BF16)
+
+    score_scale = head_dim ** (-0.5)
+
+    def attend_rows(c):
+        for first in range(0, rows, half):
+            at = pl.ds(c * rows + first, half)
+            query = q16[at, :]
+            row_id = first + lax.broadcasted_iota(jnp.int32, (half, rows), 0)
+            key_id = lax.broadcasted_iota(jnp.int32, (half, rows), 1)
+            allowed = key_id <= row_id
+            if c == 1:
+                allowed = allowed & (rows + key_id < real_length[0, 0])
+            keys = [(kv16[chunk(c), :head_dim], kv16[chunk(c), head_dim:], allowed)]
+            if c == 1:
+                keys.append((far_kv[:, :head_dim], far_kv[:, head_dim:], None))
+            scores = []
+            for key, _, mask in keys:
+                score = dot_nt(query, key) * score_scale
+                scores.append(score if mask is None else jnp.where(mask, score, MASKED))
+            most = scores[0].max(axis=1, keepdims=True)
+            for score in scores[1:]:
+                most = jnp.maximum(most, score.max(axis=1, keepdims=True))
+            exps = [jnp.exp(score - most) for score in scores]
+            total = sum(e.sum(axis=1, keepdims=True) for e in exps)
+            out = sum(dot_nn((e / total).astype(BF16), k[1]) for e, k in zip(exps, keys))
+            att16[at, :] = out.astype(BF16)
+        part[c] = dot_nn(att16[chunk(c), :], v_o[...]).astype(BF16)
+
+    def rows_of(index):
+        return pl.ds(pl.multiple_of(index * half, half), half)
+
+    def sum_copies(s, target):
+        start = pl.multiple_of((s % 2) * rows + odd * half, half)
+        final = target.at[pl.ds(start, half)]
+        return (
+            remote(part.at[s, rows_of(1 - odd)], near.at[s], s_send.at[0, s], s_recv.at[0, s], core_peer),
+            remote(near.at[s], far.at[s], s_send.at[1, s], s_recv.at[1, s], x_peer),
+            remote(final, final, s_send.at[2, s], s_recv.at[2, s], core_peer),
+        )
+
+    def sum_start(s, target):
+        sum_copies(s, target)[0].start()
+
+    def sum_cross(s, target):
+        copies = sum_copies(s, target)
+        copies[0].wait_recv()
+        near[s] = add16(part[s, rows_of(odd)], near[s])
+        copies[1].start()
+
+    def sum_back(s, target):
+        copies = sum_copies(s, target)
+        copies[1].wait_recv()
+        start = pl.multiple_of((s % 2) * rows + odd * half, half)
+        target[pl.ds(start, half), :] = add16(near[s], far[s])
+        copies[2].start()
+        copies[2].wait_recv()
+
+    def residual(at):
+        branch = attn16[at, :].astype(F32)
+        return x16[at, :].astype(F32) + branch * scale_of(branch) * gains[1:2, :]
+
+    def middle(c):
+        def body(block, _):
+            at = pl.ds(c * rows + block.start, block.size)
+            values = residual(at)
+            mid16[at, :] = (values * scale_of(values) * gains[2:3, :]).astype(BF16)
+
+        row_blocks(rows, 32, body)
+
+    def feed(c):
+        for first, size in column_tiles(hidden, 256):
+            for low in range(0, rows, half):
+                at = pl.ds(c * rows + low, half)
+                cols = pl.ds(first, size)
+                gate = dot_nt(mid16[at, :], v_g[cols, :])
+                up = dot_nt(mid16[at, :], v_u[cols, :])
+                act, slope = gelu_parts(gate)
+                hid16[at, cols] = (act * up).astype(BF16)
+                dg16[at, cols] = (slope * up).astype(BF16)
+                du16[at, cols] = act.astype(BF16)
+        for first, size in column_tiles(width, 256):
+            cols = pl.ds(first, size)
+            part[2 + c, :, cols] = dot_nn(hid16[chunk(c), :], v_d[:, cols]).astype(BF16)
+
+    def finish(c):
+        turn_in(blocks.at[2 + c], cot16, chunk(c))
+        sum_copies(c, attn16)[0].wait_send()
+        onward[c].wait_send()
+
+        def body(block, total):
+            at = pl.ds(c * rows + block.start, block.size)
+            branch = ffn16[at, :].astype(F32)
+            scale = scale_of(branch)
+            unit = branch * scale
+            grad = cot16[at, :].astype(F32)
+            part[c, block, :] = (residual(at) + unit * gains[3:4, :]).astype(BF16)
+            weighted = grad * gains[3:4, :]
+            inner = jnp.mean(unit * weighted, axis=-1, keepdims=True)
+            dffn16[at, :] = (scale * (weighted - unit * inner)).astype(BF16)
+            return total + (grad * unit).reshape(-1, 8, width).sum(axis=0)
+
+        total = row_blocks(rows, 32, body, jnp.zeros((8, width), F32))
+        if c == 0:
+            gain_sum[...] = total
+        else:
+            gain_sum[...] += total
+        for first in range(0, width, 128):
+            blocks[c, first : first + 128, :] = part[c, :, first : first + 128].T
+        lane = (ctx if c == 0 else 1 - ctx) * rows
+        mine = blocks[c, pl.ds(pl.multiple_of(tp * features, features), features), :]
+        out_t[:, pl.ds(pl.multiple_of(lane, rows), rows)] = mine
+
+    def feed_back(c):
+        for first, size in column_tiles(hidden, 256):
+            for low in range(0, rows, half):
+                at = pl.ds(c * rows + low, half)
+                cols = pl.ds(first, size)
+                d_hidden = dot_nt(dffn16[at, :], v_d[cols, :])
+                dg16[at, cols] = (d_hidden * dg16[at, cols].astype(F32)).astype(BF16)
+                du16[at, cols] = (d_hidden * du16[at, cols].astype(F32)).astype(BF16)
+
+    kv_copy = remote(kv16.at[chunk(0)], far_kv, kv_send.at[0], kv_recv.at[0], y_peer)
+    pass_on(0)
+    for copy in loads[:3]:
+        copy.wait()
+    gathered(0)
+    project(0)
+    kv_copy.start()
+    pass_on(1)
+    to_x[2].start()
+    to_x[3].start()
+    loads[3].wait()
+    attend_rows(0)
+    sum_start(0, attn16)
+    gathered(1)
+    project(1)
+    sum_cross(0, attn16)
+    kv_copy.wait_recv()
+    attend_rows(1)
+    sum_start(1, attn16)
+    pass_on(2)
+    pass_on(3)
+    sum_cross(1, attn16)
+    sum_back(0, attn16)
+    for copy in loads[4:]:
+        copy.wait()
+    middle(0)
+    feed(0)
+    sum_start(2, ffn16)
+    sum_back(1, attn16)
+    middle(1)
+    sum_cross(2, ffn16)
+    feed(1)
+    sum_start(3, ffn16)
+    gathered(2)
+    gathered(3)
+    sum_back(2, ffn16)
+    sum_cross(3, ffn16)
+    finish(0)
+    feed_back(0)
+    sum_back(3, ffn16)
+    finish(1)
+    feed_back(1)
+    for group in (to_x, to_core, onward[2:], [kv_copy]):
+        for copy in group:
+            copy.wait_send()
+    for s, target in ((0, attn16), (1, attn16), (2, ffn16), (3, ffn16)):
+        for copy in sum_copies(s, target)[1 if s < 2 else 0 :]:
+            copy.wait_send()
+
+
+def forward(real_length, tok_t, cot_t, weights, gains, head_gains, cosines, sines):
+    features, rows = tok_t.shape
+    half = rows // 2
+    width = 4 * features
+    hidden = weights[-1].shape[0]
+    head_dim = weights[1].shape[1]
+    whole = pl.BlockSpec(memory_space=pltpu.VMEM)
+    there = pl.BlockSpec(memory_space=pl.ANY)
+
+    def low(*shape):
+        return jax.ShapeDtypeStruct(shape, BF16)
+
+    return pl.pallas_call(
+        forward_kernel,
+        out_shape=(
+            low(features, rows), low(rows, width), low(rows, width), low(rows, width),
+            jax.ShapeDtypeStruct((rows, 2 * head_dim), F32), low(rows, head_dim),
+            low(rows, 2 * head_dim), low(half, 2 * head_dim), low(rows, head_dim),
+            low(rows, width), low(rows, width), low(rows, hidden), low(rows, width),
+            low(rows, hidden), low(rows, hidden), jax.ShapeDtypeStruct((8, width), F32),
+        ),
+        in_specs=[pl.BlockSpec(memory_space=pltpu.SMEM)] + [there] * 9 + [whole] * 4,
+        out_specs=[whole] * 16,
+        scratch_shapes=[
+            pltpu.VMEM((4, width, half), BF16),
+            pltpu.VMEM((width, 3 * head_dim), BF16),
+            pltpu.VMEM((head_dim, width), BF16),
+            pltpu.VMEM((hidden, width), BF16),
+            pltpu.VMEM((hidden, width), BF16),
+            pltpu.VMEM((hidden, width), BF16),
+            pltpu.VMEM((4, half, width), BF16),
+            pltpu.VMEM((4, half // 2, width), BF16),
+            pltpu.VMEM((4, half // 2, width), BF16),
+            pltpu.VMEM((rows, width), BF16),
+            pltpu.SemaphoreType.DMA((7,)),
+            pltpu.SemaphoreType.DMA((4,)),
+            pltpu.SemaphoreType.DMA((3, 4)),
+            pltpu.SemaphoreType.DMA((3, 4)),
+            pltpu.SemaphoreType.DMA((1,)),
+            pltpu.SemaphoreType.DMA((1,)),
+            pltpu.SemaphoreType.DMA((3, 4)),
+            pltpu.SemaphoreType.DMA((3, 4)),
+        ],
+        name="forward",
+        compiler_params=pltpu.CompilerParams(
+            collective_id=2, has_side_effects=True, vmem_limit_bytes=63 << 20
+        ),
+    )(real_length, tok_t, cot_t, *weights, gains, head_gains, cosines, sines)
+
+
 def positions(block, rows, bucket_row, true_row):
     stream_pos = block * rows + jnp.arange(rows, dtype=jnp.int32)
     starts = jnp.cumsum(bucket_row) - bucket_row
@@ -641,72 +1002,51 @@
         for gain in (gain_in, gain_post_attn, gain_pre_ffn, gain_post_ffn, gain_query, gain_key)
     ]
     both = range(2)
+    width = 4 * feature_cols
+    seq_pos = jnp.arange(2 * rows, dtype=jnp.int32)
+    cosines, sines = [table[:, : head_dim // 2] for table in rope_tables(seq_pos, head_dim)]
+    real_length = lax.dynamic_slice_in_dim(true_lengths, 1 - ctx_index, 1, 1)
+    gains = jnp.stack([g_in, g_pa, g_pf, g_pff])
+    head_gains = jnp.stack([g_q, g_k])
+    weights = (w_query, w_key, w_value, w_out, w_gate.T, w_up.T, w_down)
+    (
+        out_t, x16, cot16, n16, raw, q16, kv16, far_kv, att16, attn16, mid16, hid16, dffn16, dg16,
+        du16, gain_sum,
+    ) = forward(
+        real_length, tokens.T, out_grad.T, weights, gains, head_gains, cosines, sines
+    )
+
+    def two(values):
+        return [values[:rows], values[rows:]]
+
+    inputs16, cots16, normed16 = two(x16), two(cot16), two(n16)
+    inputs = [values.astype(F32) for values in inputs16]
+    cots = [values.astype(F32) for values in cots16]
+    query_raw, key_raw = two(raw[:, :head_dim]), two(raw[:, head_dim:])
+    query16, key16, value16 = two(q16), two(kv16[:, :head_dim]), two(kv16[:, head_dim:])
+    keys = [key16[0], jnp.concatenate([far_kv[:, :head_dim], key16[1]], axis=0)]
+    values_ = [value16[0], jnp.concatenate([far_kv[:, head_dim:], value16[1]], axis=0)]
+    ids = jnp.arange(rows, dtype=jnp.int32)
+    causal = ids[None, :] <= ids[:, None]
+    real = causal & (rows + ids[None, :] < real_length[0, 0])
+    allowed = [causal, jnp.concatenate([jnp.ones_like(real), real], axis=1)]
+    probs = [
+        attend(query16[i], keys[i], values_[i], allowed[i], score_scale)[0] for i in both
+    ]
+    attended16 = two(att16)
+    attention = [values.astype(F32) for values in two(attn16)]
+    residual = [inputs[i] + rms_norm(attention[i], g_pa) for i in both]
+    d_gate16, d_up16 = two(dg16), two(du16)
+    tables = [
+        [jnp.concatenate([t, t], axis=1) for t in (cosines[at], sines[at])]
+        for at in (slice(0, rows), slice(rows, 2 * rows))
+    ]
+    gain_sums = [jnp.sum(gain_sum, axis=0), 0.0]
     token_parts = halves(tokens, ctx_index)
-    cot_parts = halves(out_grad, ctx_index)
-    w_qkv = jnp.concatenate([w_query, w_key, w_value], axis=1)
-
-    blocks = (2 * ctx_index, 3 - 2 * ctx_index, 2 - 2 * ctx_index)
-    layouts = [positions(b, rows, bucket_lengths[0], true_lengths[0]) for b in blocks]
-    tables = [rope_tables(layouts[i][2], head_dim) for i in both]
-    key_layout = [jnp.concatenate([a, b]) for a, b in zip(layouts[2], layouts[1])]
-    allowed = [allowed_pairs(layouts[0], layouts[0]), allowed_pairs(layouts[1], key_layout)]
-
-    inputs16 = [tp_gather(part) for part in token_parts]
-    cots16 = [tp_gather(part) for part in cot_parts]
-    inputs = [values.astype(F32) for values in inputs16]
-    normed16 = [rms_norm(values, g_in).astype(BF16) for values in inputs]
-    raw = [jnp.dot(values, w_qkv, preferred_element_type=F32) for values in normed16]
-    query_raw = [values[:, :head_dim] for values in raw]
-    key_raw = [values[:, head_dim : 2 * head_dim] for values in raw]
-    value16 = [values[:, 2 * head_dim :].astype(BF16) for values in raw]
-    query16 = [rotate(rms_norm(query_raw[i], g_q), *tables[i]).astype(BF16) for i in both]
-    key16 = [rotate(rms_norm(key_raw[i], g_k), *tables[i]).astype(BF16) for i in both]
-    far_key, far_value = [
-        lax.ppermute(values, "ctx", MESH_PAIR) for values in (key16[0], value16[0])
-    ]
-    keys = [key16[0], jnp.concatenate([far_key, key16[1]], axis=0)]
-    values_ = [value16[0], jnp.concatenate([far_value, value16[1]], axis=0)]
-
-    probs, attended16, attention, residual, mid16 = [], [], [], [], []
-    hidden16, gate, up, ffn = [], [], [], []
-    for i in both:
-        p, a = attend(query16[i], keys[i], values_[i], allowed[i], score_scale)
-        probs.append(p)
-        attended16.append(a)
-    for i in both:
-        part = jnp.dot(attended16[i], w_out, preferred_element_type=F32).astype(BF16)
-        attention.append(tp_sum(part).astype(F32))
-        residual.append(inputs[i] + rms_norm(attention[i], g_pa))
-        mid16.append(rms_norm(residual[i], g_pf).astype(BF16))
-        gate.append(jnp.dot(mid16[i], w_gate, preferred_element_type=F32).astype(BF16))
-        up.append(jnp.dot(mid16[i], w_up, preferred_element_type=F32).astype(BF16))
-        hidden16.append(geglu(gate[i].astype(F32), up[i].astype(F32)).astype(BF16))
-        part = jnp.dot(hidden16[i], w_down, preferred_element_type=F32).astype(BF16)
-        ffn.append(tp_sum(part).astype(F32))
-
-    out_parts, d_ffn16, d_gate16, d_up16 = [], [], [], []
-    gain_sums = []
-    cots = [values.astype(F32) for values in cots16]
-    for i in both:
-        outputs = residual[i] + rms_norm(ffn[i], g_pff)
-        out_parts.append(
-            lax.dynamic_slice_in_dim(outputs, tp_index * feature_cols, feature_cols, 1).astype(BF16)
-        )
-        d_ffn, d_pff = rms_back(ffn[i], g_pff, cots[i])
-        d_ffn16.append(d_ffn.astype(BF16))
-        d_hidden = contract(d_ffn16[i], w_down, 1, 1)
-        gate32, up32 = gate[i].astype(F32), up[i].astype(F32)
-        _, pull = jax.vjp(geglu, gate32, up32)
-        d_gate, d_up = pull(d_hidden)
-        d_gate16.append(d_gate.astype(BF16))
-        d_up16.append(d_up.astype(BF16))
-        gain_sums.append(d_pff)
-    hidden_all, mid_all, d_ffn_all, d_gate_all, d_up_all = [
-        jnp.concatenate(pair, axis=0) for pair in (hidden16, mid16, d_ffn16, d_gate16, d_up16)
-    ]
-    grad_down = contract(hidden_all, d_ffn_all, 0, 0).astype(BF16)
-    grad_gate = contract(d_gate_all, mid_all, 0, 0).astype(BF16)
-    grad_up = contract(d_up_all, mid_all, 0, 0).astype(BF16)
+
+    grad_down = contract(hid16, dffn16, 0, 0).astype(BF16)
+    grad_gate = contract(dg16, mid16, 0, 0).astype(BF16)
+    grad_up = contract(du16, mid16, 0, 0).astype(BF16)
 
     d_resid, d_attn16, d_attended16 = [], [], []
     pf_sums, pa_sums = [], []
@@ -721,7 +1061,7 @@
         pf_sums.append(d_pf)
         pa_sums.append(d_pa)
     grad_out = contract(
-        jnp.concatenate(attended16, axis=0), jnp.concatenate(d_attn16, axis=0), 0, 0
+        att16, jnp.concatenate(d_attn16, axis=0), 0, 0
     ).astype(BF16)
 
     d_query, d_key, d_value = [], [], []
@@ -737,6 +1077,7 @@
     d_key = [d_key[0] + far_dk.astype(F32), d_key[1][rows:]]
     d_value = [d_value[0] + far_dv.astype(F32), d_value[1][rows:]]
 
+    w_qkv = jnp.concatenate([w_query, w_key, w_value], axis=1)
     w_blocks = w_qkv.reshape(4, feature_cols, w_qkv.shape[1])
     w_near = [
         lax.dynamic_index_in_dim(w_blocks, tp_index ^ j, keepdims=False) for j in range(4)
@@ -766,7 +1107,7 @@
         x_parts.append((resid_own + d_in).astype(BF16))
         in_sums.append(jnp.sum(u * own_in * scale, axis=0))
     grad_qkv = contract(
-        jnp.concatenate(d_qkv16, axis=0), jnp.concatenate(normed16, axis=0), 0, 0
+        jnp.concatenate(d_qkv16, axis=0), n16, 0, 0
     ).astype(BF16)
     grad_query = grad_qkv[:head_dim]
     kv_blocks = grad_qkv[head_dim:].reshape(4, head_dim // 2, -1)
@@ -790,7 +1131,6 @@
         [lax.select_n(tp_index ^ j, *kv_all) for j in range(4)], axis=0
     ).astype(F32).T
 
-    width = 4 * feature_cols
     in_full = lax.dynamic_update_slice_in_dim(
         jnp.zeros((width,), F32), in_sums[0] + in_sums[1], tp_index * feature_cols, 0
     )
@@ -804,7 +1144,7 @@
     gain_q_sum = small[4 * width : 4 * width + head_dim]
     gain_k_sum = small[4 * width + head_dim :]
     return (
-        join(*out_parts, ctx_index),
+        out_t.T,
         join(*x_parts, ctx_index),
         query_sum.astype(F32).T,
         kv_sum[:, :head_dim],

time: 661 us -> 600 us (0.908)
  Pallas kernels: 257 us -> 372 us
  waiting for transfers between devices: 108 us -> 35.8 us
  matrix products: 92.9 us -> 59.6 us
  other arithmetic: 90.2 us -> 64.1 us
  local copies, waits for them, and re-layouts: 64.4 us -> 43.3 us
  starting transfers between devices: 36.4 us -> 15.5 us
    pallas_call x0 -> x1, Pallas kernels: none -> 116 us  [forward(): pl.pallas_call(forward_kernel, out_shape=(low(features, rows), low(rows,...]
    ppermute x6 -> x2, waiting for transfers between devices: 58.6 us -> 17.3 us  [tp_sum(): own = add16(own, lax.ppermute(own, 'tp', XOR2))]
    ppermute x14 -> x0, waiting for transfers between devices: 26.6 us -> none  [the longest x4 26.5 us: tp_gather(): far = lax.ppermute(part, 'tp', XOR2)]
    dot_general x12 -> x0, matrix products: 25 us -> none  [the longest x2 9.43 us: paired_shards(): up.append(jnp.dot(mid16[i], w_up, preferred_element_type=F32).astype(BF16))]
    concatenate x5 -> x0, local copies, waits for them, and re-layouts: 15.4 us -> none  [the longest x4 13.4 us: tp_gather(): jnp.concatenate([lax.select_n(tp_index ^ j, *blocks) for j in range(4)],...]
    select_n x4 -> x0, other arithmetic: 10.4 us -> none  [tp_gather(): lax.select_n(tp_index ^ j, *blocks)]
    convert_element_type x9 -> x0, other arithmetic: 8.92 us -> none  [the longest x2 5.12 us: paired_shards(): rotate(rms_norm(key_raw[i], g_k), *tables[i]).astype(BF16)]
    ppermute x14 -> x0, starting transfers between devices: 8.54 us -> none  [the longest x4 5.3 us: tp_gather(): far = lax.ppermute(part, 'tp', XOR2)]
  transfers between devices with their start and end apart: 51 -> 25, of which waited for: 19 -> 10; matrix products, arithmetic and copies ran while one was open for 26% -> 19% of each run, Pallas kernels for 39% -> 43%
where the time goes in v3:
time: 600 us; the launch traced here: 593 us
  Pallas kernels  372 us (62%)
  other arithmetic  64.1 us (11%)
  matrix products  59.6 us (10%)
  local copies, waits for them, and re-layouts  43.3 us (7%)
  waiting for transfers between devices  35.8 us (6%)
  starting transfers between devices  15.5 us (3%)
    pallas_call x1, Pallas kernels, grid_sum(): pl.pallas_call(partial(grid_sum_kernel, step_rows, steps, lag), out_shape...  257 us
    pallas_call x1, Pallas kernels, forward(): pl.pallas_call(forward_kernel, out_shape=(low(features, rows), low(rows,...  116 us
    dot_general x27, matrix products, contract(): lax.dot_general(left, right, (((left_dim,), (right_dim,)), ((), ())), pre...  58.8 us
    unnamed x173, local copies, waits for them, and re-layouts  27.9 us
    ppermute x2, waiting for transfers between devices, tp_sum(): own = add16(own, lax.ppermute(own, 'tp', XOR2))  17.3 us
  transfers between devices with their start and end apart: 25, of which 10 were waited for; matrix products, arithmetic and copies ran while one was open for 19% of the time, Pallas kernels for 43%

profile of v3, /device:TPU:0, one launch (start us, length us, event | category | flops | bytes accessed | tf_op | source)
XLA Modules:
  0.0 593.0 jit_solution(1290390792644531285)
XLA Ops:
  5.0 3.7 fusion.67
  13.1 115.8 %forward.1 = (bf16[288,1024]{1,0:T(8,128)(2,1)}, bf16[1024,1152]{1,0:T(8,128)(2,1)}, bf16[1024,1152]{1,0:T(8,128)(2,1)}, bf16[1024,1152]{1,0:T(8,128)(2,1)}, f32...) custom-call(s32[1,1]{1,0:T(1,128)} %constant_dynamic-slice_fusion.6., ...), custom_call_target="tpu_custom_call" | custom-call | tf_op jit(solution)/shard_map/forward/pallas_call | solution.py:897
  128.9 5.2 fusion.42
  134.2 5.4 fusion.4
  141.5 2.5 fusion.45
  144.7 2.5 fusion.3
  152.9 7.6 %fusion.2 = bf16[5952,1152]{1,0:T(8,128)(2,1)} fusion(bf16[1024,1728]{1,0:T(8,128)(2,1)S(1)} %copy-done.74, bf16[1024,1152]{1,0:T(8,128)(2,1)S(1)} %copy-done.77), kind=kOutput, calls=%fused_computation.7 | convolution fusion | flops 4078854144 | bytes 9879552 | tf_op jit(solution)/shard_map/dot_general | solution.py:20
  160.5 7.4 %fusion.1 = bf16[5952,1152]{1,0:T(8,128)(2,1)} fusion(bf16[5952,1152]{1,0:T(8,128)(2,1)} %fusion.2, bf16[1024,1728]{1,0:T(8,128)(2,1)S(1)} %copy-done.73, bf16[1024,1152]{1,0:T(8,128)(2,1)S(1)} %copy-done.76), kind=kOutput, calls=%fused_computation.5 | convolution fusion | flops 4078854144 | bytes 9879552 | tf_op jit(solution)/shard_map/dot_general | solution.py:20
  168.0 7.5 %fusion = bf16[5952,1152]{1,0:T(8,128)(2,1)} fusion(bf16[5952,1152]{1,0:T(8,128)(2,1)} %fusion.1, bf16[1024,1728]{1,0:T(8,128)(2,1)S(1)} %copy-done.72, bf16[1024,1152]{1,0:T(8,128)(2,1)S(1)} %copy-done.76), kind=kOutput, calls=%fused_computation.3 | convolution fusion | flops 4078854144 | bytes 9879552 | tf_op jit(solution)/shard_map/dot_general | solution.py:20
  181.3 2.8 pad_maximum_fusion
  187.2 2.1 add_convert_fusion.3
  189.8 11.9 %collective-permute-done.4 = bf16[256,1152]{1,0:T(8,128)(2,1)S(1)} collective-permute-done((bf16[256,1152]{1,0:T(8,128)(2,1)S(1)}, bf16[256,1152]{1,0:T(8,128)(2,1)S(1)}, u32[]{:S(2)}, u32[]{:S(2)}) %collective-permute-start.4) | collective-permute-done | bytes 589856 | tf_op jit(solution)/shard_map/ppermute | solution.py:399
  203.6 1.9 copy.94
  208.0 5.4 collective-permute-done.1
  216.2 2.7 fusion.21
  220.9 5.4 fusion.28
  240.2 4.8 collective-permute-done.6
  252.9 2.3 convolution_convert_fusion.3
  262.0 2.6 fusion.89
  266.1 1.9 fusion.180
  272.2 2.6 fusion.87
  278.1 2.6 fusion.90
  280.7 2.4 collective-permute-done.17
  283.1 1.9 fusion.134
  285.8 256.6 %grid_sum.1 = bf16[5952,1152]{1,0:T(8,128)(2,1)} custom-call(bf16[5952,1152]{1,0:T(8,128)(2,1)} %broadcast_dynamic-update-slice_fusion.g), custom_call_target="tpu_custom_call" | custom-call | tf_op jit(solution)/shard_map/grid_sum/pallas_call | solution.py:543
  542.4 2.4 slice_convert_fusion.1
  544.8 11.8 %slice_convert_fusion = (f32[1728,1152]{1,0:T(8,128)}, f32[1152,1728]{0,1:T(8,128)}, f32[1152,1728]{0,1:T(8,128)}) fusion(bf16[5952,1152]{1,0:T(8,128)(2,1)} %grid_sum.1), kind=kLoop, calls=%fused_computation.18 | loop fusion | flops 5971968 | bytes 35831808 | tf_op jit(solution)/shard_map/convert_element_type | solution.py:1155
  558.5 2.5 fusion.86
  567.9 4.8 collective-permute-done.11
  573.9 2.5 broadcast_select_fusion.5
  576.9 3.6 collective-permute-done.23
  582.9 2.3 collective-permute-done.24
  (329 shorter events, 93.2 us)
Async XLA Ops:
  141.5 42.7 %collective-permute-start.3 = (bf16[256,1152]{1,0:T(8,128)(2,1)}, bf16[256,1152]{1,0:T(8,128)(2,1)}, u32[]{:S(2)}, u32[]{:S(2)}) collective-permute-start(bf16[256,1152]{1,0:T(8,128)(2,1)} %constant_dynamic-slice_fusion.4), channel_id=1, source_target_pairs={{0,1},{1,0},{2,3},{3,2},{4,5},{5,4},{6,7},{7,6},{8,9},{9,8},{10,11... | collective-permute-start | bytes 1769480 | tf_op jit(solution)/shard_map/ppermute | solution.py:398
  148.2 39.0 %collective-permute-start = (bf16[256,1152]{1,0:T(8,128)(2,1)}, bf16[256,1152]{1,0:T(8,128)(2,1)}, u32[]{:S(2)}, u32[]{:S(2)}) collective-permute-start(bf16[256,1152]{1,0:T(8,128)(2,1)} %constant_dynamic-slice_fusion.5), channel_id=1, source_target_pairs={{0,1},{1,0},{2,3},{3,2},{4,5},{5,4},{6,7},{7,6},{8,9},{9,8},{10,11... | collective-permute-start | bytes 1769480 | tf_op jit(solution)/shard_map/ppermute | solution.py:398
  185.4 17.2 %copy-start.19 = (bf16[1024,288]{0,1:T(8,128)(2,1)S(1)}, bf16[1024,288]{0,1:T(8,128)(2,1)}, u32[]{:S(2)}) copy-start(bf16[1024,288]{0,1:T(8,128)(2,1)} %param.17) | copy-start | bytes 1769476
  185.4 16.3 %collective-permute-start.4 = (bf16[256,1152]{1,0:T(8,128)(2,1)S(1)}, bf16[256,1152]{1,0:T(8,128)(2,1)S(1)}, u32[]{:S(2)}, u32[]{:S(2)}) collective-permute-start(bf16[256,1152]{1,0:T(8,128)(2,1)S(1)} %add_convert_fusion.1), channel_id=1, source_target_pairs={{0,2},{2,0},{1,3},{3,1},{4,6},{6,4},{5,7},{7,5},{8,10},{10,8},{9,1... | collective-permute-start | bytes 1769480 | tf_op jit(solution)/shard_map/ppermute | solution.py:399
  187.1 16.3 %copy-start.63 = (bf16[1152]{0:T(1024)(128)(2,1)S(1)}, bf16[1152]{0:T(1024)(128)(2,1)}, u32[]{:S(2)}) copy-start(bf16[1152]{0:T(1024)(128)(2,1)} %param.28) | copy-start | bytes 6916
  187.1 16.3 %copy-start.64 = (bf16[1152]{0:T(1024)(128)(2,1)S(1)}, bf16[1152]{0:T(1024)(128)(2,1)}, u32[]{:S(2)}) copy-start(bf16[1152]{0:T(1024)(128)(2,1)} %param.26) | copy-start | bytes 6916
  189.2 18.1 %copy-start.52 = (f32[8,1152]{1,0:T(8,128)S(1)}, f32[8,1152]{1,0:T(8,128)}, u32[]{:S(2)}) copy-start(f32[8,1152]{1,0:T(8,128)} %get-tuple-element.46) | copy-start | bytes 110596
  189.2 24.2 %collective-permute-start.1 = (bf16[256,1152]{1,0:T(8,128)(2,1)}, bf16[256,1152]{1,0:T(8,128)(2,1)}, u32[]{:S(2)}, u32[]{:S(2)}) collective-permute-start(bf16[256,1152]{1,0:T(8,128)(2,1)} %add_convert_fusion.3), channel_id=1, source_target_pairs={{0,2},{2,0},{1,3},{3,1},{4,6},{6,4},{5,7},{7,5},{8,10},{10,8},{9,1... | collective-permute-start | bytes 1769480 | tf_op jit(solution)/shard_map/ppermute | solution.py:399
  202.6 12.2 %collective-permute-start.5 = (bf16[256,1152]{1,0:T(8,128)(2,1)}, bf16[256,1152]{1,0:T(8,128)(2,1)}, u32[]{:S(2)}, u32[]{:S(2)}) collective-permute-start(bf16[256,1152]{1,0:T(8,128)(2,1)} %add_convert_fusion), channel_id=1, source_target_pairs={{0,1},{1,0},{2,3},{3,2},{4,5},{5,4},{6,7},{7,6},{8,9},{9,8},{10,11... | collective-permute-start | bytes 1769480 | tf_op jit(solution)/shard_map/ppermute | solution.py:400
  214.8 4.2 collective-permute-start.2
  218.9 20.4 %copy-start.58 = (f32[512]{0:T(512)}, f32[512]{0:T(512)S(1)}, u32[]{:S(2)}) copy-start(f32[512]{0:T(512)S(1)} %get-tuple-element.96) | copy-start | bytes 6148
  218.9 20.4 %copy-start.60 = (f32[512]{0:T(512)}, f32[512]{0:T(512)S(1)}, u32[]{:S(2)}) copy-start(f32[512]{0:T(512)S(1)} %get-tuple-element.97) | copy-start | bytes 6148
  230.6 28.0 %copy-start.48 = (bf16[512,256]{1,0:T(8,128)(2,1)}, bf16[512,256]{1,0:T(8,128)(2,1)S(1)}, u32[]{:S(2)}) copy-start(bf16[512,256]{1,0:T(8,128)(2,1)S(1)} %get-tuple-element.164) | copy-start | bytes 786436
  230.6 20.2 %collective-permute-start.7 = (bf16[512,256]{1,0:T(8,128)(2,1)S(1)}, bf16[512,256]{1,0:T(8,128)(2,1)S(1)}, u32[]{:S(2)}, u32[]{:S(2)}) collective-permute-start(bf16[512,256]{1,0:T(8,128)(2,1)S(1)} %get-tuple-element.165), channel_id=1, source_target_pairs={{0,4},{4,0},{1,5},{5,1},{2,6},{6,2},{3,7},{7,3},{8,12},{12,8},{9,1... | collective-permute-start | bytes 786440 | tf_op jit(solution)/shard_map/ppermute | solution.py:1076
  235.5 9.6 %collective-permute-start.6 = (bf16[512,256]{1,0:T(8,128)(2,1)S(1)}, bf16[512,256]{1,0:T(8,128)(2,1)S(1)}, u32[]{:S(2)}, u32[]{:S(2)}) collective-permute-start(bf16[512,256]{1,0:T(8,128)(2,1)S(1)} %slice.465), channel_id=1, source_target_pairs={{0,4},{4,0},{1,5},{5,1},{2,6},{6,2},{3,7},{7,3},{8,12},{12,8},{9,1... | collective-permute-start | bytes 786440 | tf_op jit(solution)/shard_map/ppermute | solution.py:1075
  255.3 4.8 collective-permute-start.8
  256.2 9.9 %collective-permute-start.12 = (bf16[2,512,288]{1,2,0:T(8,128)(2,1)}, bf16[2,512,288]{1,2,0:T(8,128)(2,1)}, u32[]{:S(2)}, u32[]{:S(2)}) collective-permute-start(bf16[2,512,288]{1,2,0:T(8,128)(2,1)} %pad_maximum_fusion.8), channel_id=1, source_target_pairs={{0,1},{1,0},{2,3},{3,2},{4,5},{5,4},{6,7},{7,6},{8,9},{9,8},{10,11... | collective-permute-start | bytes 1769480 | tf_op jit(solution)/shard_map/ppermute | solution.py:1094
  257.8 12.1 %collective-permute-start.16 = (bf16[2,128,1152]{2,1,0:T(8,128)(2,1)}, bf16[2,128,1152]{2,1,0:T(8,128)(2,1)}, u32[]{:S(2)}, u32[]{:S(2)}) collective-permute-start(bf16[2,128,1152]{2,1,0:T(8,128)(2,1)} %pad_maximum_fusion.9), channel_id=1, source_target_pairs={{0,1},{1,0},{2,3},{3,2},{4,5},{5,4},{6,7},{7,6},{8,9},{9,8},{10,11... | collective-permute-start | bytes 1769480 | tf_op jit(solution)/shard_map/ppermute | solution.py:1115
  264.6 293.8 %collective-permute-start.9 = (bf16[512,288]{1,0:T(8,128)(2,1)}, bf16[512,288]{1,0:T(8,128)(2,1)S(1)}, u32[]{:S(2)}, u32[]{:S(2)}) collective-permute-start(bf16[512,288]{1,0:T(8,128)(2,1)} %fusion.89), channel_id=1, source_target_pairs={{0,2},{2,0},{1,3},{3,1},{4,6},{6,4},{5,7},{7,5},{8,10},{10,8},{9,1... | collective-permute-start | bytes 884744 | tf_op jit(solution)/shard_map/ppermute | solution.py:1097
  271.6 11.5 %collective-permute-start.17 = (bf16[128,1152]{1,0:T(8,128)(2,1)}, bf16[128,1152]{1,0:T(8,128)(2,1)}, u32[]{:S(2)}, u32[]{:S(2)}) collective-permute-start(bf16[128,1152]{1,0:T(8,128)(2,1)} %fusion.133), channel_id=1, source_target_pairs={{0,2},{2,0},{1,3},{3,1},{4,6},{6,4},{5,7},{7,5},{8,10},{10,8},{9,1... | collective-permute-start | bytes 884744 | tf_op jit(solution)/shard_map/ppermute | solution.py:1117
  276.6 281.8 %collective-permute-start.13 = (bf16[512,288]{1,0:T(8,128)(2,1)}, bf16[512,288]{1,0:T(8,128)(2,1)}, u32[]{:S(2)}, u32[]{:S(2)}) collective-permute-start(bf16[512,288]{1,0:T(8,128)(2,1)} %fusion.87), channel_id=1, source_target_pairs={{0,2},{2,0},{1,3},{3,1},{4,6},{6,4},{5,7},{7,5},{8,10},{10,8},{9,1... | collective-permute-start | bytes 884744 | tf_op jit(solution)/shard_map/ppermute | solution.py:1097
  561.0 1.2 collective-permute-start.14
  561.0 4.7 collective-permute-start.10
  562.2 4.1 collective-permute-start.15
  562.7 3.6 collective-permute-start.20
  562.8 13.9 %collective-permute-start.18 = (bf16[128,1152]{1,0:T(8,128)(2,1)}, bf16[128,1152]{1,0:T(8,128)(2,1)S(1)}, u32[]{:S(2)}, u32[]{:S(2)}) collective-permute-start(bf16[128,1152]{1,0:T(8,128)(2,1)} %get-tuple-element.135), channel_id=1, source_target_pairs={{0,2},{2,0},{1,3},{3,1},{4,6},{6,4},{5,7},{7,5},{8,10},{10,8},{9,1... | collective-permute-start | bytes 884744 | tf_op jit(solution)/shard_map/ppermute | solution.py:1127
  565.8 6.9 %collective-permute-start.11 = (f32[512]{0:T(512)S(1)}, f32[512]{0:T(512)S(1)}, u32[]{:S(2)}, u32[]{:S(2)}) collective-permute-start(f32[512]{0:T(512)S(1)} %add.325), channel_id=1, source_target_pairs={{0,2},{2,0},{1,3},{3,1},{4,6},{6,4},{5,7},{7,5},{8,10},{10,8},{9,1... | collective-permute-start | bytes 6152 | tf_op jit(solution)/shard_map/ppermute | solution.py:1102
  566.3 6.6 %collective-permute-start.21 = (f32[40,128]{1,0:T(8,128)S(1)}, f32[40,128]{1,0:T(8,128)S(1)}, u32[]{:S(2)}, u32[]{:S(2)}) collective-permute-start(f32[40,128]{1,0:T(8,128)S(1)} %bitcast_add_fusion), channel_id=1, source_target_pairs={{0,2},{2,0},{1,3},{3,1},{4,6},{6,4},{5,7},{7,5},{8,10},{10,8},{9,1... | collective-permute-start | bytes 61448 | tf_op jit(solution)/shard_map/ppermute | solution.py:418
  572.9 3.8 collective-permute-start.22
  576.7 3.8 collective-permute-start.23
  576.8 9.6 %collective-permute-start.19 = (bf16[2,128,1152]{2,1,0:T(8,128)(2,1)S(1)}, bf16[2,128,1152]{2,1,0:T(8,128)(2,1)S(1)}, u32[]{:S(2)}, u32[]{:S(2)}) collective-permute-start(bf16[2,128,1152]{2,1,0:T(8,128)(2,1)S(1)} %pad_maximum_fusion.10), channel_id=1, source_target_pairs={{0,1},{1,0},{2,3},{3,2},{4,5},{5,4},{6,7},{7,6},{8,9},{9,8},{10,11... | collective-permute-start | bytes 1769480 | tf_op jit(solution)/shard_map/ppermute | solution.py:1128
  580.5 4.7 collective-permute-start.24
  (73 other events, 350.0 us)

commit v4 on v3

--- a/solution.py
+++ b/solution.py
@@ -366,7 +366,6 @@
     )
 
 
-MESH_PAIR = ((0, 1), (1, 0))
 XOR1 = ((0, 1), (1, 0), (2, 3), (3, 2))
 XOR2 = ((0, 2), (2, 0), (1, 3), (3, 1))
 MESH = pl.DeviceIdType.MESH
@@ -379,198 +378,8 @@
     return (left.astype(F32) + right.astype(F32)).astype(BF16)
 
 
-def halves(values, index):
-    size = values.shape[0] // 2
-    own = lax.dynamic_slice_in_dim(values, index * size, size)
-    other = lax.dynamic_slice_in_dim(values, (1 - index) * size, size)
-    return own, other
-
-
-def join(own, other, index):
-    first = jnp.where(index == 0, own, other)
-    second = jnp.where(index == 0, other, own)
-    return jnp.concatenate([first, second], axis=0)
-
-
-def tp_sum(values):
-    odd = lax.axis_index("tp") % 2
-    own, other = halves(values, odd)
-    own = add16(own, lax.ppermute(other, "tp", XOR1))
-    own = add16(own, lax.ppermute(own, "tp", XOR2))
-    return join(own, lax.ppermute(own, "tp", XOR1), odd)
-
-
-def tp_gather(part):
-    tp_index = lax.axis_index("tp")
-    near = lax.ppermute(part, "tp", XOR1)
-    far = lax.ppermute(part, "tp", XOR2)
-    both = lax.ppermute(far, "tp", XOR1)
-    blocks = (part, near, far, both)
-    return jnp.concatenate(
-        [lax.select_n(tp_index ^ j, *blocks) for j in range(4)], axis=1
-    )
-
-
-def sum_all(values):
-    for axis, pairs in (
-        ("tp", XOR1), ("tp", XOR2), ("ctx", MESH_PAIR), ("dp", XOR1), ("dp", XOR2)
-    ):
-        values = values + lax.ppermute(values, axis, pairs)
-    return values
-
-
-def grid_sum_kernel(s, K, L, g, out, Y2, Z2, M2, Z1, M1, Y1, *sems):
-    sy2, sz2, sm2, sfo, sfy, sz1, sm1, sy1, sfm, sfa, sfb = sems[:11]
-    ry2, rz2, rm2, rfo, rfy, rz1, rm1, ry1, rfm, rfa, rfb = sems[11:]
-    dp, ctx, tp = lax.axis_index("dp"), lax.axis_index("ctx"), lax.axis_index("tp")
-    upper = dp // 2
-    outer = (dp == 0) | (dp == 3)
-    inner = jnp.logical_not(outer)
-    zn = jnp.where(dp < 2, 1 - dp, 5 - dp)
-    zm = 3 - dp
-    ypeer, zpeer, mpeer = (dp, 1 - ctx, tp), (zn, ctx, tp), (zm, ctx, tp)
-    bar = pltpu.get_barrier_semaphore()
-    pl.semaphore_signal(bar, inc=1, device_id=ypeer, device_id_type=MESH)
-    pl.semaphore_signal(bar, inc=1, device_id=zpeer, device_id_type=MESH)
-    pl.when(inner)(lambda: pl.semaphore_signal(bar, inc=1, device_id=mpeer, device_id_type=MESH))
-    pl.semaphore_wait(bar, jnp.where(inner, 3, 2))
-    base1 = 2 * s * K
-    def rows2(k, h): return pl.ds(pl.multiple_of((2 * k + h) * s, s), s)
-    def rows1(k, h): return pl.ds(pl.multiple_of(base1 + (2 * k + h) * s, s), s)
-    def pair1(k): return pl.ds(pl.multiple_of(base1 + 2 * k * s, s), 2 * s)
-    def slot(k, n=1): return pl.ds(pl.multiple_of(k * n * s, s), n * s)
-    def half1(k, h): return pl.ds(pl.multiple_of((2 * k + h) * s, s), s)
-    def cp(src, dst, ss, rs, k, dev):
-        return pltpu.make_async_remote_copy(src_ref=src, dst_ref=dst, send_sem=ss.at[k], recv_sem=rs.at[k], device_id=dev, device_id_type=MESH)
-    def c_y2(k): return cp(g.at[rows2(k, 1 - ctx)], Y2.at[slot(k)], sy2, ry2, k, ypeer)
-    def c_z2(k): return cp(Y2.at[slot(k)], Z2.at[slot(k)], sz2, rz2, k, zpeer)
-    def c_m2(k): return cp(Z2.at[slot(k)], M2.at[slot(k)], sm2, rm2, k, mpeer)
-    def c_fo(k): return cp(out.at[rows2(k, ctx)], out.at[rows2(k, ctx)], sfo, rfo, k, zpeer)
-    def c_fy(k): return cp(out.at[rows2(k, ctx)], out.at[rows2(k, ctx)], sfy, rfy, k, ypeer)
-    def c_z1(k): return cp(g.at[pair1(k)], Z1.at[slot(k, 2)], sz1, rz1, k, zpeer)
-    def c_m1(k): return cp(Z1.at[half1(k, 1 - upper)], M1.at[slot(k)], sm1, rm1, k, mpeer)
-    def c_y1(k): return cp(M1.at[slot(k)], Y1.at[slot(k)], sy1, ry1, k, ypeer)
-    def c_fm(k): return cp(out.at[rows1(k, upper)], out.at[rows1(k, upper)], sfm, rfm, k, mpeer)
-    def c_fa(k): return cp(out.at[rows1(k, upper)], out.at[rows1(k, upper)], sfa, rfa, k, zpeer)
-    def c_fb(k): return cp(out.at[rows1(k, 1 - upper)], out.at[rows1(k, 1 - upper)], sfb, rfb, k, zpeer)
-    def add(a, b): return (a.astype(F32) + b.astype(F32)).astype(BF16)
-    def at(t, lag, cond, fn):
-        k = t - lag
-        pl.when(cond & (k >= 0) & (k < K))(lambda: fn(k))
-    yes = dp >= 0
-    def a2(k):
-        c_y2(k).start()
-    def a1(k):
-        c_z1(k).start()
-    def b2(k):
-        c_y2(k).wait_recv()
-        Y2[slot(k)] = add(Y2[slot(k)], g[rows2(k, ctx)])
-        pl.when(outer)(lambda: c_z2(k).start())
-    def b1(k):
-        c_z1(k).wait_recv()
-        Z1[slot(k, 2)] = add(Z1[slot(k, 2)], g[pair1(k)])
-        c_m1(k).start()
-    def c2(k):
-        c_z2(k).wait_recv()
-        Z2[slot(k)] = add(Z2[slot(k)], Y2[slot(k)])
-        c_m2(k).start()
-    def c1(k):
-        c_m1(k).wait_recv()
-        M1[slot(k)] = add(M1[slot(k)], Z1[half1(k, upper)])
-        c_y1(k).start()
-    def d2(k):
-        c_m2(k).wait_recv()
-        out[rows2(k, ctx)] = add(M2[slot(k)], Z2[slot(k)])
-        c_fo(k).start()
-        c_fy(k).start()
-    def d1(k):
-        c_y1(k).wait_recv()
-        out[rows1(k, upper)] = add(Y1[slot(k)], M1[slot(k)])
-        c_fm(k).start()
-        c_fa(k).start()
-    def e2(k):
-        c_fo(k).wait_recv()
-        c_fy(k).start()
-    def e1(k):
-        c_fm(k).wait_recv()
-        c_fb(k).start()
-    def f2(k):
-        c_fy(k).wait_recv()
-        c_y2(k).wait_send()
-        c_fy(k).wait_send()
-    def f2o(k):
-        c_z2(k).wait_send()
-    def f2i(k):
-        c_m2(k).wait_send()
-        c_fo(k).wait_send()
-    def f1o(k):
-        c_fa(k).wait_recv()
-        c_fb(k).wait_recv()
-        c_z1(k).wait_send()
-    def f1i(k):
-        c_m1(k).wait_send()
-        c_y1(k).wait_send()
-        c_fm(k).wait_send()
-        c_fa(k).wait_send()
-        c_fb(k).wait_send()
-    def body(t, carry):
-        at(t, 5 * L, yes, f2)
-        at(t, 5 * L, outer, f2o)
-        at(t, 5 * L, inner, f2i)
-        at(t, 5 * L, outer, f1o)
-        at(t, 5 * L, inner, f1i)
-        at(t, 4 * L, outer, e2)
-        at(t, 4 * L, inner, e1)
-        at(t, 3 * L, inner, d2)
-        at(t, 3 * L, inner, d1)
-        at(t, 2 * L, inner, c2)
-        at(t, 2 * L, inner, c1)
-        at(t, L, yes, b2)
-        at(t, L, inner, b1)
-        at(t, 0, yes, a2)
-        at(t, 0, outer, a1)
-        return carry
-    lax.fori_loop(0, K + 5 * L, body, 0)
-
-def grid_sum(grads):
-    step_rows, lag = 48, 1
-    rows, width = grads.shape
-    steps = rows // (4 * step_rows)
-
-    def slots(n):
-        return pltpu.VMEM((n * step_rows * steps, width), BF16)
-
-    return pl.pallas_call(
-        partial(grid_sum_kernel, step_rows, steps, lag),
-        out_shape=jax.ShapeDtypeStruct(grads.shape, BF16),
-        in_specs=[pl.BlockSpec(memory_space=pltpu.VMEM)],
-        out_specs=pl.BlockSpec(memory_space=pltpu.VMEM),
-        scratch_shapes=[slots(n) for n in (1, 1, 1, 2, 1, 1)]
-        + [pltpu.SemaphoreType.DMA((steps,)) for _ in range(22)],
-        name="grid_sum",
-        compiler_params=pltpu.CompilerParams(
-            collective_id=1, has_side_effects=True, vmem_limit_bytes=62 << 20
-        ),
-    )(grads)
-
-
 def scale_of(values):
     return lax.rsqrt(jnp.mean(values * values, axis=-1, keepdims=True) + EPSILON)
-
-
-def rms_back(values, gain, cotangent):
-    scale = scale_of(values)
-    weighted = gain * cotangent
-    inner = jnp.mean(values * weighted, axis=-1, keepdims=True)
-    back = scale * weighted - values * (scale * scale * scale * inner)
-    return back, jnp.sum(cotangent * values * scale, axis=0)
-
-
-def rotate_back(values, cosine_table, sine_table):
-    half_dim = values.shape[-1] // 2
-    turned = values * sine_table
-    turned = jnp.concatenate([turned[..., half_dim:], -turned[..., :half_dim]], axis=-1)
-    return values * cosine_table + turned
 
 
 def row_blocks(rows, size, body, carry=None):
@@ -932,45 +741,680 @@
     )(real_length, tok_t, cot_t, *weights, gains, head_gains, cosines, sines)
 
 
-def positions(block, rows, bucket_row, true_row):
-    stream_pos = block * rows + jnp.arange(rows, dtype=jnp.int32)
-    starts = jnp.cumsum(bucket_row) - bucket_row
-    ends = starts + bucket_row
-    inside = (
-        (stream_pos[:, None] >= starts[None, :]) & (stream_pos[:, None] < ends[None, :])
-    ).astype(jnp.int32)
-    slot_ids = jnp.arange(bucket_row.shape[0], dtype=jnp.int32)
-    seq_id = jnp.sum(inside * slot_ids[None, :], axis=1)
-    seq_pos = stream_pos - jnp.sum(inside * starts[None, :], axis=1)
-    is_valid = (seq_pos < jnp.sum(inside * true_row[None, :], axis=1)).astype(jnp.int32)
-    return seq_id, stream_pos, seq_pos, is_valid
-
-
-def allowed_pairs(query_layout, key_layout):
-    return (
-        (key_layout[3][None, :] == 1)
-        & (key_layout[0][None, :] == query_layout[0][:, None])
-        & (key_layout[1][None, :] <= query_layout[1][:, None])
-    )
-
-
-def attend(query16, key16, value16, allowed, score_scale):
-    scores = contract(query16, key16, 1, 1) * score_scale
-    scores = jnp.where(allowed, scores, MASKED)
-    exp_scores = jnp.exp(scores - jnp.max(scores, axis=-1, keepdims=True))
-    probs = exp_scores / jnp.sum(exp_scores, axis=-1, keepdims=True)
-    attended = jnp.dot(probs.astype(BF16), value16, preferred_element_type=F32)
-    return probs, attended.astype(BF16)
-
-
-def attend_back(query16, key16, value16, probs, d_attended16, score_scale):
-    d_probs = contract(d_attended16, value16, 1, 1)
-    inner = jnp.sum(probs * d_probs, axis=-1, keepdims=True)
-    d_scores16 = (probs * (d_probs - inner)).astype(BF16)
-    d_query = jnp.dot(d_scores16, key16, preferred_element_type=F32) * score_scale
-    d_key = contract(d_scores16, query16, 0, 0) * score_scale
-    d_value = contract(probs.astype(BF16), d_attended16, 0, 0)
-    return d_query, d_key, d_value
+def backward_kernel(
+    step_rows, steps, ring, gate_hidden,
+    real_length, tok, x_in, cot_in, n_in, q_in, kv_in, far_in, att_in, attn_in, mid_in, hid_in,
+    dffn_in, dg_in, du_in, gain_ffn, w_q, w_k, w_v, w_o, w_g, w_u, gains, head_gains, gain_col,
+    cosines, sines,
+    out, xg_t, gain_rows, gain_cols,
+    g, y2, z2, m2, z1, m1, y1, hid, dg, du, mid, dffn, w_tiles, acc, part, near, far, dm, cot, attn,
+    v_o, v_qkv, dkv_new, norm_near, norm_far, row_part,
+    row_near, kv_near, kv_far, turned, head_sums, row_sums, sum_slots, sum_new, col_slots,
+    col_new,
+    load_sem, tile_sem, keep_sem, chain_send, chain_recv, peer_send, peer_recv,
+):
+    dp, ctx, tp = lax.axis_index("dp"), lax.axis_index("ctx"), lax.axis_index("tp")
+    s, K = step_rows, steps
+    upper = dp // 2
+    odd = tp % 2
+    outer = (dp == 0) | (dp == 3)
+    inner = jnp.logical_not(outer)
+    yes = dp >= 0
+    core_index = tp + 1 - 2 * odd
+    x_index = (tp + 2) % 4
+    cross_index = (core_index + 2) % 4
+    z_index = dp + 1 - 2 * (dp % 2)
+    core_peer, x_peer = (dp, ctx, core_index), (dp, ctx, x_index)
+    y_peer, z_peer, m_peer = (dp, 1 - ctx, tp), (z_index, ctx, tp), (3 - dp, ctx, tp)
+    features, rows = tok.shape[0], tok.shape[1] // 2
+    width = 4 * features
+    hidden = w_g.shape[0]
+    head_dim = w_k.shape[1]
+    half = rows // 2
+    kv_rows = head_dim // 2
+    score_scale = head_dim ** (-0.5)
+
+    def remote(source, target, send, recv, peer):
+        return pltpu.make_async_remote_copy(
+            src_ref=source, dst_ref=target, send_sem=send, recv_sem=recv,
+            device_id=peer, device_id_type=MESH,
+        )
+
+    def chunk(c):
+        return pl.ds(c * rows, rows)
+
+    def multiple(start, size):
+        return pl.ds(pl.multiple_of(start, size), size)
+
+    dqkv, kv16 = dg.at[:, 0 : 3 * head_dim], dg.at[:, 3 * head_dim : 5 * head_dim]
+    dkv, dkv_far = du.at[:, 0 : 2 * head_dim], du.at[0:rows, 2 * head_dim : 4 * head_dim]
+    far_kv = du.at[rows : 2 * rows, 2 * head_dim : 4 * head_dim]
+    q16, att = du.at[:, 4 * head_dim : 5 * head_dim], du.at[:, 5 * head_dim : 6 * head_dim]
+
+    tok_own = dm.at[0:features, 0 : 2 * rows]
+
+    pairs = (
+        (hid_in, hid), (dffn_in, dffn), (dg_in, dg), (mid_in, mid), (du_in, du), (cot_in, cot),
+        (attn_in, attn), (w_o, v_o),
+        (w_q, v_qkv.at[:, 0:head_dim]), (w_k, v_qkv.at[:, head_dim : 2 * head_dim]),
+        (w_v, v_qkv.at[:, 2 * head_dim : 3 * head_dim]),
+    )
+    count = len(pairs)
+
+    def load(j):
+        return pltpu.make_async_copy(pairs[j][0], pairs[j][1], load_sem.at[j])
+
+    late_pairs = (
+        (x_in, dffn), (n_in, mid), (q_in, q16), (kv_in, kv16), (far_in, far_kv), (att_in, att),
+    )
+
+    def load_tok():
+        return pltpu.make_async_copy(tok, tok_own, load_sem.at[count + len(late_pairs)])
+
+    def late_load(j):
+        return pltpu.make_async_copy(late_pairs[j][0], late_pairs[j][1], load_sem.at[count + j])
+
+    for j in range(count):
+        load(j).start()
+    barrier = pltpu.get_barrier_semaphore()
+    for peer in (core_peer, x_peer, y_peer, z_peer, m_peer):
+        pl.semaphore_signal(barrier, inc=1, device_id=peer, device_id_type=MESH)
+    pl.semaphore_wait(barrier, 5)
+
+    base = 2 * s * K
+
+    def rows2(k, h):
+        return multiple((2 * k + h) * s, s)
+
+    def rows1(k, h):
+        return multiple(base + (2 * k + h) * s, s)
+
+    def pair1(k):
+        return pl.ds(pl.multiple_of(base + 2 * k * s, s), 2 * s)
+
+    def slot(k):
+        return multiple((k % ring) * s, s)
+
+    def slot_pair(k):
+        return multiple((k % ring) * 2 * s, 2 * s)
+
+    def slot_half(k, h):
+        return multiple(((k % ring) * 2 + h) * s, s)
+
+    def chain(j, k, source, target, peer):
+        return remote(source, target, chain_send.at[j, k], chain_recv.at[j, k], peer)
+
+    def keep(j, k, source, target):
+        return pltpu.make_async_copy(source, target, keep_sem.at[j, k])
+
+    def c_y2(k):
+        return chain(0, k, g.at[rows2(k, 1 - ctx)], y2.at[slot(k)], y_peer)
+
+    def c_z2(k):
+        return chain(1, k, y2.at[slot(k)], z2.at[slot(k)], z_peer)
+
+    def c_m2(k):
+        return chain(2, k, z2.at[slot(k)], m2.at[slot(k)], m_peer)
+
+    def c_fo(k):
+        return chain(3, k, m2.at[slot(k)], out.at[rows2(k, ctx)], z_peer)
+
+    def c_fy(k):
+        return chain(4, k, m2.at[slot(k)], out.at[rows2(k, ctx)], y_peer)
+
+    def c_fy_outer(k):
+        return chain(4, k, out.at[rows2(k, ctx)], out.at[rows2(k, ctx)], y_peer)
+
+    def c_z1(k):
+        return chain(5, k, g.at[pair1(k)], z1.at[slot_pair(k)], z_peer)
+
+    def c_m1(k):
+        return chain(6, k, z1.at[slot_half(k, 1 - upper)], m1.at[slot(k)], m_peer)
+
+    def c_y1(k):
+        return chain(7, k, m1.at[slot(k)], y1.at[slot(k)], y_peer)
+
+    def c_fm(k):
+        return chain(8, k, y1.at[slot(k)], out.at[rows1(k, upper)], m_peer)
+
+    def c_fa(k):
+        return chain(9, k, y1.at[slot(k)], out.at[rows1(k, upper)], z_peer)
+
+    def c_fb(k):
+        return chain(10, k, out.at[rows1(k, 1 - upper)], out.at[rows1(k, 1 - upper)], z_peer)
+
+    def keep2(k):
+        return keep(0, k, m2.at[slot(k)], out.at[rows2(k, ctx)])
+
+    def keep1(k):
+        return keep(1, k, y1.at[slot(k)], out.at[rows1(k, upper)])
+
+    def b2(k):
+        c_y2(k).wait_recv()
+        y2[slot(k), :] = add16(y2[slot(k), :], g[rows2(k, ctx), :])
+        pl.when(outer)(lambda: c_z2(k).start())
+
+    def b1(k):
+        c_z1(k).wait_recv()
+        z1[slot_pair(k), :] = add16(z1[slot_pair(k), :], g[pair1(k), :])
+        c_m1(k).start()
+
+    def c2(k):
+        c_z2(k).wait_recv()
+        z2[slot(k), :] = add16(z2[slot(k), :], y2[slot(k), :])
+        c_m2(k).start()
+
+    def c1(k):
+        c_m1(k).wait_recv()
+        m1[slot(k), :] = add16(m1[slot(k), :], z1[slot_half(k, upper), :])
+        c_y1(k).start()
+
+    def d2(k):
+        c_m2(k).wait_recv()
+        m2[slot(k), :] = add16(m2[slot(k), :], z2[slot(k), :])
+        c_fo(k).start()
+        c_fy(k).start()
+        keep2(k).start()
+
+    def d1(k):
+        c_y1(k).wait_recv()
+        y1[slot(k), :] = add16(y1[slot(k), :], m1[slot(k), :])
+        c_fm(k).start()
+        c_fa(k).start()
+        keep1(k).start()
+
+    def e2(k):
+        c_fo(k).wait_recv()
+        c_fy_outer(k).start()
+
+    def e1(k):
+        c_fm(k).wait_recv()
+        c_fb(k).start()
+
+    def f2(k):
+        c_fy(k).wait_recv()
+        c_y2(k).wait_send()
+
+    def f_outer(k):
+        c_z2(k).wait_send()
+        c_fy_outer(k).wait_send()
+        c_fa(k).wait_recv()
+        c_fb(k).wait_recv()
+        c_z1(k).wait_send()
+
+    def f_inner(k):
+        keep2(k).wait()
+        keep1(k).wait()
+        for copy in (c_m2, c_fo, c_fy, c_m1, c_y1, c_fm, c_fa, c_fb):
+            copy(k).wait_send()
+
+    hops = (
+        (5, yes, f2), (5, outer, f_outer), (5, inner, f_inner), (4, outer, e2), (4, inner, e1),
+        (3, inner, d2), (3, inner, d1), (2, inner, c2), (2, inner, c1), (1, yes, b2), (1, inner, b1),
+        (0, yes, lambda k: c_y2(k).start()), (0, outer, lambda k: c_z1(k).start()),
+    )
+
+    def grad_tile(index, first, size):
+        left, right = ((hid, dffn), (dg, mid), (du, mid))[index]
+        at = first if isinstance(first, int) else pl.multiple_of(first, 256)
+        tile = contract(left[:, pl.ds(at, size)], right[...], 0, 0)
+        start = index * hidden + first
+        g[pl.ds(start if isinstance(start, int) else pl.multiple_of(start, 64), size), :] = (
+            tile.astype(BF16)
+        )
+
+    full = hidden // 256
+    tail = hidden - 256 * full
+
+    def mid_part(c):
+        tiles = column_tiles(hidden, 256)
+
+        def fetch(j):
+            first, size = tiles[j]
+            return [
+                pltpu.make_async_copy(
+                    w.at[pl.ds(first, size)], w_tiles.at[i, j % 2, pl.ds(0, size)],
+                    tile_sem.at[i, j % 2],
+                )
+                for i, w in enumerate((w_g, w_u))
+            ]
+
+        for copy in fetch(0):
+            copy.start()
+        for j, (first, size) in enumerate(tiles):
+            if j + 1 < len(tiles):
+                for copy in fetch(j + 1):
+                    copy.start()
+            for copy in fetch(j):
+                copy.wait()
+            cols = pl.ds(first, size)
+            term = dot_nn(dg[chunk(c), cols], w_tiles[0, j % 2, 0:size, :]) + dot_nn(
+                du[chunk(c), cols], w_tiles[1, j % 2, 0:size, :]
+            )
+            if j == 0:
+                acc[...] = term
+            else:
+                acc[...] += term
+        part[c] = acc[...].astype(BF16)
+
+    def own_half(index):
+        return multiple(index * half, half)
+
+    def peer_copy(j, source, target, peer):
+        return remote(source, target, peer_send.at[j], peer_recv.at[j], peer)
+
+    def sum_copies(c):
+        final = dm.at[multiple(c * rows + odd * half, half)]
+        return (
+            peer_copy(3 * c, part.at[c, own_half(1 - odd)], near.at[c], core_peer),
+            peer_copy(3 * c + 1, near.at[c], far.at[c], x_peer),
+            peer_copy(3 * c + 2, final, final, core_peer),
+        )
+
+    def sum_begin(c):
+        mid_part(c)
+        sum_copies(c)[0].start()
+
+    def sum_cross(c):
+        copies = sum_copies(c)
+        copies[0].wait_recv()
+        near[c] = add16(part[c, own_half(odd)], near[c])
+        copies[1].start()
+
+    def sum_back(c):
+        copies = sum_copies(c)
+        copies[1].wait_recv()
+        dm[multiple(c * rows + odd * half, half), :] = add16(near[c], far[c])
+        copies[2].start()
+
+    def norms_back(c):
+        sum_copies(c)[2].wait_recv()
+
+        def body(block, state):
+            at = pl.ds(c * rows + block.start, block.size)
+            branch = attn[at, :].astype(F32)
+            scale_a = scale_of(branch)
+            unit_a = branch * scale_a
+            resid = dffn[at, :].astype(F32) + unit_a * gains[1:2, :]
+            scale_r = scale_of(resid)
+            unit_r = resid * scale_r
+            grad = dm[at, :].astype(F32)
+            weighted = grad * gains[2:3, :]
+            mean = jnp.mean(unit_r * weighted, axis=-1, keepdims=True)
+            d_resid = cot[at, :].astype(F32) + scale_r * (weighted - unit_r * mean)
+            weighted = d_resid * gains[1:2, :]
+            mean = jnp.mean(unit_a * weighted, axis=-1, keepdims=True)
+            cot[at, :] = d_resid.astype(BF16)
+            attn[at, :] = (scale_a * (weighted - unit_a * mean)).astype(BF16)
+            return (
+                state[0] + (d_resid * unit_a).reshape(-1, 8, width).sum(axis=0),
+                state[1] + (grad * unit_r).reshape(-1, 8, width).sum(axis=0),
+            )
+
+        zero = jnp.zeros((8, width), F32)
+        sum_a, sum_r = row_blocks(rows, 16, body, (zero, zero))
+        if c == 1:
+            row_sums[0], row_sums[1] = sum_a, sum_r
+        else:
+            row_sums[0] += sum_a
+            row_sums[1] += sum_r
+
+    def head_back(grad, at, j):
+        cosine, sine = cosines[at, :], sines[at, :]
+        low, high = grad[:, : head_dim // 2], grad[:, head_dim // 2 :]
+        grad = jnp.concatenate([low * cosine + high * sine, high * cosine - low * sine], axis=1)
+        cols = pl.ds(j * head_dim, head_dim)
+        raw = dot_nn(mid[at, :], v_qkv[:, cols])
+        scale = scale_of(raw)
+        unit = raw * scale
+        weighted = grad * head_gains[j : j + 1, :]
+        mean = jnp.mean(unit * weighted, axis=-1, keepdims=True)
+        dqkv[at, cols] = (scale * (weighted - unit * mean)).astype(BF16)
+        head_sums[j] += (grad * unit).reshape(-1, 8, head_dim).sum(axis=0)
+
+    def attend_back_rows(c):
+        d_keys, d_values = [0.0, 0.0], [0.0, 0.0]
+        for first in range(0, rows, half):
+            at = pl.ds(c * rows + first, half)
+            query = q16[at, :]
+            d_out = dot_nt(attn[at, :], v_o[...]).astype(BF16)
+            row_id = first + lax.broadcasted_iota(jnp.int32, (half, rows), 0)
+            key_id = lax.broadcasted_iota(jnp.int32, (half, rows), 1)
+            allowed = key_id <= row_id
+            if c == 1:
+                allowed = allowed & (rows + key_id < real_length[0, 0])
+            keys = [(kv16[chunk(c), :head_dim], kv16[chunk(c), head_dim:], allowed)]
+            if c == 1:
+                keys.append((far_kv[:, :head_dim], far_kv[:, head_dim:], None))
+            scores = []
+            for key, _, mask in keys:
+                score = dot_nt(query, key) * score_scale
+                scores.append(score if mask is None else jnp.where(mask, score, MASKED))
+            most = scores[0].max(axis=1, keepdims=True)
+            for score in scores[1:]:
+                most = jnp.maximum(most, score.max(axis=1, keepdims=True))
+            exps = [jnp.exp(score - most) for score in scores]
+            total = sum(e.sum(axis=1, keepdims=True) for e in exps)
+            probs = [e / total for e in exps]
+            d_probs = [dot_nt(d_out, key[1]) for key in keys]
+            mean = sum((p * d).sum(axis=1, keepdims=True) for p, d in zip(probs, d_probs))
+            d_query = 0.0
+            for i, key in enumerate(keys):
+                d_score = (probs[i] * (d_probs[i] - mean)).astype(BF16)
+                d_query += dot_nn(d_score, key[0])
+                d_keys[i] += contract(d_score, query, 0, 0)
+                d_values[i] += contract(probs[i].astype(BF16), d_out, 0, 0)
+            head_back(d_query * score_scale, at, 0)
+        dkv[chunk(c), :head_dim] = (d_keys[0] * score_scale).astype(BF16)
+        dkv[chunk(c), head_dim:] = d_values[0].astype(BF16)
+        if c == 1:
+            dkv_far[:, :head_dim] = (d_keys[1] * score_scale).astype(BF16)
+            dkv_far[:, head_dim:] = d_values[1].astype(BF16)
+            far_copy().start()
+
+    def far_copy():
+        return peer_copy(6, dkv_far, dkv_new, y_peer)
+
+    def keys_back(c):
+        if c == 0:
+            far_copy().wait_recv()
+        for first in range(0, rows, half):
+            at = pl.ds(c * rows + first, half)
+            grad = dkv[at, :].astype(F32)
+            if c == 0:
+                grad = grad + dkv_new[pl.ds(first, half), :].astype(F32)
+            head_back(grad[:, :head_dim], at, 1)
+            dqkv[at, 2 * head_dim :] = grad[:, head_dim:].astype(BF16)
+
+    def cell(c, j):
+        index = 4 * c + j
+        return hid.at[pl.ds(index // 3 * features, features), pl.ds(index % 3 * rows, rows)]
+
+    owners = (tp, core_index, x_index, cross_index)
+
+    def scatter_copies(c):
+        return (
+            peer_copy(7 + 6 * c, cell(c, 1), norm_near.at[c, 0], core_peer),
+            peer_copy(8 + 6 * c, cell(c, 3), norm_near.at[c, 1], core_peer),
+            peer_copy(9 + 6 * c, row_part.at[c, 0], row_near.at[c, 0], core_peer),
+            peer_copy(10 + 6 * c, cell(c, 2), norm_far.at[c], x_peer),
+            peer_copy(11 + 6 * c, row_part.at[c, 1], row_near.at[c, 1], x_peer),
+        )
+
+    def scatter_begin(c):
+        for j in range(4):
+            weights = v_qkv[multiple(owners[j] * features, features), :]
+            cell(c, j)[...] = dot_nt(weights, dqkv[chunk(c), :]).astype(BF16)
+        for first in range(0, rows, half):
+            at = pl.ds(c * rows + first, half)
+            raw = dot_nn(mid[at, :], v_qkv[...])
+            inner_sum = (raw * dqkv[at, :].astype(F32)).sum(axis=1, keepdims=True)
+            scale = scale_of(dffn[at, :].astype(F32))
+            lane = lax.broadcasted_iota(jnp.int32, (half, 128), 1)
+            both = jnp.where(lane == 0, inner_sum, scale)
+            row_part[c, 0, :, pl.ds(first, half)] = both.T[0:8, :]
+        for copy in scatter_copies(c)[:3]:
+            copy.start()
+
+    def scatter_cross(c):
+        copies = scatter_copies(c)
+        for copy in copies[:3]:
+            copy.wait_recv()
+        cell(c, 0)[...] = add16(cell(c, 0)[...], norm_near[c, 0])
+        cell(c, 2)[...] = add16(cell(c, 2)[...], norm_near[c, 1])
+        row_part[c, 1] = row_part[c, 0] + row_near[c, 0]
+        copies[3].start()
+        copies[4].start()
+
+    def scatter_end(c):
+        copies = scatter_copies(c)
+        copies[3].wait_recv()
+        copies[4].wait_recv()
+        for first in range(0, width, 128):
+            turned[first : first + 128, :] = cot[chunk(c), first : first + 128].T
+        lane = (ctx if c == 0 else 1 - ctx) * rows
+        lanes = pl.ds(pl.multiple_of(lane, rows), rows)
+        grad = cell(c, 0)[...].astype(F32) + norm_far[c].astype(F32)
+        values = tok_own[:, lanes].astype(F32)
+        scale = row_part[c, 0, 1:2, :]
+        inner_sum = row_part[c, 1, 0:1, :] + row_near[c, 1, 0:1, :]
+        d_in = scale * (grad * gain_col[:, 0:1]) - values * (
+            scale * scale * inner_sum * (1.0 / width)
+        )
+        d_resid = turned[multiple(tp * features, features), :].astype(F32)
+        xg_t[:, lanes] = (d_resid + d_in).astype(BF16)
+        column = jnp.sum(grad * values * scale, axis=1, keepdims=True)
+        column = jnp.broadcast_to(column, (features, 128))
+        if c == 1:
+            col_slots[0] = column
+        else:
+            col_slots[0] += column
+
+    at_out = 3 * hidden
+    at_query = at_out + head_dim
+    at_kv = at_query + head_dim
+
+    def small_grads():
+        g[pl.ds(at_out, head_dim), :] = contract(att[...], attn[...], 0, 0).astype(BF16)
+        g[pl.ds(at_query, head_dim), :] = contract(dqkv[:, :head_dim], mid[...], 0, 0).astype(BF16)
+        spare = g.shape[0] - at_kv - kv_rows
+        g[pl.ds(at_kv + kv_rows, spare), :] = jnp.zeros((spare, width), BF16)
+        sum_copies(1)[0].wait_send()
+        for j in range(4):
+            cols = multiple(head_dim + owners[j] * kv_rows, kv_rows)
+            part[1, pl.ds(j * kv_rows, kv_rows), :] = contract(dqkv[:, cols], mid[...], 0, 0).astype(
+                BF16
+            )
+        for copy in kv_copies()[:2]:
+            copy.start()
+
+    def kv_copies():
+        return (
+            peer_copy(19, part.at[1, pl.ds(kv_rows, kv_rows)], kv_near.at[0], core_peer),
+            peer_copy(20, part.at[1, pl.ds(3 * kv_rows, kv_rows)], kv_near.at[1], core_peer),
+            peer_copy(21, part.at[1, pl.ds(2 * kv_rows, kv_rows)], kv_far, x_peer),
+        )
+
+    def kv_cross():
+        copies = kv_copies()
+        copies[0].wait_recv()
+        copies[1].wait_recv()
+        for j in range(2):
+            at = pl.ds(2 * j * kv_rows, kv_rows)
+            part[1, at, :] = add16(part[1, at, :], kv_near[j])
+        copies[2].start()
+
+    def kv_end():
+        kv_copies()[2].wait_recv()
+        g[pl.ds(at_kv, kv_rows), :] = add16(part[1, pl.ds(0, kv_rows), :], kv_far[...])
+
+    sum_peers = (core_peer, x_peer, y_peer, z_peer, m_peer)
+
+    def sum_copy(j):
+        return peer_copy(22 + j, sum_slots.at[j], sum_new.at[j], sum_peers[j])
+
+    def col_copy(j):
+        return peer_copy(27 + j, col_slots.at[j], col_new.at[j], sum_peers[2 + j])
+
+    def gains_begin():
+        sum_slots[0] = jnp.zeros((8, width), F32)
+        for j, values in enumerate((row_sums[0], row_sums[1], gain_ffn[...])):
+            sum_slots[0, j : j + 1, :] = 0.25 * values.sum(axis=0, keepdims=True)
+        for j in range(2):
+            sum_slots[0, 3:4, j * head_dim : (j + 1) * head_dim] = head_sums[j].sum(
+                axis=0, keepdims=True
+            )
+        sum_copy(0).start()
+        col_copy(0).start()
+
+    def gains_hop(j):
+        sum_copy(j).wait_recv()
+        if j < 4:
+            sum_slots[j + 1] = sum_slots[j] + sum_new[j]
+            sum_copy(j + 1).start()
+        else:
+            gain_rows[...] = sum_slots[j] + sum_new[j]
+        if j < 3:
+            col_copy(j).wait_recv()
+        if j < 2:
+            col_slots[j + 1] = col_slots[j] + col_new[j]
+            col_copy(j + 1).start()
+        if j == 2:
+            mine = multiple(tp * features, features)
+            gain_cols[mine, :] = col_slots[2] + col_new[2]
+            gather_copies()[0].start()
+            gather_copies()[1].start()
+        if j == 3:
+            gather_copies()[1].wait_recv()
+            gather_copies()[2].start()
+        if j == 4:
+            gather_copies()[0].wait_recv()
+            gather_copies()[2].wait_recv()
+
+    def gather_copies():
+        mine = gain_cols.at[multiple(tp * features, features)]
+        theirs = gain_cols.at[multiple(x_index * features, features)]
+        return (
+            peer_copy(30, mine, mine, core_peer),
+            peer_copy(31, mine, mine, x_peer),
+            peer_copy(32, theirs, theirs, core_peer),
+        )
+
+    def load_late():
+        for j in range(len(late_pairs)):
+            late_load(j).start()
+
+    def wait_late():
+        for j in range(len(late_pairs)):
+            late_load(j).wait()
+        for j in range(5, count):
+            load(j).wait()
+        head_sums[...] = jnp.zeros(head_sums.shape, F32)
+
+    gate_tiles = gate_hidden // 256
+    load(0).wait()
+    load(1).wait()
+    grad_tile(0, 0, 256)
+    load(2).wait()
+    load(3).wait()
+    for j in range(gate_tiles, full):
+        grad_tile(1, 256 * j, 256)
+    if tail:
+        grad_tile(1, 256 * full, tail)
+    load(4).wait()
+
+    last_up = 1 + full
+    stages = (
+        (last_up + gate_tiles + 1, load_late),
+        (2, lambda: sum_begin(1)),
+        (3, lambda: sum_cross(1)),
+        (4, lambda: sum_begin(0)),
+        (5, lambda: sum_cross(0)),
+        (6, lambda: sum_back(1)),
+        (8, lambda: sum_back(0)),
+        (last_up + gate_tiles + 2, wait_late),
+    )
+    first_back = last_up + gate_tiles + 2
+    stages += tuple(
+        (first_back + j, action)
+        for j, action in enumerate(
+            (
+                lambda: norms_back(1),
+                lambda: attend_back_rows(1),
+                lambda: norms_back(0),
+                lambda: (sum_copies(0)[2].wait_send(), load_tok().start(), attend_back_rows(0)),
+                lambda: keys_back(1),
+                lambda: scatter_begin(1),
+                lambda: keys_back(0),
+                lambda: (scatter_cross(1), scatter_begin(0)),
+                small_grads,
+                lambda: (scatter_cross(0), kv_cross()),
+                lambda: (load_tok().wait(), scatter_end(1)),
+                lambda: (scatter_end(0), kv_end()),
+                gains_begin,
+            )
+        )
+    )
+    at_gains = first_back + 13
+    stages += tuple((at_gains + j, partial(gains_hop, j)) for j in range(5))
+
+    def body(t, carry):
+        pl.when(t < full - 1)(lambda: grad_tile(0, 256 * (t + 1), 256))
+        if tail:
+            pl.when(t == full - 1)(lambda: grad_tile(0, 256 * full, tail))
+        pl.when((t >= 1) & (t < last_up))(lambda: grad_tile(2, 256 * (t - 1), 256))
+        if tail:
+            pl.when(t == last_up)(lambda: grad_tile(2, 256 * full, tail))
+        late = t - last_up - 1
+        pl.when((late >= 0) & (late < gate_tiles))(lambda: grad_tile(1, 256 * late, 256))
+        for lag, who, action in hops:
+            k = t - lag
+            pl.when(who & (k >= 0) & (k < K))(partial(action, k))
+        for step, action in stages:
+            pl.when(t == step)(lambda action=action: action() and None)
+        return carry
+
+    lax.fori_loop(0, K + 5, body, 0)
+    done = [sum_copies(0)[j] for j in (0, 1)] + [sum_copies(1)[j] for j in (1, 2)]
+    done += [far_copy(), *scatter_copies(0), *scatter_copies(1), *kv_copies()]
+    done += [sum_copy(j) for j in range(5)] + [col_copy(j) for j in range(3)]
+    for copy in done + list(gather_copies()):
+        copy.wait_send()
+
+
+def backward(real_length, tok_t, forward_outs, gain_ffn, weights, gains, head_gains, gain_col, tables):
+    features, rows = tok_t.shape
+    half = rows // 2
+    width = 4 * features
+    w_q, w_k, w_v, w_o, w_g, w_u = weights
+    hidden, head_dim = w_g.shape[0], w_k.shape[1]
+    kv_rows = head_dim // 2
+    step_rows, ring = 48, 6
+    needed = 3 * hidden + 2 * head_dim + kv_rows
+    steps = -(-needed // (4 * step_rows))
+    total = 4 * step_rows * steps
+    gate_hidden = total // 2 - hidden
+    whole = pl.BlockSpec(memory_space=pltpu.VMEM)
+    there = pl.BlockSpec(memory_space=pl.ANY)
+
+    def low(*shape):
+        return pltpu.VMEM(shape, BF16)
+
+    def high(*shape):
+        return pltpu.VMEM(shape, F32)
+
+    slots = [low(n * step_rows * ring, width) for n in (1, 1, 1, 2, 1, 1)]
+    return pl.pallas_call(
+        partial(backward_kernel, step_rows, steps, ring, gate_hidden),
+        out_shape=(
+            jax.ShapeDtypeStruct((total, width), BF16),
+            jax.ShapeDtypeStruct((features, rows), BF16),
+            jax.ShapeDtypeStruct((8, width), F32),
+            jax.ShapeDtypeStruct((width, 128), F32),
+        ),
+        in_specs=[pl.BlockSpec(memory_space=pltpu.SMEM)] + [there] * 14 + [whole] + [there] * 6
+        + [whole] * 5,
+        out_specs=[there, whole, whole, whole],
+        scratch_shapes=[
+            low(total, width), *slots,
+            low(rows, hidden), low(rows, hidden), low(rows, hidden), low(rows, width),
+            low(rows, width), low(2, 2, 256, width), high(half, width), low(2, half, width),
+            low(2, half // 2, width), low(2, half // 2, width), low(rows, width), low(rows, width),
+            low(rows, width), low(head_dim, width), low(width, 3 * head_dim),
+            low(half, 2 * head_dim), low(2, 2, features, half), low(2, features, half),
+            high(2, 2, 8, half), high(2, 2, 8, half), low(2, kv_rows, width), low(kv_rows, width),
+            low(width, half), high(2, 8, head_dim), high(2, 8, width),
+            high(5, 8, width), high(5, 8, width), high(3, features, 128), high(3, features, 128),
+            pltpu.SemaphoreType.DMA((20,)), pltpu.SemaphoreType.DMA((2, 2)),
+            pltpu.SemaphoreType.DMA((2, steps)), pltpu.SemaphoreType.DMA((11, steps)),
+            pltpu.SemaphoreType.DMA((11, steps)), pltpu.SemaphoreType.DMA((33,)),
+            pltpu.SemaphoreType.DMA((33,)),
+        ],
+        name="backward",
+        compiler_params=pltpu.CompilerParams(
+            collective_id=1, has_side_effects=True, vmem_limit_bytes=63 << 20
+        ),
+    )(real_length, tok_t, *forward_outs, gain_ffn, *weights, gains, head_gains, gain_col, *tables)
 
 
 def paired_shards(
@@ -1001,7 +1445,6 @@
         gain.astype(F32)
         for gain in (gain_in, gain_post_attn, gain_pre_ffn, gain_post_ffn, gain_query, gain_key)
     ]
-    both = range(2)
     width = 4 * feature_cols
     seq_pos = jnp.arange(2 * rows, dtype=jnp.int32)
     cosines, sines = [table[:, : head_dim // 2] for table in rope_tables(seq_pos, head_dim)]
@@ -1016,113 +1459,16 @@
         real_length, tokens.T, out_grad.T, weights, gains, head_gains, cosines, sines
     )
 
-    def two(values):
-        return [values[:rows], values[rows:]]
-
-    inputs16, cots16, normed16 = two(x16), two(cot16), two(n16)
-    inputs = [values.astype(F32) for values in inputs16]
-    cots = [values.astype(F32) for values in cots16]
-    query_raw, key_raw = two(raw[:, :head_dim]), two(raw[:, head_dim:])
-    query16, key16, value16 = two(q16), two(kv16[:, :head_dim]), two(kv16[:, head_dim:])
-    keys = [key16[0], jnp.concatenate([far_kv[:, :head_dim], key16[1]], axis=0)]
-    values_ = [value16[0], jnp.concatenate([far_kv[:, head_dim:], value16[1]], axis=0)]
-    ids = jnp.arange(rows, dtype=jnp.int32)
-    causal = ids[None, :] <= ids[:, None]
-    real = causal & (rows + ids[None, :] < real_length[0, 0])
-    allowed = [causal, jnp.concatenate([jnp.ones_like(real), real], axis=1)]
-    probs = [
-        attend(query16[i], keys[i], values_[i], allowed[i], score_scale)[0] for i in both
-    ]
-    attended16 = two(att16)
-    attention = [values.astype(F32) for values in two(attn16)]
-    residual = [inputs[i] + rms_norm(attention[i], g_pa) for i in both]
-    d_gate16, d_up16 = two(dg16), two(du16)
-    tables = [
-        [jnp.concatenate([t, t], axis=1) for t in (cosines[at], sines[at])]
-        for at in (slice(0, rows), slice(rows, 2 * rows))
-    ]
-    gain_sums = [jnp.sum(gain_sum, axis=0), 0.0]
-    token_parts = halves(tokens, ctx_index)
-
-    grad_down = contract(hid16, dffn16, 0, 0).astype(BF16)
-    grad_gate = contract(dg16, mid16, 0, 0).astype(BF16)
-    grad_up = contract(du16, mid16, 0, 0).astype(BF16)
-
-    d_resid, d_attn16, d_attended16 = [], [], []
-    pf_sums, pa_sums = [], []
-    for i in both:
-        part = contract(d_gate16[i], w_gate, 1, 1) + contract(d_up16[i], w_up, 1, 1)
-        d_mid = tp_sum(part.astype(BF16)).astype(F32)
-        d_norm, d_pf = rms_back(residual[i], g_pf, d_mid)
-        d_resid.append(cots[i] + d_norm)
-        d_attn, d_pa = rms_back(attention[i], g_pa, d_resid[i])
-        d_attn16.append(d_attn.astype(BF16))
-        d_attended16.append(contract(d_attn16[i], w_out, 1, 1).astype(BF16))
-        pf_sums.append(d_pf)
-        pa_sums.append(d_pa)
-    grad_out = contract(
-        att16, jnp.concatenate(d_attn16, axis=0), 0, 0
-    ).astype(BF16)
-
-    d_query, d_key, d_value = [], [], []
-    for i in both:
-        dq, dk, dv = attend_back(
-            query16[i], keys[i], values_[i], probs[i], d_attended16[i], score_scale
-        )
-        d_query.append(dq)
-        d_key.append(dk)
-        d_value.append(dv)
-    far_dk = lax.ppermute(d_key[1][:rows].astype(BF16), "ctx", MESH_PAIR)
-    far_dv = lax.ppermute(d_value[1][:rows].astype(BF16), "ctx", MESH_PAIR)
-    d_key = [d_key[0] + far_dk.astype(F32), d_key[1][rows:]]
-    d_value = [d_value[0] + far_dv.astype(F32), d_value[1][rows:]]
-
-    w_qkv = jnp.concatenate([w_query, w_key, w_value], axis=1)
-    w_blocks = w_qkv.reshape(4, feature_cols, w_qkv.shape[1])
-    w_near = [
-        lax.dynamic_index_in_dim(w_blocks, tp_index ^ j, keepdims=False) for j in range(4)
-    ]
-    g_in_own = lax.dynamic_slice_in_dim(g_in, tp_index * feature_cols, feature_cols)
-    d_qkv16, x_parts, q_sums, k_sums, in_sums = [], [], [], [], []
-    for i in both:
-        dq, d_gq = rms_back(query_raw[i], g_q, rotate_back(d_query[i], *tables[i]))
-        dk, d_gk = rms_back(key_raw[i], g_k, rotate_back(d_key[i], *tables[i]))
-        q_sums.append(d_gq)
-        k_sums.append(d_gk)
-        d_qkv16.append(jnp.concatenate([dq, dk, d_value[i]], axis=1).astype(BF16))
-        parts = [contract(d_qkv16[i], w, 1, 1).astype(BF16) for w in w_near]
-        near = lax.ppermute(jnp.stack([parts[1], parts[3]]), "tp", XOR1)
-        mine = add16(parts[0], near[0])
-        theirs = add16(parts[2], near[1])
-        u = add16(mine, lax.ppermute(theirs, "tp", XOR2)).astype(F32)
-        own_in = token_parts[i].astype(F32)
-        weighted = g_in_own * u
-        inner = jnp.sum(own_in * weighted, axis=-1)
-        inner = inner + lax.ppermute(inner, "tp", XOR1)
-        inner = inner + lax.ppermute(inner, "tp", XOR2)
-        inner = inner[:, None] / (4 * feature_cols)
-        scale = scale_of(inputs[i])
-        d_in = scale * weighted - own_in * (scale * scale * scale * inner)
-        resid_own = lax.dynamic_slice_in_dim(d_resid[i], tp_index * feature_cols, feature_cols, 1)
-        x_parts.append((resid_own + d_in).astype(BF16))
-        in_sums.append(jnp.sum(u * own_in * scale, axis=0))
-    grad_qkv = contract(
-        jnp.concatenate(d_qkv16, axis=0), n16, 0, 0
-    ).astype(BF16)
-    grad_query = grad_qkv[:head_dim]
-    kv_blocks = grad_qkv[head_dim:].reshape(4, head_dim // 2, -1)
-    kv = [lax.dynamic_index_in_dim(kv_blocks, tp_index ^ j, keepdims=False) for j in range(4)]
-    near = lax.ppermute(jnp.stack([kv[1], kv[3]]), "tp", XOR1)
-    mine, theirs = add16(kv[0], near[0]), add16(kv[2], near[1])
-    grad_kv = add16(mine, lax.ppermute(theirs, "tp", XOR2))
-    grads = [grad_down, grad_gate, grad_up, grad_out, grad_query, grad_kv]
-    sizes = [grad.shape[0] for grad in grads]
-    spare = -sum(sizes) % 192
-    grads.append(jnp.zeros((spare, grad_down.shape[1]), BF16))
-    sums = grid_sum(jnp.concatenate(grads, axis=0))
-    ends = [sum(sizes[: j + 1]) for j in range(6)]
+    gain_col = lax.dynamic_slice_in_dim(g_in, tp_index * feature_cols, feature_cols)
+    sums, xg_t, gain_rows, gain_cols = backward(
+        real_length, tokens.T,
+        (x16, cot16, n16, q16, kv16, far_kv, att16, attn16, mid16, hid16, dffn16, dg16, du16),
+        gain_sum, weights[:-1], gains, head_gains, gain_col[:, None], (cosines, sines),
+    )
+    hidden = w_down.shape[0]
+    ends = [hidden, 2 * hidden, 3 * hidden, 3 * hidden + head_dim, 3 * hidden + 2 * head_dim]
     down_sum, gate_sum, up_sum, out_sum, query_sum, mine = [
-        sums[end - size : end] for size, end in zip(sizes, ends)
+        sums[start:end] for start, end in zip([0] + ends, ends + [ends[-1] + head_dim // 2])
     ]
     far = lax.ppermute(mine, "tp", XOR2)
     near = lax.ppermute(jnp.stack([mine, far]), "tp", XOR1)
@@ -1130,22 +1476,9 @@
     kv_sum = jnp.concatenate(
         [lax.select_n(tp_index ^ j, *kv_all) for j in range(4)], axis=0
     ).astype(F32).T
-
-    in_full = lax.dynamic_update_slice_in_dim(
-        jnp.zeros((width,), F32), in_sums[0] + in_sums[1], tp_index * feature_cols, 0
-    )
-    shared = [0.25 * (pair[0] + pair[1]) for pair in (pa_sums, pf_sums, gain_sums)]
-    small = sum_all(
-        jnp.concatenate([in_full, *shared, q_sums[0] + q_sums[1], k_sums[0] + k_sums[1]]).reshape(
-            -1, 128
-        )
-    ).reshape(-1)
-    gains = [small[j * width : (j + 1) * width] for j in range(4)]
-    gain_q_sum = small[4 * width : 4 * width + head_dim]
-    gain_k_sum = small[4 * width + head_dim :]
     return (
         out_t.T,
-        join(*x_parts, ctx_index),
+        xg_t.T,
         query_sum.astype(F32).T,
         kv_sum[:, :head_dim],
         kv_sum[:, head_dim:],
@@ -1153,12 +1486,12 @@
         gate_sum.astype(F32).T,
         up_sum.astype(F32).T,
         down_sum.astype(F32),
-        gains[0],
-        gains[1],
-        gains[2],
-        gains[3],
-        gain_q_sum,
-        gain_k_sum,
+        gain_cols[:, 0],
+        gain_rows[0],
+        gain_rows[1],
+        gain_rows[2],
+        gain_rows[3, :head_dim],
+        gain_rows[3, head_dim : 2 * head_dim],
     )
 
 

time: 600 us -> 461 us (0.77)
  matrix products: 59.6 us -> 0 us
  Pallas kernels: 372 us -> 416 us
  other arithmetic: 64.1 us -> 20.2 us
  waiting for transfers between devices: 35.8 us -> 0.01 us
  local copies, waits for them, and re-layouts: 43.3 us -> 16.8 us
  starting transfers between devices: 15.5 us -> 1.05 us
    dot_general x29 -> x0, matrix products: 59.6 us -> none  [the longest x27 58.8 us: contract(): lax.dot_general(left, right, (((left_dim,), (right_dim,)), ((), ())), pre...]
    pallas_call x1, Pallas kernels: 257 us -> 300 us  [backward(): pl.pallas_call(partial(backward_kernel, step_rows, steps, ring, gate_hidd...]
    ppermute x23 -> x0, waiting for transfers between devices: 35.8 us -> none  [the longest x2 17.3 us: tp_sum(): own = add16(own, lax.ppermute(own, 'tp', XOR2))]
    unnamed x173 -> x15, local copies, waits for them, and re-layouts: 27.9 us -> 5.81 us
    reduce_sum x11 -> x0, other arithmetic: 17.4 us -> none  [the longest x4 11.6 us: rms_back(): return (back, jnp.sum(cotangent * values * scale, axis=0))]
    ppermute x23 -> x0, starting transfers between devices: 13.8 us -> none  [the longest x5 3.89 us: sum_all(): values = values + lax.ppermute(values, axis, pairs)]
    convert_element_type x12 -> x0, other arithmetic: 10.6 us -> none  [the longest x5 7.39 us: add16(): return (left.astype(F32) + right.astype(F32)).astype(BF16)]
  transfers between devices with their start and end apart: 25 -> 2, of which waited for: 10 -> 0; matrix products, arithmetic and copies ran while one was open for 19% -> 4% of each run, Pallas kernels for 43% -> 0%
where the time goes in v4:
time: 461 us; the launch traced here: 455 us
  Pallas kernels  416 us (90%)
  other arithmetic  20.2 us (4%)
  local copies, waits for them, and re-layouts  16.8 us (4%)
    pallas_call x1, Pallas kernels, backward(): pl.pallas_call(partial(backward_kernel, step_rows, steps, ring, gate_hidd...  300 us
    pallas_call x1, Pallas kernels, forward(): pl.pallas_call(forward_kernel, out_shape=(low(features, rows), low(rows,...  116 us
    convert_element_type x1, other arithmetic, paired_shards(): down_sum.astype(F32)  11.2 us
  transfers between devices with their start and end apart: 2, of which 0 were waited for; matrix products, arithmetic and copies ran while one was open for 4% of the time, Pallas kernels for 0%

profile of v4, /device:TPU:0, one launch (start us, length us, event | category | flops | bytes accessed | tf_op | source)
XLA Modules:
  0.0 455.2 jit_solution(15608197480798861340)
XLA Ops:
  0.7 0.7 reshape.41
  1.4 0.7 reshape.40
  2.1 0.7 reshape.39
  2.8 0.7 stack.46
  3.5 0.7 stack.55
  4.1 0.7 stack.54
  4.8 0.2 broadcast_multiply_fusion
  5.0 2.7 fusion.2
  7.7 0.8 dynamic_slice.7
  8.5 0.8 broadcast_in_dim.6.gain_col
  9.2 0.6 constant_dynamic-slice_fusion.real_length
  9.8 0.6 maximum_convert_fusion.head_gains
  10.4 0.6 pad_maximum_fusion.2.gains
  11.0 116.0 %forward.1 = (bf16[288,1024]{1,0:T(8,128)(2,1)}, bf16[1024,1152]{1,0:T(8,128)(2,1)}, bf16[1024,1152]{1,0:T(8,128)(2,1)}, bf16[1024,1152]{1,0:T(8,128)(2,1)}, f32...) custom-call(s32[1,1]{1,0:T(1,128)} %constant_dynamic-slice_fusion.re, ...), custom_call_target="tpu_custom_call" | custom-call | tf_op jit(solution)/shard_map/forward/pallas_call | solution.py:706
  127.1 299.9 %backward.1 = (bf16[5952,1152]{1,0:T(8,128)(2,1)}, bf16[288,1024]{1,0:T(8,128)(2,1)}, f32[8,1152]{1,0:T(8,128)}, f32[1152,128]{1,0:T(8,128)}) custom-call(s32[1,1]{1,0:T(1,128)} %constant_dynamic-slice_fusion.real_length, bf16[288,1024]{1,0:T(8,128)(2,1)} %bitcast.45, bf16[1024,1152]{1,0:T(8,128)(2,1)} %get-tuple-element.35.x_in, ...), custom_call_target="tpu_custom_call" | custom-call | tf_op jit(solution)/shard_map/backward/pallas_call | solution.py:1387
  427.0 1.0 slice_bitcast_fusion.2
  428.0 1.0 collective-permute-start
  429.0 11.2 %slice_convert_fusion = (f32[1728,1152]{1,0:T(8,128)}, f32[1152,1728]{0,1:T(8,128)}, f32[1152,1728]{0,1:T(8,128)}) fusion(bf16[5952,1152]{1,0:T(8,128)(2,1)} %get-tuple-element.50), kind=kLoop, calls=%fused_computation.2 | loop fusion | flops 5971968 | bytes 35831808 | tf_op jit(solution)/shard_map/convert_element_type | solution.py:1488
  440.3 0.1 collective-permute-start.1
  440.3 2.5 slice_convert_fusion.1
  442.8 1.4 copy.35
  444.2 1.5 slice_reduce_fusion.1
  445.7 0.8 slice_reduce_fusion
  446.6 1.3 fusion.4
  447.8 1.0 select_select_fusion.2
  448.9 1.1 select_select_fusion.3
  450.0 0.2 convert_bitcast_fusion.2
  450.2 0.2 fusion.3
  450.4 1.4 copy.36
  451.7 1.4 copy.37
  453.1 0.8 copy.40
  454.0 0.8 copy.41
  (15 shorter events, 0.1 us)
Async XLA Ops:
  0.6 8.6 %copy-start = (s32[1,2]{1,0:T(1,128)S(1)}, s32[1,2]{1,0:T(1,128)}, u32[]{:S(2)}) copy-start(s32[1,2]{1,0:T(1,128)} %param.32) | copy-start | bytes 28
  428.0 12.2 %collective-permute-start = (bf16[128,1152]{1,0:T(8,128)(2,1)S(1)}, bf16[128,1152]{1,0:T(8,128)(2,1)S(1)}, u32[]{:S(2)}, u32[]{:S(2)}) collective-permute-start(bf16[128,1152]{1,0:T(8,128)(2,1)S(1)} %get-tuple-element.95), channel_id=1, source_target_pairs={{0,2},{2,0},{1,3},{3,1},{4,6},{6,4},{5,7},{7,5},{8,10},{10,8},{9,1... | collective-permute-start | bytes 884744 | tf_op jit(solution)/shard_map/ppermute | solution.py:1473
  440.3 5.5 %copy-start.4 = (f32[1152,128]{1,0:T(8,128)S(1)}, f32[1152,128]{1,0:T(8,128)}, u32[]{:S(2)}) copy-start(f32[1152,128]{1,0:T(8,128)} %get-tuple-element.51) | copy-start | bytes 1769476
  440.3 7.6 %collective-permute-start.1 = (bf16[2,128,1152]{2,1,0:T(8,128)(2,1)S(1)}, bf16[2,128,1152]{2,1,0:T(8,128)(2,1)S(1)}, u32[]{:S(2)}, u32[]{:S(2)}) collective-permute-start(bf16[2,128,1152]{2,1,0:T(8,128)(2,1)S(1)} %pad_maximum_fusion), channel_id=1, source_target_pairs={{0,1},{1,0},{2,3},{3,2},{4,5},{5,4},{6,7},{7,6},{8,9},{9,8},{10,11... | collective-permute-start | bytes 1769480 | tf_op jit(solution)/shard_map/ppermute | solution.py:1474
  450.4 2.8 copy-start.2
  451.7 2.2 copy-start.3
  451.7 3.0 copy-start.1

commit v5 on v4

--- a/solution.py
+++ b/solution.py
@@ -3,6 +3,7 @@
 
 import jax
 import jax.numpy as jnp
+import numpy as np
 from jax import lax
 from jax.experimental import pallas as pl
 from jax.experimental.pallas import tpu as pltpu
@@ -378,15 +379,40 @@
     return (left.astype(F32) + right.astype(F32)).astype(BF16)
 
 
+def block_tables(length, head_dim):
+    freq_index = np.arange(head_dim // 2, dtype=np.float32)
+    inverse = np.float32(ROPE_BASE) ** (np.float32(-2.0) * freq_index / np.float32(head_dim))
+    angles = np.arange(length, dtype=np.float32)[:, None] * inverse.astype(np.float32)[None, :]
+    angles = angles.astype(np.float64)
+    return np.cos(angles).astype(np.float32), np.sin(angles).astype(np.float32)
+
+
 def scale_of(values):
     return lax.rsqrt(jnp.mean(values * values, axis=-1, keepdims=True) + EPSILON)
 
 
-def row_blocks(rows, size, body, carry=None):
+STORED = 13
+
+
+def row_blocks(base, rows, size, body, carry=None):
     def step(i, state):
-        return body(pl.ds(pl.multiple_of(i * size, size), size), state)
+        at = pl.ds(pl.multiple_of(base + i * size, size), size)
+        return body(at, pl.ds(pl.multiple_of(i * size, size), size), state)
 
     return lax.fori_loop(0, rows // size, step, carry)
+
+
+def spread_gains(packed, gains, head_gains):
+    columns = gains.shape[1] // 128
+    for j in range(4):
+        for i in range(columns):
+            at = j * columns + i
+            gains[j : j + 1, 128 * i : 128 * i + 128] = packed[at : at + 1, :]
+    head_columns = head_gains.shape[1] // 128
+    for j in range(2):
+        for i in range(head_columns):
+            at = 4 * columns + j * head_columns + i
+            head_gains[j : j + 1, 128 * i : 128 * i + 128] = packed[at : at + 1, :]
 
 
 def turn_in(source, target, rows):
@@ -415,12 +441,14 @@
 
 
 def forward_kernel(
-    real_length, tok, cot, w_q, w_k, w_v, w_o, w_g, w_u, w_d, gains, head_gains, cosines, sines,
-    out_t, x16, cot16, n16, raw, q16, kv16, far_kv, att16, attn16, mid16, hid16, dffn16, dg16, du16,
-    gain_sum,
-    blocks, v_qkv, v_o, v_g, v_u, v_d, part, near, far, ffn16,
-    load_sem, own_sem, g_send, g_recv, kv_send, kv_recv, s_send, s_recv,
+    real_lengths, tok, cot, w_q, w_k, w_v, w_o, w_g, w_u, w_d, packed, cosines, sines,
+    out_t, gain_sum, *refs,
 ):
+    stored, refs = refs[:STORED], refs[STORED:]
+    kept, refs = refs[:STORED], refs[STORED:]
+    x16, cot16, n16, q16, kv16, far_kv, att16, attn16, mid16, hid16, dffn16, dg16, du16 = kept
+    blocks, v_qkv, v_o, v_g, v_u, v_d, part, near, far, ffn16, gains, head_gains = refs[:12]
+    load_sem, own_sem, store_sem, g_send, g_recv, kv_send, kv_recv, s_send, s_recv = refs[12:]
     dp, ctx, tp = lax.axis_index("dp"), lax.axis_index("ctx"), lax.axis_index("tp")
     core_peer = (dp, ctx, tp + 1 - 2 * (tp % 2))
     x_index = (tp + 2) % 4
@@ -486,6 +514,12 @@
     to_x[0].start()
     to_x[1].start()
 
+    spread_gains(packed, gains, head_gains)
+
+    def store(j, c):
+        at = slice(None) if c is None else chunk(c)
+        return pltpu.make_async_copy(kept[j].at[at], stored[j].at[at], store_sem.at[j, c or 0])
+
     def pass_on(j):
         to_x[j].wait_recv()
         onward[j].start()
@@ -501,17 +535,15 @@
     def project(c):
         turn_in(blocks.at[c], x16, chunk(c))
 
-        def norm(block, _):
-            at = pl.ds(c * rows + block.start, block.size)
+        def norm(at, _, carry):
             values = x16[at, :].astype(F32)
             n16[at, :] = (values * scale_of(values) * gains[0:1, :]).astype(BF16)
 
-        row_blocks(rows, 32, norm)
+        row_blocks(c * rows, rows, 64, norm)
         for first in range(0, rows, half):
             at = pl.ds(c * rows + first, half)
             tables = pl.ds(c * rows + first, half)
             values = dot_nn(n16[at, :], v_qkv[...])
-            raw[at, :] = values[:, : 2 * head_dim]
             cosine, sine = cosines[tables, :], sines[tables, :]
             for j, target in ((0, q16.at[at, :]), (1, kv16.at[at, 0:head_dim])):
                 head = values[:, j * head_dim : (j + 1) * head_dim]
@@ -531,7 +563,7 @@
             key_id = lax.broadcasted_iota(jnp.int32, (half, rows), 1)
             allowed = key_id <= row_id
             if c == 1:
-                allowed = allowed & (rows + key_id < real_length[0, 0])
+                allowed = allowed & (rows + key_id < real_lengths[0, 1 - ctx])
             keys = [(kv16[chunk(c), :head_dim], kv16[chunk(c), head_dim:], allowed)]
             if c == 1:
                 keys.append((far_kv[:, :head_dim], far_kv[:, head_dim:], None))
@@ -582,12 +614,11 @@
         return x16[at, :].astype(F32) + branch * scale_of(branch) * gains[1:2, :]
 
     def middle(c):
-        def body(block, _):
-            at = pl.ds(c * rows + block.start, block.size)
+        def body(at, _, carry):
             values = residual(at)
             mid16[at, :] = (values * scale_of(values) * gains[2:3, :]).astype(BF16)
 
-        row_blocks(rows, 32, body)
+        row_blocks(c * rows, rows, 64, body)
 
     def feed(c):
         for first, size in column_tiles(hidden, 256):
@@ -609,8 +640,7 @@
         sum_copies(c, attn16)[0].wait_send()
         onward[c].wait_send()
 
-        def body(block, total):
-            at = pl.ds(c * rows + block.start, block.size)
+        def body(at, block, total):
             branch = ffn16[at, :].astype(F32)
             scale = scale_of(branch)
             unit = branch * scale
@@ -621,7 +651,7 @@
             dffn16[at, :] = (scale * (weighted - unit * inner)).astype(BF16)
             return total + (grad * unit).reshape(-1, 8, width).sum(axis=0)
 
-        total = row_blocks(rows, 32, body, jnp.zeros((8, width), F32))
+        total = row_blocks(c * rows, rows, 64, body, jnp.zeros((8, width), F32))
         if c == 0:
             gain_sum[...] = total
         else:
@@ -642,12 +672,21 @@
                 du16[at, cols] = (d_hidden * du16[at, cols].astype(F32)).astype(BF16)
 
     kv_copy = remote(kv16.at[chunk(0)], far_kv, kv_send.at[0], kv_recv.at[0], y_peer)
+    X, COT, N, Q, KV, FAR, ATT, ATTN, MID, HID, DFFN, DG, DU = range(STORED)
+    started = []
+
+    def store_all(c, *which):
+        for j in which:
+            store(j, c).start()
+            started.append((j, c))
+
     pass_on(0)
     for copy in loads[:3]:
         copy.wait()
     gathered(0)
     project(0)
     kv_copy.start()
+    store_all(0, X, N, Q, KV)
     pass_on(1)
     to_x[2].start()
     to_x[3].start()
@@ -656,10 +695,14 @@
     sum_start(0, attn16)
     gathered(1)
     project(1)
+    store_all(1, X, N, Q, KV)
     sum_cross(0, attn16)
     kv_copy.wait_recv()
     attend_rows(1)
     sum_start(1, attn16)
+    store_all(None, FAR)
+    store_all(0, ATT)
+    store_all(1, ATT)
     pass_on(2)
     pass_on(3)
     sum_cross(1, attn16)
@@ -667,31 +710,41 @@
     for copy in loads[4:]:
         copy.wait()
     middle(0)
+    store_all(0, ATTN, MID)
     feed(0)
     sum_start(2, ffn16)
+    store_all(0, HID)
     sum_back(1, attn16)
     middle(1)
+    store_all(1, ATTN, MID)
     sum_cross(2, ffn16)
     feed(1)
     sum_start(3, ffn16)
+    store_all(1, HID)
     gathered(2)
     gathered(3)
     sum_back(2, ffn16)
     sum_cross(3, ffn16)
     finish(0)
+    store_all(0, COT, DFFN)
     feed_back(0)
+    store_all(0, DG, DU)
     sum_back(3, ffn16)
     finish(1)
+    store_all(1, COT, DFFN)
     feed_back(1)
+    store_all(1, DG, DU)
     for group in (to_x, to_core, onward[2:], [kv_copy]):
         for copy in group:
             copy.wait_send()
     for s, target in ((0, attn16), (1, attn16), (2, ffn16), (3, ffn16)):
         for copy in sum_copies(s, target)[1 if s < 2 else 0 :]:
             copy.wait_send()
-
-
-def forward(real_length, tok_t, cot_t, weights, gains, head_gains, cosines, sines):
+    for j, c in started:
+        store(j, c).wait()
+
+
+def forward(real_lengths, tok_t, cot_t, weights, packed, tables):
     features, rows = tok_t.shape
     half = rows // 2
     width = 4 * features
@@ -699,22 +752,22 @@
     head_dim = weights[1].shape[1]
     whole = pl.BlockSpec(memory_space=pltpu.VMEM)
     there = pl.BlockSpec(memory_space=pl.ANY)
-
-    def low(*shape):
-        return jax.ShapeDtypeStruct(shape, BF16)
+    kept = [
+        (rows, width), (rows, width), (rows, width), (rows, head_dim), (rows, 2 * head_dim),
+        (half, 2 * head_dim), (rows, head_dim), (rows, width), (rows, width), (rows, hidden),
+        (rows, width), (rows, hidden), (rows, hidden),
+    ]
 
     return pl.pallas_call(
         forward_kernel,
         out_shape=(
-            low(features, rows), low(rows, width), low(rows, width), low(rows, width),
-            jax.ShapeDtypeStruct((rows, 2 * head_dim), F32), low(rows, head_dim),
-            low(rows, 2 * head_dim), low(half, 2 * head_dim), low(rows, head_dim),
-            low(rows, width), low(rows, width), low(rows, hidden), low(rows, width),
-            low(rows, hidden), low(rows, hidden), jax.ShapeDtypeStruct((8, width), F32),
+            jax.ShapeDtypeStruct((features, rows), BF16), jax.ShapeDtypeStruct((8, width), F32),
+            *[jax.ShapeDtypeStruct(shape, BF16) for shape in kept],
         ),
-        in_specs=[pl.BlockSpec(memory_space=pltpu.SMEM)] + [there] * 9 + [whole] * 4,
-        out_specs=[whole] * 16,
-        scratch_shapes=[
+        in_specs=[pl.BlockSpec(memory_space=pltpu.SMEM)] + [there] * 9 + [whole] * 3,
+        out_specs=[whole] * 2 + [there] * STORED,
+        scratch_shapes=[pltpu.VMEM(shape, BF16) for shape in kept]
+        + [
             pltpu.VMEM((4, width, half), BF16),
             pltpu.VMEM((width, 3 * head_dim), BF16),
             pltpu.VMEM((head_dim, width), BF16),
@@ -725,8 +778,11 @@
             pltpu.VMEM((4, half // 2, width), BF16),
             pltpu.VMEM((4, half // 2, width), BF16),
             pltpu.VMEM((rows, width), BF16),
+            pltpu.VMEM((4, width), F32),
+            pltpu.VMEM((2, head_dim), F32),
             pltpu.SemaphoreType.DMA((7,)),
             pltpu.SemaphoreType.DMA((4,)),
+            pltpu.SemaphoreType.DMA((STORED, 2)),
             pltpu.SemaphoreType.DMA((3, 4)),
             pltpu.SemaphoreType.DMA((3, 4)),
             pltpu.SemaphoreType.DMA((1,)),
@@ -738,23 +794,22 @@
         compiler_params=pltpu.CompilerParams(
             collective_id=2, has_side_effects=True, vmem_limit_bytes=63 << 20
         ),
-    )(real_length, tok_t, cot_t, *weights, gains, head_gains, cosines, sines)
+    )(real_lengths, tok_t, cot_t, *weights, packed, *tables)
 
 
 def backward_kernel(
-    step_rows, steps, ring, gate_hidden,
-    real_length, tok, x_in, cot_in, n_in, q_in, kv_in, far_in, att_in, attn_in, mid_in, hid_in,
-    dffn_in, dg_in, du_in, gain_ffn, w_q, w_k, w_v, w_o, w_g, w_u, gains, head_gains, gain_col,
-    cosines, sines,
+    step_rows, steps, steps_low, lag, ring, gate_hidden,
+    real_lengths, tok, x_in, cot_in, n_in, q_in, kv_in, far_in, att_in, attn_in, mid_in, hid_in,
+    dffn_in, dg_in, du_in, gain_ffn, w_q, w_k, w_v, w_o, w_g, w_u, packed, cosines, sines,
     out, xg_t, gain_rows, gain_cols,
-    g, y2, z2, m2, z1, m1, y1, hid, dg, du, mid, dffn, w_tiles, acc, part, near, far, dm, cot, attn,
+    g, y2, z2, m2, z1, m1, y1, hid, dg, du, mid, dffn, w_tiles, part, near, far, dm, cot, attn,
     v_o, v_qkv, dkv_new, norm_near, norm_far, row_part,
     row_near, kv_near, kv_far, turned, head_sums, row_sums, sum_slots, sum_new, col_slots,
-    col_new,
+    col_new, gains, head_gains, gain_col,
     load_sem, tile_sem, keep_sem, chain_send, chain_recv, peer_send, peer_recv,
 ):
     dp, ctx, tp = lax.axis_index("dp"), lax.axis_index("ctx"), lax.axis_index("tp")
-    s, K = step_rows, steps
+    s, K, low_steps = step_rows, steps, steps_low
     upper = dp // 2
     odd = tp % 2
     outer = (dp == 0) | (dp == 3)
@@ -935,23 +990,35 @@
         c_fy(k).wait_recv()
         c_y2(k).wait_send()
 
-    def f_outer(k):
-        c_z2(k).wait_send()
+    def f2_outer(k):
         c_fy_outer(k).wait_send()
+
+    def f1_outer(k):
         c_fa(k).wait_recv()
         c_fb(k).wait_recv()
         c_z1(k).wait_send()
 
-    def f_inner(k):
+    def f2_inner(k):
         keep2(k).wait()
+        c_fo(k).wait_send()
+        c_fy(k).wait_send()
+
+    def f1_inner(k):
         keep1(k).wait()
-        for copy in (c_m2, c_fo, c_fy, c_m1, c_y1, c_fm, c_fa, c_fb):
+        for copy in (c_fm, c_fa, c_fb):
             copy(k).wait_send()
 
     hops = (
-        (5, yes, f2), (5, outer, f_outer), (5, inner, f_inner), (4, outer, e2), (4, inner, e1),
-        (3, inner, d2), (3, inner, d1), (2, inner, c2), (2, inner, c1), (1, yes, b2), (1, inner, b1),
-        (0, yes, lambda k: c_y2(k).start()), (0, outer, lambda k: c_z1(k).start()),
+        (5, yes, K, f2), (5, outer, K, f2_outer), (5, outer, low_steps, f1_outer),
+        (5, inner, K, f2_inner), (5, inner, low_steps, f1_inner),
+        (4, inner, K, lambda k: c_m2(k).wait_send()),
+        (4, inner, low_steps, lambda k: c_y1(k).wait_send()),
+        (3, outer, K, lambda k: c_z2(k).wait_send()),
+        (3, inner, low_steps, lambda k: c_m1(k).wait_send()),
+        (4, outer, K, e2),
+        (4, inner, low_steps, e1), (3, inner, K, d2), (3, inner, low_steps, d1), (2, inner, K, c2),
+        (2, inner, low_steps, c1), (1, yes, K, b2), (1, inner, low_steps, b1),
+        (0, yes, K, lambda k: c_y2(k).start()), (0, outer, low_steps, lambda k: c_z1(k).start()),
     )
 
     def grad_tile(index, first, size):
@@ -966,36 +1033,31 @@
     full = hidden // 256
     tail = hidden - 256 * full
 
-    def mid_part(c):
-        tiles = column_tiles(hidden, 256)
-
-        def fetch(j):
-            first, size = tiles[j]
-            return [
-                pltpu.make_async_copy(
-                    w.at[pl.ds(first, size)], w_tiles.at[i, j % 2, pl.ds(0, size)],
-                    tile_sem.at[i, j % 2],
-                )
-                for i, w in enumerate((w_g, w_u))
-            ]
-
-        for copy in fetch(0):
-            copy.start()
-        for j, (first, size) in enumerate(tiles):
-            if j + 1 < len(tiles):
+    mid_tiles = column_tiles(width, 256)
+
+    def fetch(j):
+        first, size = mid_tiles[j % len(mid_tiles)]
+        return [
+            pltpu.make_async_copy(
+                w.at[:, pl.ds(first, size)], w_tiles.at[i, j % 2, :, pl.ds(0, size)],
+                tile_sem.at[i, j % 2],
+            )
+            for i, w in enumerate((w_g, w_u))
+        ]
+
+    def mid_part(c, low, high):
+        base = (1 - c) * len(mid_tiles)
+        for j in range(base + low, base + high):
+            first, size = mid_tiles[j - base]
+            if j + 1 < 2 * len(mid_tiles):
                 for copy in fetch(j + 1):
                     copy.start()
             for copy in fetch(j):
                 copy.wait()
-            cols = pl.ds(first, size)
-            term = dot_nn(dg[chunk(c), cols], w_tiles[0, j % 2, 0:size, :]) + dot_nn(
-                du[chunk(c), cols], w_tiles[1, j % 2, 0:size, :]
+            term = dot_nn(dg[chunk(c), :], w_tiles[0, j % 2, :, 0:size]) + dot_nn(
+                du[chunk(c), :], w_tiles[1, j % 2, :, 0:size]
             )
-            if j == 0:
-                acc[...] = term
-            else:
-                acc[...] += term
-        part[c] = acc[...].astype(BF16)
+            part[c, :, pl.ds(first, size)] = term.astype(BF16)
 
     def own_half(index):
         return multiple(index * half, half)
@@ -1011,8 +1073,10 @@
             peer_copy(3 * c + 2, final, final, core_peer),
         )
 
+    mid_split = (len(mid_tiles) + 1) // 2
+
     def sum_begin(c):
-        mid_part(c)
+        mid_part(c, mid_split, len(mid_tiles))
         sum_copies(c)[0].start()
 
     def sum_cross(c):
@@ -1027,11 +1091,11 @@
         dm[multiple(c * rows + odd * half, half), :] = add16(near[c], far[c])
         copies[2].start()
 
-    def norms_back(c):
-        sum_copies(c)[2].wait_recv()
-
-        def body(block, state):
-            at = pl.ds(c * rows + block.start, block.size)
+    def norms_back(c, second):
+        if not second:
+            sum_copies(c)[2].wait_recv()
+
+        def body(at, _, state):
             branch = attn[at, :].astype(F32)
             scale_a = scale_of(branch)
             unit_a = branch * scale_a
@@ -1052,8 +1116,8 @@
             )
 
         zero = jnp.zeros((8, width), F32)
-        sum_a, sum_r = row_blocks(rows, 16, body, (zero, zero))
-        if c == 1:
+        sum_a, sum_r = row_blocks(c * rows + second * half, half, 64, body, (zero, zero))
+        if c == 1 and not second:
             row_sums[0], row_sums[1] = sum_a, sum_r
         else:
             row_sums[0] += sum_a
@@ -1072,9 +1136,9 @@
         dqkv[at, cols] = (scale * (weighted - unit * mean)).astype(BF16)
         head_sums[j] += (grad * unit).reshape(-1, 8, head_dim).sum(axis=0)
 
-    def attend_back_rows(c):
+    def attend_back_rows(c, second):
         d_keys, d_values = [0.0, 0.0], [0.0, 0.0]
-        for first in range(0, rows, half):
+        for first in (second * half,):
             at = pl.ds(c * rows + first, half)
             query = q16[at, :]
             d_out = dot_nt(attn[at, :], v_o[...]).astype(BF16)
@@ -1082,7 +1146,7 @@
             key_id = lax.broadcasted_iota(jnp.int32, (half, rows), 1)
             allowed = key_id <= row_id
             if c == 1:
-                allowed = allowed & (rows + key_id < real_length[0, 0])
+                allowed = allowed & (rows + key_id < real_lengths[0, 1 - ctx])
             keys = [(kv16[chunk(c), :head_dim], kv16[chunk(c), head_dim:], allowed)]
             if c == 1:
                 keys.append((far_kv[:, :head_dim], far_kv[:, head_dim:], None))
@@ -1105,24 +1169,48 @@
                 d_keys[i] += contract(d_score, query, 0, 0)
                 d_values[i] += contract(probs[i].astype(BF16), d_out, 0, 0)
             head_back(d_query * score_scale, at, 0)
-        dkv[chunk(c), :head_dim] = (d_keys[0] * score_scale).astype(BF16)
-        dkv[chunk(c), head_dim:] = d_values[0].astype(BF16)
-        if c == 1:
-            dkv_far[:, :head_dim] = (d_keys[1] * score_scale).astype(BF16)
-            dkv_far[:, head_dim:] = d_values[1].astype(BF16)
-            far_copy().start()
-
-    def far_copy():
-        return peer_copy(6, dkv_far, dkv_new, y_peer)
+        places = [dkv.at[chunk(c), :]] + [dkv_far] * c
+        for i, place in enumerate(places):
+            for cols, term in (
+                (pl.ds(0, head_dim), d_keys[i] * score_scale),
+                (pl.ds(head_dim, head_dim), d_values[i]),
+            ):
+                if second:
+                    term = term + place[:, cols].astype(F32)
+                place[:, cols] = term.astype(BF16)
+        if c == 1 and second:
+            far_copies()[0].start()
+
+    quarter = half // 2
+    far_rows = multiple(odd * half + tp // 2 * quarter, quarter)
+
+    def far_copies():
+        given = dkv_far.at[multiple(odd * half + (1 - tp // 2) * quarter, quarter), :]
+        return (
+            peer_copy(33, dkv_far.at[own_half(1 - odd), :], dkv_new.at[0:half], core_peer),
+            peer_copy(34, given, dkv_new.at[half : half + quarter], x_peer),
+            peer_copy(6, dkv_far.at[far_rows, :], dkv_new.at[half + quarter : 2 * half], y_peer),
+        )
+
+    def far_cross():
+        copies = far_copies()
+        copies[0].wait_recv()
+        dkv_far[own_half(odd), :] = add16(dkv_far[own_half(odd), :], dkv_new[0:half, :])
+        copies[1].start()
+
+    def far_up():
+        copies = far_copies()
+        copies[1].wait_recv()
+        dkv_far[far_rows, :] = add16(dkv_far[far_rows, :], dkv_new[half : half + quarter, :])
+        copies[2].start()
 
     def keys_back(c):
         if c == 0:
-            far_copy().wait_recv()
+            far_copies()[2].wait_recv()
+            dkv[far_rows, :] = add16(dkv[far_rows, :], dkv_new[half + quarter : 2 * half, :])
         for first in range(0, rows, half):
             at = pl.ds(c * rows + first, half)
             grad = dkv[at, :].astype(F32)
-            if c == 0:
-                grad = grad + dkv_new[pl.ds(first, half), :].astype(F32)
             head_back(grad[:, :head_dim], at, 1)
             dqkv[at, 2 * head_dim :] = grad[:, head_dim:].astype(BF16)
 
@@ -1194,9 +1282,13 @@
     at_query = at_out + head_dim
     at_kv = at_query + head_dim
 
-    def small_grads():
+    def out_grad():
         g[pl.ds(at_out, head_dim), :] = contract(att[...], attn[...], 0, 0).astype(BF16)
+
+    def query_grad():
         g[pl.ds(at_query, head_dim), :] = contract(dqkv[:, :head_dim], mid[...], 0, 0).astype(BF16)
+
+    def kv_grads():
         spare = g.shape[0] - at_kv - kv_rows
         g[pl.ds(at_kv + kv_rows, spare), :] = jnp.zeros((spare, width), BF16)
         sum_copies(1)[0].wait_send()
@@ -1280,13 +1372,15 @@
             peer_copy(32, theirs, theirs, core_peer),
         )
 
-    def load_late():
-        for j in range(len(late_pairs)):
+    def late(low, high):
+        for j in range(low, high):
             late_load(j).start()
 
-    def wait_late():
-        for j in range(len(late_pairs)):
+    def wait_late(low, high):
+        for j in range(low, high):
             late_load(j).wait()
+
+    def wait_rest():
         for j in range(5, count):
             load(j).wait()
         head_sums[...] = jnp.zeros(head_sums.shape, F32)
@@ -1297,83 +1391,100 @@
     grad_tile(0, 0, 256)
     load(2).wait()
     load(3).wait()
-    for j in range(gate_tiles, full):
-        grad_tile(1, 256 * j, 256)
-    if tail:
-        grad_tile(1, 256 * full, tail)
-    load(4).wait()
-
-    last_up = 1 + full
-    stages = (
-        (last_up + gate_tiles + 1, load_late),
+    grad_tile(1, 256 * gate_tiles, 256)
+    for copy in fetch(0):
+        copy.start()
+    spread_gains(packed, gains, head_gains)
+    for first in range(0, width, 128):
+        row = gains[0:1, first : first + 128]
+        gain_cols[first : first + 128, :] = jnp.broadcast_to(row, (128, 128)).T
+    gain_col[...] = gain_cols[multiple(tp * features, features), :]
+
+    first_up = full + 1
+    first_gate = first_up + full + 1
+    freed = first_gate + gate_tiles
+    stages = [
+        (0, load(4).wait),
+        (0, lambda: [grad_tile(1, 256 * j, 256) for j in range(gate_tiles + 1, full)]),
+        (1, lambda: mid_part(1, 0, mid_split)),
         (2, lambda: sum_begin(1)),
-        (3, lambda: sum_cross(1)),
+        (3, lambda: (sum_cross(1), mid_part(0, 0, mid_split))),
         (4, lambda: sum_begin(0)),
         (5, lambda: sum_cross(0)),
-        (6, lambda: sum_back(1)),
-        (8, lambda: sum_back(0)),
-        (last_up + gate_tiles + 2, wait_late),
-    )
-    first_back = last_up + gate_tiles + 2
-    stages += tuple(
-        (first_back + j, action)
-        for j, action in enumerate(
-            (
-                lambda: norms_back(1),
-                lambda: attend_back_rows(1),
-                lambda: norms_back(0),
-                lambda: (sum_copies(0)[2].wait_send(), load_tok().start(), attend_back_rows(0)),
-                lambda: keys_back(1),
-                lambda: scatter_begin(1),
-                lambda: keys_back(0),
-                lambda: (scatter_cross(1), scatter_begin(0)),
-                small_grads,
-                lambda: (scatter_cross(0), kv_cross()),
-                lambda: (load_tok().wait(), scatter_end(1)),
-                lambda: (scatter_end(0), kv_end()),
-                gains_begin,
-            )
-        )
-    )
-    at_gains = first_back + 13
-    stages += tuple((at_gains + j, partial(gains_hop, j)) for j in range(5))
+        (7, lambda: (late(0, 1), sum_back(1))),
+        (9, lambda: (wait_late(0, 1), wait_rest())),
+        (9, lambda: norms_back(1, 0)),
+        (10, lambda: norms_back(1, 1)),
+        (11, lambda: sum_back(0)),
+        (13, lambda: norms_back(0, 0)),
+        (14, lambda: norms_back(0, 1)),
+        (freed, lambda: late(1, len(late_pairs))),
+    ]
+    chain_stages = (
+        (1, lambda: wait_late(1, len(late_pairs))),
+        (1, lambda: attend_back_rows(1, 0)),
+        (2, lambda: attend_back_rows(1, 1)),
+        (3, lambda: (sum_copies(0)[2].wait_send(), load_tok().start())),
+        (3, lambda: attend_back_rows(0, 0)),
+        (4, lambda: attend_back_rows(0, 1)),
+        (5, lambda: (far_cross(), keys_back(1))),
+        (6, lambda: scatter_begin(1)),
+        (7, lambda: scatter_cross(1)),
+        (8, lambda: (far_up(), out_grad())),
+        (11, lambda: (load_tok().wait(), scatter_end(1))),
+        (14, lambda: keys_back(0)),
+        (15, lambda: scatter_begin(0)),
+        (16, query_grad),
+        (17, lambda: (scatter_cross(0), kv_grads())),
+        (18, kv_cross),
+        (20, lambda: scatter_end(0)),
+        (21, gains_begin),
+        (22, kv_end),
+    )
+    stages += [(freed + j, action) for j, action in chain_stages]
+    stages += [(freed + 23 + 2 * j, partial(gains_hop, j)) for j in range(5)]
 
     def body(t, carry):
-        pl.when(t < full - 1)(lambda: grad_tile(0, 256 * (t + 1), 256))
+        pl.when((t < full) & (t != 2))(
+            lambda: grad_tile(0, 256 * (t + 1 - jnp.minimum(t // 2, 1)), 256)
+        )
         if tail:
-            pl.when(t == full - 1)(lambda: grad_tile(0, 256 * full, tail))
-        pl.when((t >= 1) & (t < last_up))(lambda: grad_tile(2, 256 * (t - 1), 256))
-        if tail:
-            pl.when(t == last_up)(lambda: grad_tile(2, 256 * full, tail))
-        late = t - last_up - 1
-        pl.when((late >= 0) & (late < gate_tiles))(lambda: grad_tile(1, 256 * late, 256))
-        for lag, who, action in hops:
-            k = t - lag
-            pl.when(who & (k >= 0) & (k < K))(partial(action, k))
+            pl.when(t == 2)(lambda: grad_tile(1, 256 * full, tail))
+            pl.when(t == full)(lambda: grad_tile(0, 256 * full, tail))
+            pl.when(t == first_gate - 1)(lambda: grad_tile(2, 256 * full, tail))
+        up = t - first_up
+        pl.when((up >= 0) & (up < full))(lambda: grad_tile(2, 256 * up, 256))
+        gate = t - first_gate
+        pl.when((gate >= 0) & (gate < gate_tiles))(lambda: grad_tile(1, 256 * gate, 256))
+        for stage, who, limit, action in hops:
+            k = t - stage * lag
+            pl.when(who & (k >= 0) & (k < limit))(partial(action, k))
         for step, action in stages:
             pl.when(t == step)(lambda action=action: action() and None)
         return carry
 
-    lax.fori_loop(0, K + 5, body, 0)
+    lax.fori_loop(0, K + 5 * lag, body, 0)
     done = [sum_copies(0)[j] for j in (0, 1)] + [sum_copies(1)[j] for j in (1, 2)]
-    done += [far_copy(), *scatter_copies(0), *scatter_copies(1), *kv_copies()]
+    done += [*far_copies(), *scatter_copies(0), *scatter_copies(1), *kv_copies()]
     done += [sum_copy(j) for j in range(5)] + [col_copy(j) for j in range(3)]
     for copy in done + list(gather_copies()):
         copy.wait_send()
 
 
-def backward(real_length, tok_t, forward_outs, gain_ffn, weights, gains, head_gains, gain_col, tables):
+def backward(real_lengths, tok_t, forward_outs, gain_ffn, weights, packed, tables):
     features, rows = tok_t.shape
     half = rows // 2
     width = 4 * features
     w_q, w_k, w_v, w_o, w_g, w_u = weights
     hidden, head_dim = w_g.shape[0], w_k.shape[1]
     kv_rows = head_dim // 2
-    step_rows, ring = 48, 6
+    step_rows, lag = 32, 2
+    ring = 4 * lag + 1
     needed = 3 * hidden + 2 * head_dim + kv_rows
     steps = -(-needed // (4 * step_rows))
     total = 4 * step_rows * steps
     gate_hidden = total // 2 - hidden
+    steps_low = -(-(needed - total // 2) // (2 * step_rows))
     whole = pl.BlockSpec(memory_space=pltpu.VMEM)
     there = pl.BlockSpec(memory_space=pl.ANY)
 
@@ -1385,7 +1496,7 @@
 
     slots = [low(n * step_rows * ring, width) for n in (1, 1, 1, 2, 1, 1)]
     return pl.pallas_call(
-        partial(backward_kernel, step_rows, steps, ring, gate_hidden),
+        partial(backward_kernel, step_rows, steps, steps_low, lag, ring, gate_hidden),
         out_shape=(
             jax.ShapeDtypeStruct((total, width), BF16),
             jax.ShapeDtypeStruct((features, rows), BF16),
@@ -1393,28 +1504,29 @@
             jax.ShapeDtypeStruct((width, 128), F32),
         ),
         in_specs=[pl.BlockSpec(memory_space=pltpu.SMEM)] + [there] * 14 + [whole] + [there] * 6
-        + [whole] * 5,
+        + [whole] * 3,
         out_specs=[there, whole, whole, whole],
         scratch_shapes=[
             low(total, width), *slots,
             low(rows, hidden), low(rows, hidden), low(rows, hidden), low(rows, width),
-            low(rows, width), low(2, 2, 256, width), high(half, width), low(2, half, width),
+            low(rows, width), low(2, 2, hidden, 256), low(2, half, width),
             low(2, half // 2, width), low(2, half // 2, width), low(rows, width), low(rows, width),
             low(rows, width), low(head_dim, width), low(width, 3 * head_dim),
             low(half, 2 * head_dim), low(2, 2, features, half), low(2, features, half),
             high(2, 2, 8, half), high(2, 2, 8, half), low(2, kv_rows, width), low(kv_rows, width),
             low(width, half), high(2, 8, head_dim), high(2, 8, width),
             high(5, 8, width), high(5, 8, width), high(3, features, 128), high(3, features, 128),
+            high(4, width), high(2, head_dim), high(features, 128),
             pltpu.SemaphoreType.DMA((20,)), pltpu.SemaphoreType.DMA((2, 2)),
             pltpu.SemaphoreType.DMA((2, steps)), pltpu.SemaphoreType.DMA((11, steps)),
-            pltpu.SemaphoreType.DMA((11, steps)), pltpu.SemaphoreType.DMA((33,)),
-            pltpu.SemaphoreType.DMA((33,)),
+            pltpu.SemaphoreType.DMA((11, steps)), pltpu.SemaphoreType.DMA((35,)),
+            pltpu.SemaphoreType.DMA((35,)),
         ],
         name="backward",
         compiler_params=pltpu.CompilerParams(
             collective_id=1, has_side_effects=True, vmem_limit_bytes=63 << 20
         ),
-    )(real_length, tok_t, *forward_outs, gain_ffn, *weights, gains, head_gains, gain_col, *tables)
+    )(real_lengths, tok_t, *forward_outs, gain_ffn, *weights, packed, *tables)
 
 
 def paired_shards(
@@ -1436,34 +1548,20 @@
     bucket_lengths,
     true_lengths,
 ):
-    ctx_index, tp_index = lax.axis_index("ctx"), lax.axis_index("tp")
+    tp_index = lax.axis_index("tp")
     rows = tokens.shape[0] // 2
-    feature_cols = tokens.shape[1]
     head_dim = w_key.shape[1]
     score_scale = head_dim ** (-0.5)
-    g_in, g_pa, g_pf, g_pff, g_q, g_k = [
-        gain.astype(F32)
-        for gain in (gain_in, gain_post_attn, gain_pre_ffn, gain_post_ffn, gain_query, gain_key)
-    ]
-    width = 4 * feature_cols
-    seq_pos = jnp.arange(2 * rows, dtype=jnp.int32)
-    cosines, sines = [table[:, : head_dim // 2] for table in rope_tables(seq_pos, head_dim)]
-    real_length = lax.dynamic_slice_in_dim(true_lengths, 1 - ctx_index, 1, 1)
-    gains = jnp.stack([g_in, g_pa, g_pf, g_pff])
-    head_gains = jnp.stack([g_q, g_k])
+    tables = block_tables(2 * rows, head_dim)
+    packed = jnp.concatenate(
+        [gain_in, gain_post_attn, gain_pre_ffn, gain_post_ffn, gain_query, gain_key]
+    ).astype(F32).reshape(-1, 128)
     weights = (w_query, w_key, w_value, w_out, w_gate.T, w_up.T, w_down)
-    (
-        out_t, x16, cot16, n16, raw, q16, kv16, far_kv, att16, attn16, mid16, hid16, dffn16, dg16,
-        du16, gain_sum,
-    ) = forward(
-        real_length, tokens.T, out_grad.T, weights, gains, head_gains, cosines, sines
-    )
-
-    gain_col = lax.dynamic_slice_in_dim(g_in, tp_index * feature_cols, feature_cols)
+    out_t, gain_sum, *kept = forward(
+        true_lengths, tokens.T, out_grad.T, weights, packed, tables
+    )
     sums, xg_t, gain_rows, gain_cols = backward(
-        real_length, tokens.T,
-        (x16, cot16, n16, q16, kv16, far_kv, att16, attn16, mid16, hid16, dffn16, dg16, du16),
-        gain_sum, weights[:-1], gains, head_gains, gain_col[:, None], (cosines, sines),
+        true_lengths, tokens.T, kept, gain_sum, weights[:-1], packed, tables
     )
     hidden = w_down.shape[0]
     ends = [hidden, 2 * hidden, 3 * hidden, 3 * hidden + head_dim, 3 * hidden + 2 * head_dim]

time: 461 us -> 431 us (0.935)
  Pallas kernels: 416 us -> 390 us
    pallas_call x2, Pallas kernels: 416 us -> 390 us  [the longest x1 286 us: backward(): pl.pallas_call(partial(backward_kernel, step_rows, steps, steps_low, lag,...]
    unnamed x15 -> x16, local copies, waits for them, and re-layouts: 5.81 us -> 10.1 us
where the time goes in v5:
time: 431 us; the launch traced here: 425 us
  Pallas kernels  390 us (90%)
  other arithmetic  16.6 us (4%)
  local copies, waits for them, and re-layouts  15.8 us (4%)
    pallas_call x1, Pallas kernels, backward(): pl.pallas_call(partial(backward_kernel, step_rows, steps, steps_low, lag,...  286 us
    pallas_call x1, Pallas kernels, forward(): pl.pallas_call(forward_kernel, out_shape=(jax.ShapeDtypeStruct((features,...  104 us
    convert_element_type x1, other arithmetic, paired_shards(): down_sum.astype(F32)  11.2 us
    unnamed x16, local copies, waits for them, and re-layouts  10.1 us
  transfers between devices with their start and end apart: 2, of which 0 were waited for; matrix products, arithmetic and copies ran while one was open for 4% of the time, Pallas kernels for 0%

profile of v5, /device:TPU:0, one launch (start us, length us, event | category | flops | bytes accessed | tf_op | source)
XLA Modules:
  0.0 425.2 jit_solution(10836058147868658680)
XLA Ops:
  0.7 0.9 dynamic-update-slice
  1.6 0.9 dynamic-update-slice.1
  2.4 0.9 dynamic-update-slice.2
  3.3 0.9 dynamic-update-slice.3
  4.2 0.8 dynamic-update-slice.4
  5.0 0.8 dynamic-update-slice.5
  5.8 0.6 bitcast_convert_fusion.packed
  6.4 104.5 %forward.1 = (bf16[288,1024]{1,0:T(8,128)(2,1)}, f32[8,1152]{1,0:T(8,128)}, bf16[1024,1152]{1,0:T(8,128)(2,1)}, bf16[1024,1152]{1,0:T(8,128)(2,1)}, bf16[1024,11...) custom-call(s32[1,2]{1,0:T(1,128)} %real_lengths.3, ...), custom_call_target="tpu_custom_call" | custom-call | tf_op jit(solution)/shard_map/forward/pallas_call | solution.py:761
  110.9 285.6 %backward.1 = (bf16[5888,1152]{1,0:T(8,128)(2,1)}, bf16[288,1024]{1,0:T(8,128)(2,1)}, f32[8,1152]{1,0:T(8,128)}, f32[1152,128]{1,0:T(8,128)}) custom-call(s32[1,2]{1,0:T(1,128)} %real_lengths.3, bf16[288,1024]{1,0:T(8,128)(2,1)} %bitcast.48, bf16[1024,1152]{1,0:T(8,128)(2,1)} %get-tuple-element.35.x_in, bf16[1024,1152]{1,0:T(8,128)(2,1)} %get-tuple-element.36.cot_in, ...), custom_call_target="tpu_custom_call" | custom-call | tf_op jit(solution)/shard_map/backward/pallas_call | solution.py:1498
  396.6 1.0 slice_bitcast_fusion.2
  397.6 1.6 collective-permute-start
  399.1 11.2 %slice_convert_fusion = (f32[1728,1152]{1,0:T(8,128)}, f32[1152,1728]{0,1:T(8,128)}, f32[1152,1728]{0,1:T(8,128)}) fusion(bf16[5888,1152]{1,0:T(8,128)(2,1)} %get-tuple-element.50), kind=kLoop, calls=%fused_computation.2 | loop fusion | flops 5971968 | bytes 35831808 | tf_op jit(solution)/shard_map/convert_element_type | solution.py:1586
  410.3 0.0 collective-permute-done
  410.3 0.1 pad_maximum_fusion
  410.4 0.0 copy-start.2
  410.4 0.1 collective-permute-start.1
  410.5 2.5 slice_convert_fusion.1
  412.9 1.4 copy.36
  414.3 1.5 slice_reduce_fusion.1
  415.8 0.0 copy-done.2
  415.8 0.8 slice_reduce_fusion
  416.7 1.3 fusion.1
  418.0 0.0 collective-permute-done.1
  418.0 1.0 select_select_fusion.2
  419.0 1.1 select_select_fusion.3
  420.1 0.2 convert_bitcast_fusion.2
  420.3 0.2 fusion
  420.4 0.0 copy-start
  420.4 1.4 copy.38
  421.8 1.4 copy.37
  423.2 0.8 copy.47
  424.0 0.8 copy.48
  (4 shorter events, 0.0 us)
Async XLA Ops:
  397.6 12.7 %collective-permute-start = (bf16[128,1152]{1,0:T(8,128)(2,1)S(1)}, bf16[128,1152]{1,0:T(8,128)(2,1)S(1)}, u32[]{:S(2)}, u32[]{:S(2)}) collective-permute-start(bf16[128,1152]{1,0:T(8,128)(2,1)S(1)} %get-tuple-element.95), channel_id=1, source_target_pairs={{0,2},{2,0},{1,3},{3,1},{4,6},{6,4},{5,7},{7,5},{8,10},{10,8},{9,1... | collective-permute-start | bytes 884744 | tf_op jit(solution)/shard_map/ppermute | solution.py:1571
  410.4 5.5 %copy-start.2 = (f32[1152,128]{1,0:T(8,128)S(1)}, f32[1152,128]{1,0:T(8,128)}, u32[]{:S(2)}) copy-start(f32[1152,128]{1,0:T(8,128)} %get-tuple-element.51) | copy-start | bytes 1769476
  410.4 7.6 %collective-permute-start.1 = (bf16[2,128,1152]{2,1,0:T(8,128)(2,1)S(1)}, bf16[2,128,1152]{2,1,0:T(8,128)(2,1)S(1)}, u32[]{:S(2)}, u32[]{:S(2)}) collective-permute-start(bf16[2,128,1152]{2,1,0:T(8,128)(2,1)S(1)} %pad_maximum_fusion), channel_id=1, source_target_pairs={{0,1},{1,0},{2,3},{3,2},{4,5},{5,4},{6,7},{7,6},{8,9},{9,8},{10,11... | collective-permute-start | bytes 1769480 | tf_op jit(solution)/shard_map/ppermute | solution.py:1572
  420.4 2.8 copy-start
  421.8 2.2 copy-start.1

commit v6 on v5

--- a/solution.py
+++ b/solution.py
@@ -532,7 +532,7 @@
     def chunk(c):
         return pl.ds(c * rows, rows)
 
-    def project(c):
+    def normalise(c):
         turn_in(blocks.at[c], x16, chunk(c))
 
         def norm(at, _, carry):
@@ -540,6 +540,8 @@
             n16[at, :] = (values * scale_of(values) * gains[0:1, :]).astype(BF16)
 
         row_blocks(c * rows, rows, 64, norm)
+
+    def project(c):
         for first in range(0, rows, half):
             at = pl.ds(c * rows + first, half)
             tables = pl.ds(c * rows + first, half)
@@ -684,19 +686,20 @@
     for copy in loads[:3]:
         copy.wait()
     gathered(0)
+    normalise(0)
     project(0)
     kv_copy.start()
     store_all(0, X, N, Q, KV)
     pass_on(1)
     to_x[2].start()
-    to_x[3].start()
     loads[3].wait()
     attend_rows(0)
     sum_start(0, attn16)
     gathered(1)
+    normalise(1)
+    sum_cross(0, attn16)
     project(1)
     store_all(1, X, N, Q, KV)
-    sum_cross(0, attn16)
     kv_copy.wait_recv()
     attend_rows(1)
     sum_start(1, attn16)
@@ -704,12 +707,12 @@
     store_all(0, ATT)
     store_all(1, ATT)
     pass_on(2)
-    pass_on(3)
     sum_cross(1, attn16)
     sum_back(0, attn16)
     for copy in loads[4:]:
         copy.wait()
     middle(0)
+    to_x[3].start()
     store_all(0, ATTN, MID)
     feed(0)
     sum_start(2, ffn16)
@@ -718,17 +721,18 @@
     middle(1)
     store_all(1, ATTN, MID)
     sum_cross(2, ffn16)
+    pass_on(3)
     feed(1)
     sum_start(3, ffn16)
     store_all(1, HID)
     gathered(2)
-    gathered(3)
+    sum_cross(3, ffn16)
     sum_back(2, ffn16)
-    sum_cross(3, ffn16)
     finish(0)
     store_all(0, COT, DFFN)
     feed_back(0)
     store_all(0, DG, DU)
+    gathered(3)
     sum_back(3, ffn16)
     finish(1)
     store_all(1, COT, DFFN)
@@ -798,18 +802,19 @@
 
 
 def backward_kernel(
-    step_rows, steps, steps_low, lag, ring, gate_hidden,
+    step_rows, steps, few, lag,
     real_lengths, tok, x_in, cot_in, n_in, q_in, kv_in, far_in, att_in, attn_in, mid_in, hid_in,
     dffn_in, dg_in, du_in, gain_ffn, w_q, w_k, w_v, w_o, w_g, w_u, packed, cosines, sines,
     out, xg_t, gain_rows, gain_cols,
-    g, y2, z2, m2, z1, m1, y1, hid, dg, du, mid, dffn, w_tiles, part, near, far, dm, cot, attn,
+    g, y2, z2, m2, z1, m1, y1, a3, b3, hid, dg, du, mid, dffn, w_tiles, part, near, far, dm, cot, attn,
     v_o, v_qkv, dkv_new, norm_near, norm_far, row_part,
     row_near, kv_near, kv_far, turned, head_sums, row_sums, sum_slots, sum_new, col_slots,
-    col_new, gains, head_gains, gain_col,
-    load_sem, tile_sem, keep_sem, chain_send, chain_recv, peer_send, peer_recv,
+    col_new, gains, head_gains, gain_col, col_part,
+    load_sem, tile_sem, keep_sem, keep_few, chain_send, chain_recv, few_send, few_recv, peer_send,
+    peer_recv,
 ):
     dp, ctx, tp = lax.axis_index("dp"), lax.axis_index("ctx"), lax.axis_index("tp")
-    s, K, low_steps = step_rows, steps, steps_low
+    s, K = step_rows, steps
     upper = dp // 2
     odd = tp % 2
     outer = (dp == 0) | (dp == 3)
@@ -849,7 +854,7 @@
     tok_own = dm.at[0:features, 0 : 2 * rows]
 
     pairs = (
-        (hid_in, hid), (dffn_in, dffn), (dg_in, dg), (mid_in, mid), (du_in, du), (cot_in, cot),
+        (hid_in, hid), (dffn_in, dffn), (du_in, du), (mid_in, mid), (dg_in, dg), (cot_in, cot),
         (attn_in, attn), (w_o, v_o),
         (w_q, v_qkv.at[:, 0:head_dim]), (w_k, v_qkv.at[:, head_dim : 2 * head_dim]),
         (w_v, v_qkv.at[:, 2 * head_dim : 3 * head_dim]),
@@ -876,7 +881,11 @@
         pl.semaphore_signal(barrier, inc=1, device_id=peer, device_id_type=MESH)
     pl.semaphore_wait(barrier, 5)
 
-    base = 2 * s * K
+    third = 3
+    enter1, enter3 = 2 * lag, 0
+    base3 = 2 * s * K
+    base = base3 + 2 * s * few
+    ring, ring_few = 4 * lag + 1, -(-(4 * lag + 1) // third) + 1
 
     def rows2(k, h):
         return multiple((2 * k + h) * s, s)
@@ -884,23 +893,28 @@
     def rows1(k, h):
         return multiple(base + (2 * k + h) * s, s)
 
+    def rows3(k, h):
+        return multiple(base3 + (2 * k + h) * s, s)
+
     def pair1(k):
         return pl.ds(pl.multiple_of(base + 2 * k * s, s), 2 * s)
 
     def slot(k):
         return multiple((k % ring) * s, s)
 
+    def slot_few(k):
+        return multiple((k % ring_few) * s, s)
+
     def slot_pair(k):
-        return multiple((k % ring) * 2 * s, 2 * s)
+        return multiple((k % ring_few) * 2 * s, 2 * s)
 
     def slot_half(k, h):
-        return multiple(((k % ring) * 2 + h) * s, s)
+        return multiple(((k % ring_few) * 2 + h) * s, s)
 
     def chain(j, k, source, target, peer):
-        return remote(source, target, chain_send.at[j, k], chain_recv.at[j, k], peer)
-
-    def keep(j, k, source, target):
-        return pltpu.make_async_copy(source, target, keep_sem.at[j, k])
+        if j < 5:
+            return remote(source, target, chain_send.at[j, k], chain_recv.at[j, k], peer)
+        return remote(source, target, few_send.at[j - 5, k], few_recv.at[j - 5, k], peer)
 
     def c_y2(k):
         return chain(0, k, g.at[rows2(k, 1 - ctx)], y2.at[slot(k)], y_peer)
@@ -924,25 +938,90 @@
         return chain(5, k, g.at[pair1(k)], z1.at[slot_pair(k)], z_peer)
 
     def c_m1(k):
-        return chain(6, k, z1.at[slot_half(k, 1 - upper)], m1.at[slot(k)], m_peer)
+        return chain(6, k, z1.at[slot_half(k, 1 - upper)], m1.at[slot_few(k)], m_peer)
 
     def c_y1(k):
-        return chain(7, k, m1.at[slot(k)], y1.at[slot(k)], y_peer)
+        return chain(7, k, m1.at[slot_few(k)], y1.at[slot_few(k)], y_peer)
 
     def c_fm(k):
-        return chain(8, k, y1.at[slot(k)], out.at[rows1(k, upper)], m_peer)
+        return chain(8, k, y1.at[slot_few(k)], out.at[rows1(k, upper)], m_peer)
 
     def c_fa(k):
-        return chain(9, k, y1.at[slot(k)], out.at[rows1(k, upper)], z_peer)
+        return chain(9, k, y1.at[slot_few(k)], out.at[rows1(k, upper)], z_peer)
 
     def c_fb(k):
         return chain(10, k, out.at[rows1(k, 1 - upper)], out.at[rows1(k, 1 - upper)], z_peer)
 
+    def c_3up(k):
+        return chain(11, k, g.at[rows3(k, 1 - upper)], a3.at[slot_few(k)], z_peer)
+
+    def c_3mid(k):
+        return chain(12, k, a3.at[slot_few(k)], b3.at[slot_few(k)], m_peer)
+
+    def c_3end(k):
+        return chain(13, k, b3.at[slot_few(k)], a3.at[slot_few(k)], z_peer)
+
+    def c_3y(k):
+        return chain(14, k, a3.at[slot_few(k)], b3.at[slot_few(k)], y_peer)
+
+    def c_3back(k):
+        return chain(15, k, b3.at[slot_few(k)], out.at[rows3(k, upper)], z_peer)
+
+    def c_3over(k):
+        return chain(16, k, out.at[rows3(k, upper)], out.at[rows3(k, upper)], m_peer)
+
+    def c_3last(k):
+        return chain(17, k, out.at[rows3(k, 1 - upper)], out.at[rows3(k, 1 - upper)], z_peer)
+
     def keep2(k):
-        return keep(0, k, m2.at[slot(k)], out.at[rows2(k, ctx)])
+        return pltpu.make_async_copy(m2.at[slot(k)], out.at[rows2(k, ctx)], keep_sem.at[k])
 
     def keep1(k):
-        return keep(1, k, y1.at[slot(k)], out.at[rows1(k, upper)])
+        return pltpu.make_async_copy(y1.at[slot_few(k)], out.at[rows1(k, upper)], keep_few.at[0, k])
+
+    def keep3(k):
+        return pltpu.make_async_copy(b3.at[slot_few(k)], out.at[rows3(k, upper)], keep_few.at[1, k])
+
+    def inner3_mid(k):
+        c_3up(k).wait_recv()
+        a3[slot_few(k), :] = add16(a3[slot_few(k), :], g[rows3(k, 1 - upper), :])
+        c_3mid(k).start()
+
+    def inner3_end(k):
+        c_3mid(k).wait_recv()
+        b3[slot_few(k), :] = add16(b3[slot_few(k), :], g[rows3(k, upper), :])
+        c_3end(k).start()
+
+    def outer3_y(k):
+        c_3end(k).wait_recv()
+        a3[slot_few(k), :] = add16(a3[slot_few(k), :], g[rows3(k, upper), :])
+        c_3y(k).start()
+
+    def outer3_back(k):
+        c_3y(k).wait_recv()
+        b3[slot_few(k), :] = add16(b3[slot_few(k), :], a3[slot_few(k), :])
+        c_3back(k).start()
+        keep3(k).start()
+
+    def inner3_over(k):
+        c_3back(k).wait_recv()
+        c_3over(k).start()
+
+    def inner3_last(k):
+        c_3over(k).wait_recv()
+        c_3last(k).start()
+
+    def outer3_done(k):
+        c_3last(k).wait_recv()
+        c_3up(k).wait_send()
+
+    def inner3_done(k):
+        c_3over(k).wait_send()
+        c_3last(k).wait_send()
+
+    def outer3_sent(k):
+        c_3back(k).wait_send()
+        keep3(k).wait()
 
     def b2(k):
         c_y2(k).wait_recv()
@@ -961,7 +1040,7 @@
 
     def c1(k):
         c_m1(k).wait_recv()
-        m1[slot(k), :] = add16(m1[slot(k), :], z1[slot_half(k, upper), :])
+        m1[slot_few(k), :] = add16(m1[slot_few(k), :], z1[slot_half(k, upper), :])
         c_y1(k).start()
 
     def d2(k):
@@ -973,7 +1052,7 @@
 
     def d1(k):
         c_y1(k).wait_recv()
-        y1[slot(k), :] = add16(y1[slot(k), :], m1[slot(k), :])
+        y1[slot_few(k), :] = add16(y1[slot_few(k), :], m1[slot_few(k), :])
         c_fm(k).start()
         c_fa(k).start()
         keep1(k).start()
@@ -1008,17 +1087,26 @@
         for copy in (c_fm, c_fa, c_fb):
             copy(k).wait_send()
 
+    two, one, three = (K, 1, 0), (few, third, enter1), (few, third, enter3)
     hops = (
-        (5, yes, K, f2), (5, outer, K, f2_outer), (5, outer, low_steps, f1_outer),
-        (5, inner, K, f2_inner), (5, inner, low_steps, f1_inner),
-        (4, inner, K, lambda k: c_m2(k).wait_send()),
-        (4, inner, low_steps, lambda k: c_y1(k).wait_send()),
-        (3, outer, K, lambda k: c_z2(k).wait_send()),
-        (3, inner, low_steps, lambda k: c_m1(k).wait_send()),
-        (4, outer, K, e2),
-        (4, inner, low_steps, e1), (3, inner, K, d2), (3, inner, low_steps, d1), (2, inner, K, c2),
-        (2, inner, low_steps, c1), (1, yes, K, b2), (1, inner, low_steps, b1),
-        (0, yes, K, lambda k: c_y2(k).start()), (0, outer, low_steps, lambda k: c_z1(k).start()),
+        (5, yes, two, f2), (5, outer, two, f2_outer), (5, outer, one, f1_outer),
+        (5, inner, two, f2_inner), (5, inner, one, f1_inner),
+        (7, outer, three, outer3_done), (7, inner, three, inner3_done),
+        (6, outer, three, outer3_sent),
+        (5, outer, three, lambda k: c_3y(k).wait_send()),
+        (4, inner, two, lambda k: c_m2(k).wait_send()),
+        (4, inner, one, lambda k: c_y1(k).wait_send()),
+        (3, outer, two, lambda k: c_z2(k).wait_send()),
+        (3, inner, one, lambda k: c_m1(k).wait_send()),
+        (3, inner, three, lambda k: c_3mid(k).wait_send()),
+        (3, inner, three, lambda k: c_3end(k).wait_send()),
+        (6, inner, three, inner3_last), (5, inner, three, inner3_over),
+        (4, outer, two, e2), (4, inner, one, e1), (4, outer, three, outer3_back),
+        (3, inner, two, d2), (3, inner, one, d1), (3, outer, three, outer3_y),
+        (2, inner, two, c2), (2, inner, one, c1), (2, inner, three, inner3_end),
+        (1, yes, two, b2), (1, inner, one, b1), (1, inner, three, inner3_mid),
+        (0, yes, two, lambda k: c_y2(k).start()), (0, outer, one, lambda k: c_z1(k).start()),
+        (0, outer, three, lambda k: c_3up(k).start()),
     )
 
     def grad_tile(index, first, size):
@@ -1073,10 +1161,8 @@
             peer_copy(3 * c + 2, final, final, core_peer),
         )
 
-    mid_split = (len(mid_tiles) + 1) // 2
-
     def sum_begin(c):
-        mid_part(c, mid_split, len(mid_tiles))
+        mid_part(c, cuts[2], tiles)
         sum_copies(c)[0].start()
 
     def sum_cross(c):
@@ -1273,10 +1359,15 @@
         xg_t[:, lanes] = (d_resid + d_in).astype(BF16)
         column = jnp.sum(grad * values * scale, axis=1, keepdims=True)
         column = jnp.broadcast_to(column, (features, 128))
-        if c == 1:
-            col_slots[0] = column
-        else:
-            col_slots[0] += column
+        for first, size in column_tiles(features, 128):
+            block = column[first : first + size, :]
+            if size < 128:
+                block = jnp.concatenate([block, jnp.zeros((128 - size, 128), F32)], axis=0)
+            cols = pl.ds(first, 128)
+            if c == 1:
+                col_slots[0, :, cols] = block.T[0:8, :]
+            else:
+                col_slots[0, :, cols] += block.T[0:8, :]
 
     at_out = 3 * hidden
     at_query = at_out + head_dim
@@ -1289,8 +1380,6 @@
         g[pl.ds(at_query, head_dim), :] = contract(dqkv[:, :head_dim], mid[...], 0, 0).astype(BF16)
 
     def kv_grads():
-        spare = g.shape[0] - at_kv - kv_rows
-        g[pl.ds(at_kv + kv_rows, spare), :] = jnp.zeros((spare, width), BF16)
         sum_copies(1)[0].wait_send()
         for j in range(4):
             cols = multiple(head_dim + owners[j] * kv_rows, kv_rows)
@@ -1352,8 +1441,7 @@
             col_slots[j + 1] = col_slots[j] + col_new[j]
             col_copy(j + 1).start()
         if j == 2:
-            mine = multiple(tp * features, features)
-            gain_cols[mine, :] = col_slots[2] + col_new[2]
+            gain_cols[tp] = col_slots[2] + col_new[2]
             gather_copies()[0].start()
             gather_copies()[1].start()
         if j == 3:
@@ -1364,8 +1452,7 @@
             gather_copies()[2].wait_recv()
 
     def gather_copies():
-        mine = gain_cols.at[multiple(tp * features, features)]
-        theirs = gain_cols.at[multiple(x_index * features, features)]
+        mine, theirs = gain_cols.at[tp], gain_cols.at[x_index]
         return (
             peer_copy(30, mine, mine, core_peer),
             peer_copy(31, mine, mine, x_peer),
@@ -1385,39 +1472,65 @@
             load(j).wait()
         head_sums[...] = jnp.zeros(head_sums.shape, F32)
 
-    gate_tiles = gate_hidden // 256
     load(0).wait()
     load(1).wait()
     grad_tile(0, 0, 256)
     load(2).wait()
     load(3).wait()
-    grad_tile(1, 256 * gate_tiles, 256)
+    grad_tile(2, 0, 256)
     for copy in fetch(0):
         copy.start()
     spread_gains(packed, gains, head_gains)
     for first in range(0, width, 128):
         row = gains[0:1, first : first + 128]
-        gain_cols[first : first + 128, :] = jnp.broadcast_to(row, (128, 128)).T
-    gain_col[...] = gain_cols[multiple(tp * features, features), :]
-
-    first_up = full + 1
-    first_gate = first_up + full + 1
-    freed = first_gate + gate_tiles
-    stages = [
-        (0, load(4).wait),
-        (0, lambda: [grad_tile(1, 256 * j, 256) for j in range(gate_tiles + 1, full)]),
-        (1, lambda: mid_part(1, 0, mid_split)),
-        (2, lambda: sum_begin(1)),
-        (3, lambda: (sum_cross(1), mid_part(0, 0, mid_split))),
-        (4, lambda: sum_begin(0)),
-        (5, lambda: sum_cross(0)),
-        (7, lambda: (late(0, 1), sum_back(1))),
-        (9, lambda: (wait_late(0, 1), wait_rest())),
-        (9, lambda: norms_back(1, 0)),
-        (10, lambda: norms_back(1, 1)),
-        (11, lambda: sum_back(0)),
-        (13, lambda: norms_back(0, 0)),
-        (14, lambda: norms_back(0, 1)),
+        col_part[first : first + 128, :] = jnp.broadcast_to(row, (128, 128)).T
+    gain_col[...] = col_part[multiple(tp * features, features), :]
+
+    lone = full - 2
+    order = [(0, 1), (2, lone), (0, 2), (2, lone + 1), (2, 1)] + [(0, j) for j in range(3, full + 1)]
+    order += [(2, full)] + [(2, j) for j in range(2, lone)]
+    first_gate = len(order) + 1
+    freed = first_gate + full + 1
+    tiles = len(mid_tiles)
+    cuts = [0, tiles // 3, tiles // 3 + (tiles + 1) // 3]
+
+    order += [(1, j) for j in range(full + 1)]
+
+    def tiles_at(t):
+        for index in range(3):
+            steps_of = [(1 + i, j) for i, (which, j) in enumerate(order) if which == index]
+            part_of = [(step, j) for step, j in steps_of if j < full]
+            if not isinstance(t, int):
+                number = sum(jnp.where(t == step, j + 1, 0) for step, j in part_of)
+                pl.when(number > 0)(partial(grad_tile, index, 256 * (number - 1), 256))
+            for step, j in steps_of:
+                if j == full and tail:
+                    pl.when(t == step)(partial(grad_tile, index, 256 * full, tail))
+
+    def choose(t, table):
+        middle = len(table) // 2
+        if middle == 0:
+            pl.when(t == table[0][0])(lambda: [action() for action in table[0][1]] and None)
+        else:
+            pl.when(t < table[middle][0])(lambda: choose(t, table[:middle]))
+            pl.when(t >= table[middle][0])(lambda: choose(t, table[middle:]))
+
+    stages = [(1, load(4).wait)]
+    after = [
+        (4, lambda: mid_part(1, cuts[0], cuts[1])),
+        (5, lambda: mid_part(1, cuts[1], cuts[2])),
+        (6, lambda: sum_begin(1)),
+        (7, lambda: (sum_cross(1), mid_part(0, cuts[0], cuts[1]))),
+        (8, lambda: mid_part(0, cuts[1], cuts[2])),
+        (9, lambda: (late(0, 1), sum_begin(0))),
+        (10, lambda: sum_cross(0)),
+        (11, lambda: sum_back(1)),
+        (12, lambda: (wait_late(0, 1), wait_rest())),
+        (13, lambda: norms_back(1, 0)),
+        (14, lambda: norms_back(1, 1)),
+        (15, lambda: sum_back(0)),
+        (17, lambda: norms_back(0, 0)),
+        (18, lambda: norms_back(0, 1)),
         (freed, lambda: late(1, len(late_pairs))),
     ]
     chain_stages = (
@@ -1429,8 +1542,8 @@
         (4, lambda: attend_back_rows(0, 1)),
         (5, lambda: (far_cross(), keys_back(1))),
         (6, lambda: scatter_begin(1)),
-        (7, lambda: scatter_cross(1)),
-        (8, lambda: (far_up(), out_grad())),
+        (7, lambda: (scatter_cross(1), out_grad())),
+        (8, far_up),
         (11, lambda: (load_tok().wait(), scatter_end(1))),
         (14, lambda: keys_back(0)),
         (15, lambda: scatter_begin(0)),
@@ -1441,29 +1554,28 @@
         (21, gains_begin),
         (22, kv_end),
     )
-    stages += [(freed + j, action) for j, action in chain_stages]
+    stages += after + [(freed + j, action) for j, action in chain_stages]
     stages += [(freed + 23 + 2 * j, partial(gains_hop, j)) for j in range(5)]
 
+    table = [
+        (step, [action for at, action in stages if at == step])
+        for step in sorted({at for at, _ in stages})
+    ]
+
     def body(t, carry):
-        pl.when((t < full) & (t != 2))(
-            lambda: grad_tile(0, 256 * (t + 1 - jnp.minimum(t // 2, 1)), 256)
-        )
-        if tail:
-            pl.when(t == 2)(lambda: grad_tile(1, 256 * full, tail))
-            pl.when(t == full)(lambda: grad_tile(0, 256 * full, tail))
-            pl.when(t == first_gate - 1)(lambda: grad_tile(2, 256 * full, tail))
-        up = t - first_up
-        pl.when((up >= 0) & (up < full))(lambda: grad_tile(2, 256 * up, 256))
-        gate = t - first_gate
-        pl.when((gate >= 0) & (gate < gate_tiles))(lambda: grad_tile(1, 256 * gate, 256))
-        for stage, who, limit, action in hops:
-            k = t - stage * lag
-            pl.when(who & (k >= 0) & (k < limit))(partial(action, k))
-        for step, action in stages:
-            pl.when(t == step)(lambda action=action: action() and None)
+        pl.when(t <= len(order))(lambda: tiles_at(t))
+        for hop, who, (limit, spacing, first), action in hops:
+            entered = t - hop * lag - first
+            k = entered // spacing
+            now = who & (entered >= 0) & (k < limit)
+            if spacing > 1:
+                now = now & (entered % spacing == 0)
+            pl.when(now)(partial(action, k))
+        choose(t, table)
         return carry
 
-    lax.fori_loop(0, K + 5 * lag, body, 0)
+    last = max(K + 5 * lag, third * (few - 1) + 1 + max(enter1 + 5 * lag, enter3 + 7 * lag))
+    lax.fori_loop(0, last, body, 0)
     done = [sum_copies(0)[j] for j in (0, 1)] + [sum_copies(1)[j] for j in (1, 2)]
     done += [*far_copies(), *scatter_copies(0), *scatter_copies(1), *kv_copies()]
     done += [sum_copy(j) for j in range(5)] + [col_copy(j) for j in range(3)]
@@ -1479,12 +1591,11 @@
     hidden, head_dim = w_g.shape[0], w_k.shape[1]
     kv_rows = head_dim // 2
     step_rows, lag = 32, 2
-    ring = 4 * lag + 1
-    needed = 3 * hidden + 2 * head_dim + kv_rows
-    steps = -(-needed // (4 * step_rows))
-    total = 4 * step_rows * steps
-    gate_hidden = total // 2 - hidden
-    steps_low = -(-(needed - total // 2) // (2 * step_rows))
+    total = 3 * hidden + 2 * head_dim + kv_rows
+    few = total // (10 * step_rows)
+    steps = total // (2 * step_rows) - 2 * few
+    ring, ring_few = 4 * lag + 1, -(-(4 * lag + 1) // 3) + 1
+    spread = -(-features // 128) * 128
     whole = pl.BlockSpec(memory_space=pltpu.VMEM)
     there = pl.BlockSpec(memory_space=pl.ANY)
 
@@ -1494,14 +1605,15 @@
     def high(*shape):
         return pltpu.VMEM(shape, F32)
 
-    slots = [low(n * step_rows * ring, width) for n in (1, 1, 1, 2, 1, 1)]
+    slots = [low(step_rows * ring, width)] * 3
+    slots += [low(n * step_rows * ring_few, width) for n in (2, 1, 1, 1, 1)]
     return pl.pallas_call(
-        partial(backward_kernel, step_rows, steps, steps_low, lag, ring, gate_hidden),
+        partial(backward_kernel, step_rows, steps, few, lag),
         out_shape=(
             jax.ShapeDtypeStruct((total, width), BF16),
             jax.ShapeDtypeStruct((features, rows), BF16),
             jax.ShapeDtypeStruct((8, width), F32),
-            jax.ShapeDtypeStruct((width, 128), F32),
+            jax.ShapeDtypeStruct((4, 8, spread), F32),
         ),
         in_specs=[pl.BlockSpec(memory_space=pltpu.SMEM)] + [there] * 14 + [whole] + [there] * 6
         + [whole] * 3,
@@ -1515,11 +1627,13 @@
             low(half, 2 * head_dim), low(2, 2, features, half), low(2, features, half),
             high(2, 2, 8, half), high(2, 2, 8, half), low(2, kv_rows, width), low(kv_rows, width),
             low(width, half), high(2, 8, head_dim), high(2, 8, width),
-            high(5, 8, width), high(5, 8, width), high(3, features, 128), high(3, features, 128),
-            high(4, width), high(2, head_dim), high(features, 128),
+            high(5, 8, width), high(5, 8, width), high(3, 8, spread), high(3, 8, spread),
+            high(4, width), high(2, head_dim), high(features, 128), high(width, 128),
             pltpu.SemaphoreType.DMA((20,)), pltpu.SemaphoreType.DMA((2, 2)),
-            pltpu.SemaphoreType.DMA((2, steps)), pltpu.SemaphoreType.DMA((11, steps)),
-            pltpu.SemaphoreType.DMA((11, steps)), pltpu.SemaphoreType.DMA((35,)),
+            pltpu.SemaphoreType.DMA((steps,)), pltpu.SemaphoreType.DMA((2, few)),
+            pltpu.SemaphoreType.DMA((5, steps)), pltpu.SemaphoreType.DMA((5, steps)),
+            pltpu.SemaphoreType.DMA((13, few)), pltpu.SemaphoreType.DMA((13, few)),
+            pltpu.SemaphoreType.DMA((35,)),
             pltpu.SemaphoreType.DMA((35,)),
         ],
         name="backward",
@@ -1553,9 +1667,13 @@
     head_dim = w_key.shape[1]
     score_scale = head_dim ** (-0.5)
     tables = block_tables(2 * rows, head_dim)
-    packed = jnp.concatenate(
-        [gain_in, gain_post_attn, gain_pre_ffn, gain_post_ffn, gain_query, gain_key]
-    ).astype(F32).reshape(-1, 128)
+    packed, offset = 0.0, 0
+    all_gains = (gain_in, gain_post_attn, gain_pre_ffn, gain_post_ffn, gain_query, gain_key)
+    length = sum(gain.size for gain in all_gains)
+    for gain in all_gains:
+        placed = jnp.pad(gain.astype(F32), (offset, length - offset - gain.size))
+        packed, offset = packed + placed, offset + gain.size
+    packed = packed.reshape(-1, 128)
     weights = (w_query, w_key, w_value, w_out, w_gate.T, w_up.T, w_down)
     out_t, gain_sum, *kept = forward(
         true_lengths, tokens.T, out_grad.T, weights, packed, tables
@@ -1564,9 +1682,10 @@
         true_lengths, tokens.T, kept, gain_sum, weights[:-1], packed, tables
     )
     hidden = w_down.shape[0]
-    ends = [hidden, 2 * hidden, 3 * hidden, 3 * hidden + head_dim, 3 * hidden + 2 * head_dim]
+    sizes = [hidden, hidden, hidden, head_dim, head_dim, head_dim // 2]
+    ends = [sum(sizes[: j + 1]) for j in range(len(sizes))]
     down_sum, gate_sum, up_sum, out_sum, query_sum, mine = [
-        sums[start:end] for start, end in zip([0] + ends, ends + [ends[-1] + head_dim // 2])
+        sums[end - size : end] for size, end in zip(sizes, ends)
     ]
     far = lax.ppermute(mine, "tp", XOR2)
     near = lax.ppermute(jnp.stack([mine, far]), "tp", XOR1)
@@ -1584,7 +1703,7 @@
         gate_sum.astype(F32).T,
         up_sum.astype(F32).T,
         down_sum.astype(F32),
-        gain_cols[:, 0],
+        gain_cols[:, 0, : tokens.shape[1]].reshape(-1),
         gain_rows[0],
         gain_rows[1],
         gain_rows[2],

time: 431 us -> 390 us (0.905)
  Pallas kernels: 390 us -> 354 us
  local copies, waits for them, and re-layouts: 15.8 us -> 11.3 us
    pallas_call x1, Pallas kernels: 286 us -> 258 us  [backward(): pl.pallas_call(partial(backward_kernel, step_rows, steps, few, lag), out_...]
    pallas_call x1, Pallas kernels: 104 us -> 95.9 us  [forward(): pl.pallas_call(forward_kernel, out_shape=(jax.ShapeDtypeStruct((features,...]
    unnamed x16 -> x9, local copies, waits for them, and re-layouts: 10.1 us -> 5.79 us
  transfers between devices with their start and end apart: 2 -> 2, of which waited for: 0 -> 0; matrix products, arithmetic and copies ran while one was open for 4% -> 5% of each run, Pallas kernels for 0% -> 0%
where the time goes in v6:
time: 390 us; the launch traced here: 385 us
  Pallas kernels  354 us (91%)
  other arithmetic  17.3 us (4%)
  local copies, waits for them, and re-layouts  11.3 us (3%)
    pallas_call x1, Pallas kernels, backward(): pl.pallas_call(partial(backward_kernel, step_rows, steps, few, lag), out_...  258 us
    pallas_call x1, Pallas kernels, forward(): pl.pallas_call(forward_kernel, out_shape=(jax.ShapeDtypeStruct((features,...  95.9 us
    convert_element_type x1, other arithmetic, paired_shards(): down_sum.astype(F32)  11.2 us
  transfers between devices with their start and end apart: 2, of which 0 were waited for; matrix products, arithmetic and copies ran while one was open for 5% of the time, Pallas kernels for 0%

profile of v6, /device:TPU:0, one launch (start us, length us, event | category | flops | bytes accessed | tf_op | source)
XLA Modules:
  0.0 384.8 jit_solution(17900394971277304093)
XLA Ops:
  0.6 1.4 add_bitcast_fusion.packed
  2.0 95.9 %forward.1 = (bf16[288,1024]{1,0:T(8,128)(2,1)}, f32[8,1152]{1,0:T(8,128)}, bf16[1024,1152]{1,0:T(8,128)(2,1)}, bf16[1024,1152]{1,0:T(8,128)(2,1)}, bf16[1024,11...) custom-call(s32[1,2]{1,0:T(1,128)} %real_lengths.3, ...), custom_call_target="tpu_custom_call" | custom-call | tf_op jit(solution)/shard_map/forward/pallas_call | solution.py:765
  97.9 258.0 %backward.1 = (bf16[5824,1152]{1,0:T(8,128)(2,1)}, bf16[288,1024]{1,0:T(8,128)(2,1)}, f32[8,1152]{1,0:T(8,128)}, f32[4,8,384]{2,1,0:T(8,128)}) custom-call(s32[1,2]{1,0:T(1,128)} %real_lengths.3, bf16[288,1024]{1,0:T(8,128)(2,1)} %bitcast.47, bf16[1024,1152]{1,0:T(8,128)(2,1)} %get-tuple-element.35.x_in, bf16[1024,1152]{1,0:T(8,128)(2,1)} %get-tuple-element.36.cot_in, ...), custom_call_target="tpu_custom_call" | custom-call | tf_op jit(solution)/shard_map/backward/pallas_call | solution.py:1610
  355.9 1.0 slice_bitcast_fusion.2
  356.9 1.2 collective-permute-start
  358.1 11.2 %slice_convert_fusion = (f32[1728,1152]{1,0:T(8,128)}, f32[1152,1728]{0,1:T(8,128)}, f32[1152,1728]{0,1:T(8,128)}) fusion(bf16[5824,1152]{1,0:T(8,128)(2,1)} %get-tuple-element.50), kind=kLoop, calls=%fused_computation.2 | loop fusion | flops 5971968 | bytes 35831808 | tf_op jit(solution)/shard_map/convert_element_type | solution.py:1705
  369.3 0.0 collective-permute-done
  369.3 0.1 pad_maximum_fusion
  369.3 0.1 collective-permute-start.1
  369.4 2.4 slice_convert_fusion.1
  371.8 0.8 slice_reduce_fusion
  372.6 0.7 reshape_squeeze.3
  373.3 1.4 copy.33
  374.7 1.5 slice_reduce_fusion.1
  376.2 1.3 fusion.1
  377.5 0.0 collective-permute-done.1
  377.5 1.0 select_select_fusion.2
  378.5 1.1 select_select_fusion.3
  379.7 0.2 convert_bitcast_fusion.2
  379.8 0.2 fusion
  380.0 0.0 copy-start
  380.0 1.4 copy.35
  381.4 0.0 copy-start.1
  381.4 1.4 copy.34
  382.8 0.0 copy-done
  382.8 0.8 copy.38
  383.6 0.0 copy-done.1
  383.6 0.8 copy.39
Async XLA Ops:
  356.9 12.4 %collective-permute-start = (bf16[128,1152]{1,0:T(8,128)(2,1)S(1)}, bf16[128,1152]{1,0:T(8,128)(2,1)S(1)}, u32[]{:S(2)}, u32[]{:S(2)}) collective-permute-start(bf16[128,1152]{1,0:T(8,128)(2,1)S(1)} %get-tuple-element.80), channel_id=1, source_target_pairs={{0,2},{2,0},{1,3},{3,1},{4,6},{6,4},{5,7},{7,5},{8,10},{10,8},{9,1... | collective-permute-start | bytes 884744 | tf_op jit(solution)/shard_map/ppermute | solution.py:1690
  369.3 8.2 %collective-permute-start.1 = (bf16[2,128,1152]{2,1,0:T(8,128)(2,1)S(1)}, bf16[2,128,1152]{2,1,0:T(8,128)(2,1)S(1)}, u32[]{:S(2)}, u32[]{:S(2)}) collective-permute-start(bf16[2,128,1152]{2,1,0:T(8,128)(2,1)S(1)} %pad_maximum_fusion), channel_id=1, source_target_pairs={{0,1},{1,0},{2,3},{3,2},{4,5},{5,4},{6,7},{7,6},{8,9},{9,8},{10,11... | collective-permute-start | bytes 1769480 | tf_op jit(solution)/shard_map/ppermute | solution.py:1691
  380.0 2.8 copy-start
  381.4 2.2 copy-start.1

commit v7 on v6

--- a/solution.py
+++ b/solution.py
@@ -822,7 +822,6 @@
     yes = dp >= 0
     core_index = tp + 1 - 2 * odd
     x_index = (tp + 2) % 4
-    cross_index = (core_index + 2) % 4
     z_index = dp + 1 - 2 * (dp % 2)
     core_peer, x_peer = (dp, ctx, core_index), (dp, ctx, x_index)
     y_peer, z_peer, m_peer = (dp, 1 - ctx, tp), (z_index, ctx, tp), (3 - dp, ctx, tp)
@@ -1121,31 +1120,62 @@
     full = hidden // 256
     tail = hidden - 256 * full
 
-    mid_tiles = column_tiles(width, 256)
-
-    def fetch(j):
-        first, size = mid_tiles[j % len(mid_tiles)]
+    wide = width // 256
+    rest = width - 256 * wide
+    tiles = wide + (rest > 0)
+
+    def fetch(slot, first, size):
         return [
             pltpu.make_async_copy(
-                w.at[:, pl.ds(first, size)], w_tiles.at[i, j % 2, :, pl.ds(0, size)],
-                tile_sem.at[i, j % 2],
+                w.at[:, pl.ds(first, size)], w_tiles.at[i, slot, :, pl.ds(0, size)],
+                tile_sem.at[i, slot],
             )
             for i, w in enumerate((w_g, w_u))
         ]
 
-    def mid_part(c, low, high):
-        base = (1 - c) * len(mid_tiles)
-        for j in range(base + low, base + high):
-            first, size = mid_tiles[j - base]
-            if j + 1 < 2 * len(mid_tiles):
-                for copy in fetch(j + 1):
-                    copy.start()
-            for copy in fetch(j):
-                copy.wait()
-            term = dot_nn(dg[chunk(c), :], w_tiles[0, j % 2, :, 0:size]) + dot_nn(
-                du[chunk(c), :], w_tiles[1, j % 2, :, 0:size]
+    def fetch_start(slot, first, size):
+        for copy in fetch(slot, first, size):
+            copy.start()
+
+    def mid_term(c, slot, first, size):
+        for copy in fetch(slot, first, size):
+            copy.wait()
+        at = multiple(c * rows, rows)
+        term = dot_nn(dg[at, :], w_tiles[0, slot, :, 0:size]) + dot_nn(
+            du[at, :], w_tiles[1, slot, :, 0:size]
+        )
+        part[c, :, pl.ds(first, size)] = term.astype(BF16)
+
+    mid_first, mid_each = 4, (wide + 1) // 2
+
+    def mid_at(t):
+        since = t - mid_first
+        c = 1 - since // (mid_each + 1)
+        turn = since % (mid_each + 1)
+
+        def tile(i, carry):
+            n = 2 * turn + i
+            slot = ((1 - c) * tiles + n) % 2
+            pl.when(n + 1 < wide)(
+                lambda: fetch_start(1 - slot, pl.multiple_of(256 * (n + 1), 256), 256)
             )
-            part[c, :, pl.ds(first, size)] = term.astype(BF16)
+            if rest:
+                pl.when(n + 1 == wide)(lambda: fetch_start(1 - slot, 256 * wide, rest))
+            mid_term(c, slot, pl.multiple_of(256 * n, 256), 256)
+            return carry
+
+        def full_tiles():
+            lax.fori_loop(0, 2, tile, 0)
+
+        pl.when(turn < mid_each)(full_tiles)
+
+        def last_tile():
+            slot = ((1 - c) * tiles + wide) % 2
+            pl.when(c == 1)(lambda: fetch_start(1 - slot, 0, 256))
+            if rest:
+                mid_term(c, slot, 256 * wide, rest)
+
+        pl.when(turn == mid_each)(last_tile)
 
     def own_half(index):
         return multiple(index * half, half)
@@ -1161,10 +1191,6 @@
             peer_copy(3 * c + 2, final, final, core_peer),
         )
 
-    def sum_begin(c):
-        mid_part(c, cuts[2], tiles)
-        sum_copies(c)[0].start()
-
     def sum_cross(c):
         copies = sum_copies(c)
         copies[0].wait_recv()
@@ -1177,10 +1203,7 @@
         dm[multiple(c * rows + odd * half, half), :] = add16(near[c], far[c])
         copies[2].start()
 
-    def norms_back(c, second):
-        if not second:
-            sum_copies(c)[2].wait_recv()
-
+    def norms_back(base):
         def body(at, _, state):
             branch = attn[at, :].astype(F32)
             scale_a = scale_of(branch)
@@ -1202,12 +1225,16 @@
             )
 
         zero = jnp.zeros((8, width), F32)
-        sum_a, sum_r = row_blocks(c * rows + second * half, half, 64, body, (zero, zero))
-        if c == 1 and not second:
-            row_sums[0], row_sums[1] = sum_a, sum_r
-        else:
-            row_sums[0] += sum_a
-            row_sums[1] += sum_r
+        sum_a, sum_r = row_blocks(base, half, 64, body, (zero, zero))
+        row_sums[0] += sum_a
+        row_sums[1] += sum_r
+
+    norm_steps = ((13, rows), (14, rows + half), (17, 0), (18, half))
+
+    def norms_at(t):
+        base = sum(jnp.where(t == step, start, 0) for step, start in norm_steps)
+        now = sum(jnp.where(t == step, 1, 0) for step, _ in norm_steps)
+        pl.when(now > 0)(lambda: norms_back(base))
 
     def head_back(grad, at, j):
         cosine, sine = cosines[at, :], sines[at, :]
@@ -1222,14 +1249,23 @@
         dqkv[at, cols] = (scale * (weighted - unit * mean)).astype(BF16)
         head_sums[j] += (grad * unit).reshape(-1, 8, head_dim).sum(axis=0)
 
+    block_rows = 128
+
+    def over_rows(low, high, body):
+        def step(i, carry):
+            body(pl.multiple_of(low + i * block_rows, block_rows))
+            return carry
+
+        lax.fori_loop(0, (high - low) // block_rows, step, 0)
+
     def attend_back_rows(c, second):
-        d_keys, d_values = [0.0, 0.0], [0.0, 0.0]
-        for first in (second * half,):
-            at = pl.ds(c * rows + first, half)
+        def block(first):
+            d_keys, d_values = [0.0, 0.0], [0.0, 0.0]
+            at = multiple(c * rows + first, block_rows)
             query = q16[at, :]
             d_out = dot_nt(attn[at, :], v_o[...]).astype(BF16)
-            row_id = first + lax.broadcasted_iota(jnp.int32, (half, rows), 0)
-            key_id = lax.broadcasted_iota(jnp.int32, (half, rows), 1)
+            row_id = first + lax.broadcasted_iota(jnp.int32, (block_rows, rows), 0)
+            key_id = lax.broadcasted_iota(jnp.int32, (block_rows, rows), 1)
             allowed = key_id <= row_id
             if c == 1:
                 allowed = allowed & (rows + key_id < real_lengths[0, 1 - ctx])
@@ -1255,15 +1291,18 @@
                 d_keys[i] += contract(d_score, query, 0, 0)
                 d_values[i] += contract(probs[i].astype(BF16), d_out, 0, 0)
             head_back(d_query * score_scale, at, 0)
-        places = [dkv.at[chunk(c), :]] + [dkv_far] * c
-        for i, place in enumerate(places):
-            for cols, term in (
-                (pl.ds(0, head_dim), d_keys[i] * score_scale),
-                (pl.ds(head_dim, head_dim), d_values[i]),
-            ):
-                if second:
-                    term = term + place[:, cols].astype(F32)
-                place[:, cols] = term.astype(BF16)
+            places = [dkv.at[chunk(c), :]] + [dkv_far] * c
+            for i, place in enumerate(places):
+                for cols, term in (
+                    (pl.ds(0, head_dim), d_keys[i] * score_scale),
+                    (pl.ds(head_dim, head_dim), d_values[i]),
+                ):
+                    place[:, cols] = (place[:, cols].astype(F32) + term).astype(BF16)
+
+        if c == 1 and not second:
+            dkv[...] = jnp.zeros((2 * rows, 2 * head_dim), BF16)
+            dkv_far[...] = jnp.zeros((rows, 2 * head_dim), BF16)
+        over_rows(second * half, second * half + half, block)
         if c == 1 and second:
             far_copies()[0].start()
 
@@ -1294,17 +1333,26 @@
         if c == 0:
             far_copies()[2].wait_recv()
             dkv[far_rows, :] = add16(dkv[far_rows, :], dkv_new[half + quarter : 2 * half, :])
-        for first in range(0, rows, half):
-            at = pl.ds(c * rows + first, half)
+        def block(first):
+            at = multiple(c * rows + first, block_rows)
             grad = dkv[at, :].astype(F32)
             head_back(grad[:, :head_dim], at, 1)
             dqkv[at, 2 * head_dim :] = grad[:, head_dim:].astype(BF16)
 
+        over_rows(0, rows, block)
+
     def cell(c, j):
         index = 4 * c + j
         return hid.at[pl.ds(index // 3 * features, features), pl.ds(index % 3 * rows, rows)]
 
-    owners = (tp, core_index, x_index, cross_index)
+    def owner_of(j):
+        near_one = tp + (j % 2) * (1 - 2 * odd)
+        return (near_one + 2 * (j // 2)) % 4
+
+    def cell_at(index):
+        return hid.at[
+            multiple(index // 3 * features, features), multiple(index % 3 * rows, rows)
+        ]
 
     def scatter_copies(c):
         return (
@@ -1316,17 +1364,22 @@
         )
 
     def scatter_begin(c):
-        for j in range(4):
-            weights = v_qkv[multiple(owners[j] * features, features), :]
-            cell(c, j)[...] = dot_nt(weights, dqkv[chunk(c), :]).astype(BF16)
-        for first in range(0, rows, half):
-            at = pl.ds(c * rows + first, half)
+        def features_of(j, carry):
+            weights = v_qkv[multiple(owner_of(j) * features, features), :]
+            cell_at(4 * c + j)[...] = dot_nt(weights, dqkv[chunk(c), :]).astype(BF16)
+            return carry
+
+        lax.fori_loop(0, 4, features_of, 0)
+        def block(first):
+            at = multiple(c * rows + first, block_rows)
             raw = dot_nn(mid[at, :], v_qkv[...])
             inner_sum = (raw * dqkv[at, :].astype(F32)).sum(axis=1, keepdims=True)
             scale = scale_of(dffn[at, :].astype(F32))
-            lane = lax.broadcasted_iota(jnp.int32, (half, 128), 1)
+            lane = lax.broadcasted_iota(jnp.int32, (block_rows, 128), 1)
             both = jnp.where(lane == 0, inner_sum, scale)
-            row_part[c, 0, :, pl.ds(first, half)] = both.T[0:8, :]
+            row_part[c, 0, :, pl.ds(first, block_rows)] = both.T[0:8, :]
+
+        over_rows(0, rows, block)
         for copy in scatter_copies(c)[:3]:
             copy.start()
 
@@ -1381,11 +1434,14 @@
 
     def kv_grads():
         sum_copies(1)[0].wait_send()
-        for j in range(4):
-            cols = multiple(head_dim + owners[j] * kv_rows, kv_rows)
-            part[1, pl.ds(j * kv_rows, kv_rows), :] = contract(dqkv[:, cols], mid[...], 0, 0).astype(
-                BF16
-            )
+
+        def block(j, carry):
+            cols = multiple(head_dim + owner_of(j) * kv_rows, kv_rows)
+            term = contract(dqkv[:, cols], mid[...], 0, 0)
+            part[1, multiple(j * kv_rows, kv_rows), :] = term.astype(BF16)
+            return carry
+
+        lax.fori_loop(0, 4, block, 0)
         for copy in kv_copies()[:2]:
             copy.start()
 
@@ -1471,6 +1527,7 @@
         for j in range(5, count):
             load(j).wait()
         head_sums[...] = jnp.zeros(head_sums.shape, F32)
+        row_sums[...] = jnp.zeros(row_sums.shape, F32)
 
     load(0).wait()
     load(1).wait()
@@ -1478,8 +1535,7 @@
     load(2).wait()
     load(3).wait()
     grad_tile(2, 0, 256)
-    for copy in fetch(0):
-        copy.start()
+    fetch_start(0, 0, 256)
     spread_gains(packed, gains, head_gains)
     for first in range(0, width, 128):
         row = gains[0:1, first : first + 128]
@@ -1491,8 +1547,6 @@
     order += [(2, full)] + [(2, j) for j in range(2, lone)]
     first_gate = len(order) + 1
     freed = first_gate + full + 1
-    tiles = len(mid_tiles)
-    cuts = [0, tiles // 3, tiles // 3 + (tiles + 1) // 3]
 
     order += [(1, j) for j in range(full + 1)]
 
@@ -1517,20 +1571,15 @@
 
     stages = [(1, load(4).wait)]
     after = [
-        (4, lambda: mid_part(1, cuts[0], cuts[1])),
-        (5, lambda: mid_part(1, cuts[1], cuts[2])),
-        (6, lambda: sum_begin(1)),
-        (7, lambda: (sum_cross(1), mid_part(0, cuts[0], cuts[1]))),
-        (8, lambda: mid_part(0, cuts[1], cuts[2])),
-        (9, lambda: (late(0, 1), sum_begin(0))),
+        (6, lambda: sum_copies(1)[0].start()),
+        (7, lambda: sum_cross(1)),
+        (9, lambda: (late(0, 1), sum_copies(0)[0].start())),
         (10, lambda: sum_cross(0)),
         (11, lambda: sum_back(1)),
         (12, lambda: (wait_late(0, 1), wait_rest())),
-        (13, lambda: norms_back(1, 0)),
-        (14, lambda: norms_back(1, 1)),
+        (13, lambda: sum_copies(1)[2].wait_recv()),
         (15, lambda: sum_back(0)),
-        (17, lambda: norms_back(0, 0)),
-        (18, lambda: norms_back(0, 1)),
+        (17, lambda: sum_copies(0)[2].wait_recv()),
         (freed, lambda: late(1, len(late_pairs))),
     ]
     chain_stages = (
@@ -1571,7 +1620,9 @@
             if spacing > 1:
                 now = now & (entered % spacing == 0)
             pl.when(now)(partial(action, k))
+        pl.when((t >= mid_first) & (t < mid_first + 2 * (mid_each + 1)))(lambda: mid_at(t))
         choose(t, table)
+        pl.when((t >= norm_steps[0][0]) & (t <= norm_steps[-1][0]))(lambda: norms_at(t))
         return carry
 
     last = max(K + 5 * lag, third * (few - 1) + 1 + max(enter1 + 5 * lag, enter3 + 7 * lag))

time: 390 us -> 381 us (0.977)
  Pallas kernels: 354 us -> 345 us
    pallas_call x1, Pallas kernels: 258 us -> 249 us  [backward(): pl.pallas_call(partial(backward_kernel, step_rows, steps, few, lag), out_...]
where the time goes in v7:
time: 381 us; the launch traced here: 375 us
  Pallas kernels  345 us (91%)
  other arithmetic  17.3 us (5%)
  local copies, waits for them, and re-layouts  11.3 us (3%)
    pallas_call x1, Pallas kernels, backward(): pl.pallas_call(partial(backward_kernel, step_rows, steps, few, lag), out_...  249 us
    pallas_call x1, Pallas kernels, forward(): pl.pallas_call(forward_kernel, out_shape=(jax.ShapeDtypeStruct((features,...  95.8 us
    convert_element_type x1, other arithmetic, paired_shards(): down_sum.astype(F32)  11.2 us
  transfers between devices with their start and end apart: 2, of which 0 were waited for; matrix products, arithmetic and copies ran while one was open for 5% of the time, Pallas kernels for 0%

profile of v7, /device:TPU:0, one launch (start us, length us, event | category | flops | bytes accessed | tf_op | source)
XLA Modules:
  0.0 375.2 jit_solution(9345268502879200512)
XLA Ops:
  0.6 1.4 add_bitcast_fusion.packed
  2.0 95.8 %forward.1 = (bf16[288,1024]{1,0:T(8,128)(2,1)}, f32[8,1152]{1,0:T(8,128)}, bf16[1024,1152]{1,0:T(8,128)(2,1)}, bf16[1024,1152]{1,0:T(8,128)(2,1)}, bf16[1024,11...) custom-call(s32[1,2]{1,0:T(1,128)} %real_lengths.3, ...), custom_call_target="tpu_custom_call" | custom-call | tf_op jit(solution)/shard_map/forward/pallas_call | solution.py:765
  97.8 249.1 %backward.1 = (bf16[5824,1152]{1,0:T(8,128)(2,1)}, bf16[288,1024]{1,0:T(8,128)(2,1)}, f32[8,1152]{1,0:T(8,128)}, f32[4,8,384]{2,1,0:T(8,128)}) custom-call(s32[1,2]{1,0:T(1,128)} %real_lengths.3, bf16[288,1024]{1,0:T(8,128)(2,1)} %bitcast.47, bf16[1024,1152]{1,0:T(8,128)(2,1)} %get-tuple-element.35.x_in, bf16[1024,1152]{1,0:T(8,128)(2,1)} %get-tuple-element.36.cot_in, ...), custom_call_target="tpu_custom_call" | custom-call | tf_op jit(solution)/shard_map/backward/pallas_call | solution.py:1661
  346.9 1.0 slice_bitcast_fusion.2
  347.9 0.7 collective-permute-start
  348.6 11.2 %slice_convert_fusion = (f32[1728,1152]{1,0:T(8,128)}, f32[1152,1728]{0,1:T(8,128)}, f32[1152,1728]{0,1:T(8,128)}) fusion(bf16[5824,1152]{1,0:T(8,128)(2,1)} %get-tuple-element.50), kind=kLoop, calls=%fused_computation.2 | loop fusion | flops 5971968 | bytes 35831808 | tf_op jit(solution)/shard_map/convert_element_type | solution.py:1756
  359.8 0.0 collective-permute-done
  359.8 0.1 pad_maximum_fusion
  359.9 0.1 collective-permute-start.1
  359.9 2.4 slice_convert_fusion.1
  362.4 0.8 slice_reduce_fusion
  363.2 0.7 reshape_squeeze.3
  363.9 1.4 copy.33
  365.3 1.5 slice_reduce_fusion.1
  366.8 1.3 fusion.1
  368.1 0.0 collective-permute-done.1
  368.1 1.0 select_select_fusion.2
  369.1 1.1 select_select_fusion.3
  370.2 0.2 convert_bitcast_fusion.2
  370.4 0.2 fusion
  370.5 0.0 copy-start
  370.5 1.4 copy.35
  371.9 0.0 copy-start.1
  371.9 1.4 copy.34
  373.3 0.0 copy-done
  373.3 0.8 copy.38
  374.1 0.0 copy-done.1
  374.1 0.8 copy.39
Async XLA Ops:
  347.9 11.9 %collective-permute-start = (bf16[128,1152]{1,0:T(8,128)(2,1)S(1)}, bf16[128,1152]{1,0:T(8,128)(2,1)S(1)}, u32[]{:S(2)}, u32[]{:S(2)}) collective-permute-start(bf16[128,1152]{1,0:T(8,128)(2,1)S(1)} %get-tuple-element.80), channel_id=1, source_target_pairs={{0,2},{2,0},{1,3},{3,1},{4,6},{6,4},{5,7},{7,5},{8,10},{10,8},{9,1... | collective-permute-start | bytes 884744 | tf_op jit(solution)/shard_map/ppermute | solution.py:1741
  359.9 8.2 %collective-permute-start.1 = (bf16[2,128,1152]{2,1,0:T(8,128)(2,1)S(1)}, bf16[2,128,1152]{2,1,0:T(8,128)(2,1)S(1)}, u32[]{:S(2)}, u32[]{:S(2)}) collective-permute-start(bf16[2,128,1152]{2,1,0:T(8,128)(2,1)S(1)} %pad_maximum_fusion), channel_id=1, source_target_pairs={{0,1},{1,0},{2,3},{3,2},{4,5},{5,4},{6,7},{7,6},{8,9},{9,8},{10,11... | collective-permute-start | bytes 1769480 | tf_op jit(solution)/shard_map/ppermute | solution.py:1742
  370.5 2.8 copy-start
  371.9 2.2 copy-start.1

commit v8 on v7

--- a/solution.py
+++ b/solution.py
@@ -873,7 +873,7 @@
     def late_load(j):
         return pltpu.make_async_copy(late_pairs[j][0], late_pairs[j][1], load_sem.at[count + j])
 
-    for j in range(count):
+    for j in range(2):
         load(j).start()
     barrier = pltpu.get_barrier_semaphore()
     for peer in (core_peer, x_peer, y_peer, z_peer, m_peer):
@@ -1251,14 +1251,14 @@
 
     block_rows = 128
 
-    def over_rows(low, high, body):
+    def over_rows(low, count_rows, body):
         def step(i, carry):
             body(pl.multiple_of(low + i * block_rows, block_rows))
             return carry
 
-        lax.fori_loop(0, (high - low) // block_rows, step, 0)
-
-    def attend_back_rows(c, second):
+        lax.fori_loop(0, count_rows // block_rows, step, 0)
+
+    def attend_back_rows(c, low):
         def block(first):
             d_keys, d_values = [0.0, 0.0], [0.0, 0.0]
             at = multiple(c * rows + first, block_rows)
@@ -1299,12 +1299,19 @@
                 ):
                     place[:, cols] = (place[:, cols].astype(F32) + term).astype(BF16)
 
-        if c == 1 and not second:
-            dkv[...] = jnp.zeros((2 * rows, 2 * head_dim), BF16)
-            dkv_far[...] = jnp.zeros((rows, 2 * head_dim), BF16)
-        over_rows(second * half, second * half + half, block)
-        if c == 1 and second:
-            far_copies()[0].start()
+        over_rows(low, half, block)
+
+    attend_steps = ((21, 0), (22, half)), ((23, 0), (24, half))
+
+    def attend_at(t):
+        for c, steps_of in ((1, attend_steps[0]), (0, attend_steps[1])):
+            low = steps_of[1][1] * (t - steps_of[0][0])
+            now = (t >= steps_of[0][0]) & (t <= steps_of[1][0])
+            pl.when(now)(partial(attend_back_rows, c, low))
+
+    def clear_keys():
+        dkv[...] = jnp.zeros((2 * rows, 2 * head_dim), BF16)
+        dkv_far[...] = jnp.zeros((rows, 2 * head_dim), BF16)
 
     quarter = half // 2
     far_rows = multiple(odd * half + tp // 2 * quarter, quarter)
@@ -1329,12 +1336,13 @@
         dkv_far[far_rows, :] = add16(dkv_far[far_rows, :], dkv_new[half : half + quarter, :])
         copies[2].start()
 
-    def keys_back(c):
-        if c == 0:
-            far_copies()[2].wait_recv()
-            dkv[far_rows, :] = add16(dkv[far_rows, :], dkv_new[half + quarter : 2 * half, :])
+    def far_down():
+        far_copies()[2].wait_recv()
+        dkv[far_rows, :] = add16(dkv[far_rows, :], dkv_new[half + quarter : 2 * half, :])
+
+    def keys_back(base):
         def block(first):
-            at = multiple(c * rows + first, block_rows)
+            at = multiple(base + first, block_rows)
             grad = dkv[at, :].astype(F32)
             head_back(grad[:, :head_dim], at, 1)
             dqkv[at, 2 * head_dim :] = grad[:, head_dim:].astype(BF16)
@@ -1366,7 +1374,8 @@
     def scatter_begin(c):
         def features_of(j, carry):
             weights = v_qkv[multiple(owner_of(j) * features, features), :]
-            cell_at(4 * c + j)[...] = dot_nt(weights, dqkv[chunk(c), :]).astype(BF16)
+            values = dqkv[multiple(c * rows, rows), :]
+            cell_at(4 * c + j)[...] = dot_nt(weights, values).astype(BF16)
             return carry
 
         lax.fori_loop(0, 4, features_of, 0)
@@ -1380,6 +1389,8 @@
             row_part[c, 0, :, pl.ds(first, block_rows)] = both.T[0:8, :]
 
         over_rows(0, rows, block)
+
+    def scatter_start(c):
         for copy in scatter_copies(c)[:3]:
             copy.start()
 
@@ -1531,16 +1542,19 @@
 
     load(0).wait()
     load(1).wait()
+    for j in range(2, count):
+        load(j).start()
     grad_tile(0, 0, 256)
     load(2).wait()
     load(3).wait()
     grad_tile(2, 0, 256)
-    fetch_start(0, 0, 256)
-    spread_gains(packed, gains, head_gains)
-    for first in range(0, width, 128):
-        row = gains[0:1, first : first + 128]
-        col_part[first : first + 128, :] = jnp.broadcast_to(row, (128, 128)).T
-    gain_col[...] = col_part[multiple(tp * features, features), :]
+
+    def take_gains():
+        spread_gains(packed, gains, head_gains)
+        for first in range(0, width, 128):
+            row = gains[0:1, first : first + 128]
+            col_part[first : first + 128, :] = jnp.broadcast_to(row, (128, 128)).T
+        gain_col[...] = col_part[multiple(tp * features, features), :]
 
     lone = full - 2
     order = [(0, 1), (2, lone), (0, 2), (2, lone + 1), (2, 1)] + [(0, j) for j in range(3, full + 1)]
@@ -1569,7 +1583,7 @@
             pl.when(t < table[middle][0])(lambda: choose(t, table[:middle]))
             pl.when(t >= table[middle][0])(lambda: choose(t, table[middle:]))
 
-    stages = [(1, load(4).wait)]
+    stages = [(1, load(4).wait), (2, lambda: fetch_start(0, 0, 256)), (11, take_gains)]
     after = [
         (6, lambda: sum_copies(1)[0].start()),
         (7, lambda: sum_cross(1)),
@@ -1582,29 +1596,30 @@
         (17, lambda: sum_copies(0)[2].wait_recv()),
         (freed, lambda: late(1, len(late_pairs))),
     ]
-    chain_stages = (
-        (1, lambda: wait_late(1, len(late_pairs))),
-        (1, lambda: attend_back_rows(1, 0)),
-        (2, lambda: attend_back_rows(1, 1)),
-        (3, lambda: (sum_copies(0)[2].wait_send(), load_tok().start())),
-        (3, lambda: attend_back_rows(0, 0)),
-        (4, lambda: attend_back_rows(0, 1)),
-        (5, lambda: (far_cross(), keys_back(1))),
-        (6, lambda: scatter_begin(1)),
-        (7, lambda: (scatter_cross(1), out_grad())),
-        (8, far_up),
-        (11, lambda: (load_tok().wait(), scatter_end(1))),
-        (14, lambda: keys_back(0)),
-        (15, lambda: scatter_begin(0)),
-        (16, query_grad),
-        (17, lambda: (scatter_cross(0), kv_grads())),
-        (18, kv_cross),
-        (20, lambda: scatter_end(0)),
-        (21, gains_begin),
-        (22, kv_end),
-    )
-    stages += after + [(freed + j, action) for j, action in chain_stages]
-    stages += [(freed + 23 + 2 * j, partial(gains_hop, j)) for j in range(5)]
+    stages += after + [
+        (freed, clear_keys),
+        (21, lambda: wait_late(1, len(late_pairs))),
+        (23, lambda: far_copies()[0].start()),
+        (23, lambda: (sum_copies(0)[2].wait_send(), load_tok().start())),
+        (25, far_cross),
+        (27, lambda: (scatter_start(1), out_grad())),
+        (28, far_up),
+        (29, lambda: scatter_cross(1)),
+        (33, lambda: (load_tok().wait(), scatter_end(1))),
+        (34, far_down),
+        (36, lambda: (scatter_start(0), query_grad())),
+        (37, kv_grads),
+        (38, lambda: scatter_cross(0)),
+        (39, kv_cross),
+        (42, lambda: scatter_end(0)),
+        (43, lambda: (gains_begin(), kv_end())),
+    ]
+    stages += [(45 + 2 * j, partial(gains_hop, j)) for j in range(5)]
+
+    def late_at(t):
+        pl.when((t >= attend_steps[0][0][0]) & (t <= attend_steps[1][1][0]))(lambda: attend_at(t))
+        pl.when((t == 25) | (t == 34))(lambda: keys_back(jnp.where(t == 25, rows, 0)))
+        pl.when((t == 26) | (t == 35))(lambda: scatter_begin(jnp.where(t == 26, 1, 0)))
 
     table = [
         (step, [action for at, action in stages if at == step])
@@ -1623,6 +1638,7 @@
         pl.when((t >= mid_first) & (t < mid_first + 2 * (mid_each + 1)))(lambda: mid_at(t))
         choose(t, table)
         pl.when((t >= norm_steps[0][0]) & (t <= norm_steps[-1][0]))(lambda: norms_at(t))
+        pl.when((t >= 21) & (t <= 35))(lambda: late_at(t))
         return carry
 
     last = max(K + 5 * lag, third * (few - 1) + 1 + max(enter1 + 5 * lag, enter3 + 7 * lag))

time: 381 us -> 387 us (1.016); the launches traced: 375 us -> 386 us
  Pallas kernels: 345 us -> 356 us
    pallas_call x1, Pallas kernels: 249 us -> 260 us  [backward(): pl.pallas_call(partial(backward_kernel, step_rows, steps, few, lag), out_...]
where the time goes in v8:
time: 387 us; the launch traced here: 386 us
  Pallas kernels  356 us (92%)
  other arithmetic  17.3 us (4%)
  local copies, waits for them, and re-layouts  11.3 us (3%)
    pallas_call x1, Pallas kernels, backward(): pl.pallas_call(partial(backward_kernel, step_rows, steps, few, lag), out_...  260 us
    pallas_call x1, Pallas kernels, forward(): pl.pallas_call(forward_kernel, out_shape=(jax.ShapeDtypeStruct((features,...  95.4 us
    convert_element_type x1, other arithmetic, paired_shards(): down_sum.astype(F32)  11.2 us
  transfers between devices with their start and end apart: 2, of which 0 were waited for; matrix products, arithmetic and copies ran while one was open for 5% of the time, Pallas kernels for 0%

profile of v8, /device:TPU:0, one launch (start us, length us, event | category | flops | bytes accessed | tf_op | source)
XLA Modules:
  0.0 385.5 jit_solution(2877368629708682340)
XLA Ops:
  0.6 1.4 add_bitcast_fusion.packed
  2.0 95.4 %forward.1 = (bf16[288,1024]{1,0:T(8,128)(2,1)}, f32[8,1152]{1,0:T(8,128)}, bf16[1024,1152]{1,0:T(8,128)(2,1)}, bf16[1024,1152]{1,0:T(8,128)(2,1)}, bf16[1024,11...) custom-call(s32[1,2]{1,0:T(1,128)} %real_lengths.3, ...), custom_call_target="tpu_custom_call" | custom-call | tf_op jit(solution)/shard_map/forward/pallas_call | solution.py:765
  97.5 260.4 %backward.1 = (bf16[5824,1152]{1,0:T(8,128)(2,1)}, bf16[288,1024]{1,0:T(8,128)(2,1)}, f32[8,1152]{1,0:T(8,128)}, f32[4,8,384]{2,1,0:T(8,128)}) custom-call(s32[1,2]{1,0:T(1,128)} %real_lengths.3, bf16[288,1024]{1,0:T(8,128)(2,1)} %bitcast.47, bf16[1024,1152]{1,0:T(8,128)(2,1)} %get-tuple-element.35.x_in, bf16[1024,1152]{1,0:T(8,128)(2,1)} %get-tuple-element.36.cot_in, ...), custom_call_target="tpu_custom_call" | custom-call | tf_op jit(solution)/shard_map/backward/pallas_call | solution.py:1677
  357.9 1.0 slice_bitcast_fusion.2
  358.9 0.1 collective-permute-start
  359.0 11.2 %slice_convert_fusion = (f32[1728,1152]{1,0:T(8,128)}, f32[1152,1728]{0,1:T(8,128)}, f32[1152,1728]{0,1:T(8,128)}) fusion(bf16[5824,1152]{1,0:T(8,128)(2,1)} %get-tuple-element.50), kind=kLoop, calls=%fused_computation.2 | loop fusion | flops 5971968 | bytes 35831808 | tf_op jit(solution)/shard_map/convert_element_type | solution.py:1772
  370.1 0.0 collective-permute-done
  370.1 0.1 pad_maximum_fusion
  370.2 0.1 collective-permute-start.1
  370.3 2.4 slice_convert_fusion.1
  372.7 0.8 slice_reduce_fusion
  373.5 0.7 reshape_squeeze.3
  374.2 1.4 copy.33
  375.6 1.5 slice_reduce_fusion.1
  377.1 1.3 fusion.1
  378.4 0.0 collective-permute-done.1
  378.4 1.0 select_select_fusion.2
  379.4 1.1 select_select_fusion.3
  380.6 0.2 convert_bitcast_fusion.2
  380.7 0.2 fusion
  380.9 0.0 copy-start
  380.9 1.4 copy.35
  382.3 0.0 copy-start.1
  382.3 1.4 copy.34
  383.7 0.0 copy-done
  383.7 0.8 copy.38
  384.5 0.0 copy-done.1
  384.5 0.8 copy.39
Async XLA Ops:
  358.9 11.3 %collective-permute-start = (bf16[128,1152]{1,0:T(8,128)(2,1)S(1)}, bf16[128,1152]{1,0:T(8,128)(2,1)S(1)}, u32[]{:S(2)}, u32[]{:S(2)}) collective-permute-start(bf16[128,1152]{1,0:T(8,128)(2,1)S(1)} %get-tuple-element.80), channel_id=1, source_target_pairs={{0,2},{2,0},{1,3},{3,1},{4,6},{6,4},{5,7},{7,5},{8,10},{10,8},{9,1... | collective-permute-start | bytes 884744 | tf_op jit(solution)/shard_map/ppermute | solution.py:1757
  370.2 8.2 %collective-permute-start.1 = (bf16[2,128,1152]{2,1,0:T(8,128)(2,1)S(1)}, bf16[2,128,1152]{2,1,0:T(8,128)(2,1)S(1)}, u32[]{:S(2)}, u32[]{:S(2)}) collective-permute-start(bf16[2,128,1152]{2,1,0:T(8,128)(2,1)S(1)} %pad_maximum_fusion), channel_id=1, source_target_pairs={{0,1},{1,0},{2,3},{3,2},{4,5},{5,4},{6,7},{7,6},{8,9},{9,8},{10,11... | collective-permute-start | bytes 1769480 | tf_op jit(solution)/shard_map/ppermute | solution.py:1758
  380.9 2.8 copy-start
  382.3 2.2 copy-start.1
